TPU v7x, 512 devices: a whole 4x4x16 slice. The times are simulated.
512 devices in a mesh: cp: 128 (over z_lo, y, x, core), tp: 4 (over z_hi).
Axes of the slice: x: 4, y: 4, z: 16 (z_hi: 4, z_lo: 4; z = z_hi * 4 + z_lo), core: 2. Of those that a mesh axis runs over, the one named last changes fastest.
Arguments:
- queries: bfloat16 [2, 128, 256, 4096], P(None, 'cp', None, 'tp'), may hold values from -40 to 40
- keys: bfloat16 [2, 128, 256, 512], P(None, 'cp', 'tp'), may hold values from -8 to 8
- values: bfloat16 [2, 128, 256, 512], P(None, 'cp', 'tp'), may hold values from -6 to 6
- out_grad: bfloat16 [2, 128, 256, 4096], P(None, 'cp', None, 'tp'), may hold values from -6 to 6
- doc_lengths: int32 [256], replicated, may hold values from 1 to 512, 65536 in all
Outputs:
- attn_out: bfloat16 [2, 128, 256, 4096], P(None, 'cp', None, 'tp')
- q_grad: bfloat16 [2, 128, 256, 4096], P(None, 'cp', None, 'tp')
- k_grad: bfloat16 [2, 128, 256, 512], P(None, 'cp', 'tp')
- v_grad: bfloat16 [2, 128, 256, 512], P(None, 'cp', 'tp')
Inputs may be any that keep to these rules, and one draw needn't show every extreme that they name: `doc_lengths`: the documents lie in order and tile the whole sequence; one of them is exactly 512 tokens long.
All inputs are finite; a program needn't handle non-finite values.
Results may differ from a plain program's by a relative error of at most 0.012.
The roundings to bfloat16 on the way count: a program that leaves them out, or rounds other values in their place, can miss the bound.
Values may be sent and summed in bfloat16 or wider, within the bound.
No kernel may reach another device: no remote copies, remote signals or barrier semaphores. Data moves between devices by JAX's collectives and lax.ppermute only.
A program may use at most 64 MiB of HBM per device.

v0:
```python
import math

import jax
import jax.numpy as jnp
from jax import lax
from jax.sharding import PartitionSpec as P

REACH = 2
KV = 4
HD = 128


def from_behind(block, axis, distance):
    devices = range(lax.axis_size(axis))
    route = [(i - distance, i) for i in devices if i - distance in devices]
    return lax.ppermute(block, axis, route)


def document_ids(positions, ends):
    return jnp.sum((ends <= positions[..., None]).astype(jnp.int32), axis=-1)


def attend_block(query_part, grad_part, key_rows, value_rows, allowed, factor):
    scores = (
        jnp.einsum("hqgrd,hkgd->hqgrk", query_part, key_rows, preferred_element_type=jnp.float32)
        * factor
    )
    scores = jnp.where(allowed, scores, -jnp.inf)
    top = jnp.max(scores, axis=-1, keepdims=True)
    lse = top + jnp.log(jnp.sum(jnp.exp(scores - top), axis=-1, keepdims=True))
    probs = jnp.exp(scores - lse)
    probs_low = probs.astype(jnp.bfloat16)
    attn = jnp.einsum(
        "hqgrk,hkgd->hqgrd", probs_low, value_rows, preferred_element_type=jnp.float32
    ).astype(jnp.bfloat16)
    delta = jnp.sum(
        attn.astype(jnp.float32) * grad_part.astype(jnp.float32), axis=-1, keepdims=True
    )
    dprobs = jnp.einsum(
        "hqgrd,hkgd->hqgrk", grad_part, value_rows, preferred_element_type=jnp.float32
    )
    dscores = (probs * (dprobs - delta)).astype(jnp.bfloat16)
    query_grad = (
        jnp.einsum("hqgrk,hkgd->hqgrd", dscores, key_rows, preferred_element_type=jnp.float32)
        * factor
    ).astype(jnp.bfloat16)
    key_grad = (
        jnp.einsum("hqgrk,hqgrd->hkgd", dscores, query_part, preferred_element_type=jnp.float32)
        * factor
    )
    value_grad = jnp.einsum(
        "hqgrk,hqgrd->hkgd", probs_low, grad_part, preferred_element_type=jnp.float32
    )
    return (attn, query_grad, key_grad, value_grad)


def local(queries, keys, values, out_grad, doc_lengths):
    stretch = queries.shape[2]
    factor = 1.0 / math.sqrt(HD)
    context_count = lax.axis_size("cp")
    head_groups = lax.axis_size("tp")
    own_index = lax.axis_index("cp")
    per_device = queries.shape[3] // HD
    kv_device = KV // head_groups
    per_group = per_device // kv_device
    piece_rows = keys.shape[2]
    ends = jnp.cumsum(doc_lengths)
    key_split = keys.reshape(2, piece_rows, KV, HD)
    value_split = values.reshape(2, piece_rows, KV, HD)
    key_four, value_four = (
        lax.all_to_all(key_split, "tp", split_axis=2, concat_axis=1, tiled=True),
        lax.all_to_all(value_split, "tp", split_axis=2, concat_axis=1, tiled=True),
    )
    query_five = queries.reshape(2, stretch, kv_device, per_group, HD)
    grad_five = out_grad.reshape(2, stretch, kv_device, per_group, HD)
    kv_heads_here = key_four.shape[2]
    lower = []
    for step in range(1, REACH + 1):
        lower.append(from_behind((key_four[0], value_four[0]), "cp", step))
    upper_first = []
    upper_second = []
    for step in range(1, REACH + 1):
        both_keys, both_values = from_behind((key_four, value_four), "cp", -step)
        upper_first.append((both_keys[0], both_values[0]))
        upper_second.append((both_keys[1], both_values[1]))
    stack_keys = jnp.stack(
        [lower[m - 1][0] for m in range(REACH, 0, -1)]
        + [key_four[0]]
        + [upper_first[m - 1][0] for m in range(1, REACH + 1)]
    )
    stack_values = jnp.stack(
        [lower[m - 1][1] for m in range(REACH, 0, -1)]
        + [value_four[0]]
        + [upper_first[m - 1][1] for m in range(1, REACH + 1)]
    )
    second_stretch = 2 * context_count - 1 - own_index
    lead_keys = [key_four[0]] + [lower[m - 1][0] for m in range(1, REACH + 1)]
    lead_values = [value_four[0]] + [lower[m - 1][1] for m in range(1, REACH + 1)]
    tail_keys = [key_four[1]]
    tail_values = [value_four[1]]
    inside_flags = []
    offset_list = []
    for step in range(1, REACH + 1):
        inside = own_index + step <= context_count - 1
        offset = jnp.clip(second_stretch - step - own_index, -REACH, REACH)
        picked_key = lax.dynamic_index_in_dim(stack_keys, offset + REACH, 0, keepdims=False)
        picked_value = lax.dynamic_index_in_dim(stack_values, offset + REACH, 0, keepdims=False)
        tail_keys.append(jnp.where(inside, upper_second[step - 1][0], picked_key))
        tail_values.append(jnp.where(inside, upper_second[step - 1][1], picked_value))
        inside_flags.append(inside)
        offset_list.append(offset)
    key_rows = jnp.stack([jnp.concatenate(lead_keys, 0), jnp.concatenate(tail_keys, 0)])
    value_rows = jnp.stack([jnp.concatenate(lead_values, 0), jnp.concatenate(tail_values, 0)])
    reach_steps = jnp.arange(REACH + 1, dtype=jnp.int32)
    query_stretches = jnp.stack([own_index, second_stretch])
    key_stretches = query_stretches[:, None] - reach_steps[None, :]
    inner = jnp.arange(stretch, dtype=jnp.int32)
    query_pos = query_stretches[:, None] * stretch + inner[None, :]
    key_pos = (key_stretches[:, :, None] * stretch + inner[None, None, :]).reshape(2, -1)
    query_docs = document_ids(query_pos, ends)
    key_docs = document_ids(key_pos, ends)
    allowed = (
        (key_pos[:, None, :] >= 0)
        & (key_pos[:, None, :] <= query_pos[:, :, None])
        & (key_docs[:, None, :] == query_docs[:, :, None])
    )
    allowed = allowed[:, :, None, None, :]
    half_heads = per_group // 2

    def split_heads(field):
        return jnp.moveaxis(field.reshape(2, stretch, kv_heads_here, 2, half_heads, HD), 3, 0)

    def head_block(pair):
        return attend_block(pair[0], pair[1], key_rows, value_rows, allowed, factor)

    attn, query_grad, key_grad, value_grad = lax.map(
        head_block, (split_heads(query_five), split_heads(grad_five))
    )
    attn = jnp.moveaxis(attn, 0, 3).reshape(2, stretch, kv_heads_here, per_group, HD)
    query_grad = jnp.moveaxis(query_grad, 0, 3).reshape(2, stretch, kv_heads_here, per_group, HD)
    blocks_k = jnp.sum(key_grad, axis=0).reshape(2, REACH + 1, stretch, kv_heads_here, HD)
    blocks_v = jnp.sum(value_grad, axis=0).reshape(2, REACH + 1, stretch, kv_heads_here, HD)
    spare = jnp.zeros((REACH, stretch, kv_heads_here, HD), jnp.float32)
    first_k = jnp.concatenate([jnp.flip(blocks_k[0], axis=0), spare], axis=0)
    first_v = jnp.concatenate([jnp.flip(blocks_v[0], axis=0), spare], axis=0)
    slot_ids = jnp.arange(2 * REACH + 1, dtype=jnp.int32)[:, None, None, None]
    upper_k = []
    upper_v = []
    for step in range(1, REACH + 1):
        inside = inside_flags[step - 1]
        target = slot_ids == offset_list[step - 1] + REACH
        first_k = first_k + jnp.where(
            target & jnp.logical_not(inside), blocks_k[1, step][None], 0.0
        )
        first_v = first_v + jnp.where(
            target & jnp.logical_not(inside), blocks_v[1, step][None], 0.0
        )
        upper_k.append(jnp.where(inside, blocks_k[1, step], 0.0))
        upper_v.append(jnp.where(inside, blocks_v[1, step], 0.0))
    key_first = first_k[REACH]
    value_first = first_v[REACH]
    key_second = blocks_k[1, 0]
    value_second = blocks_v[1, 0]
    for step in range(1, REACH + 1):
        back_k, back_v = from_behind((first_k[REACH - step], first_v[REACH - step]), "cp", -step)
        key_first = key_first + back_k
        value_first = value_first + back_v
    for step in range(1, REACH + 1):
        sent_k = jnp.stack([first_k[REACH + step], upper_k[step - 1]])
        sent_v = jnp.stack([first_v[REACH + step], upper_v[step - 1]])
        came_k, came_v = from_behind((sent_k, sent_v), "cp", step)
        key_first = key_first + came_k[0]
        value_first = value_first + came_v[0]
        key_second = key_second + came_k[1]
        value_second = value_second + came_v[1]
    key_total = jnp.stack([key_first, key_second]).astype(jnp.bfloat16)
    value_total = jnp.stack([value_first, value_second]).astype(jnp.bfloat16)
    key_back, value_back = (
        lax.all_to_all(key_total, "tp", split_axis=1, concat_axis=2, tiled=True),
        lax.all_to_all(value_total, "tp", split_axis=1, concat_axis=2, tiled=True),
    )
    attn_out = attn.reshape(2, 1, stretch, per_device * HD)
    q_grad = query_grad.reshape(2, 1, stretch, per_device * HD)
    k_grad = key_back.reshape(2, 1, piece_rows, KV * HD)
    v_grad = value_back.reshape(2, 1, piece_rows, KV * HD)
    return (attn_out, q_grad, k_grad, v_grad)


def solution(mesh):
    in_specs = (
        P(None, "cp", None, "tp"),
        P(None, "cp", "tp", None),
        P(None, "cp", "tp", None),
        P(None, "cp", None, "tp"),
        P(),
    )
    out_specs = (
        P(None, "cp", None, "tp"),
        P(None, "cp", None, "tp"),
        P(None, "cp", "tp", None),
        P(None, "cp", "tp", None),
    )
    return jax.shard_map(local, mesh=mesh, in_specs=in_specs, out_specs=out_specs, check_vma=False)
```

profile of v0, /device:TPU:30, one launch (start us, length us, event | category | flops | bytes accessed | tf_op | source)
XLA Modules:
  0.0 198.1 jit_solution(11500589363152337383)
XLA Ops:
  2.3 15.1 %all-to-all-start.1 = ((bf16[2,64,4,128]{3,1,0,2:T(8,128)(2,1)}), bf16[2,64,4,128]{3,1,0,2:T(8,128)(2,1)S(1)}, u32[]{:S(2)}, u32[]{:S(2)}) async-start(bf16[2,64,4,128]{3,1,0,2:T(8,128)(2,1)} %copy.206), calls=%async_computation.1 | async-start | bytes 262144 | tf_op jit(solution)/shard_map/all_to_all | solution.py:72
  22.0 9.8 %all-to-all-done.1 = bf16[2,64,4,128]{3,1,0,2:T(8,128)(2,1)S(1)} async-done(((bf16[2,64,4,128]{3,1,0,2:T(8,128)(2,1)}), bf16[2,64,4,128]{3,1,0,2:T(8,128)(2,1)S(1)}, u32[]{:S(2)}, u32[]{:S(2)}) %all-to-all-start.1) | async-done | bytes 131104 | tf_op jit(solution)/shard_map/all_to_all | solution.py:72
  31.8 4.2 %all-to-all-start = ((bf16[2,64,4,128]{3,1,0,2:T(8,128)(2,1)}), bf16[2,64,4,128]{3,1,0,2:T(8,128)(2,1)S(1)}, u32[]{:S(2)}, u32[]{:S(2)}) async-start(bf16[2,64,4,128]{3,1,0,2:T(8,128)(2,1)} %copy.200), calls=%async_computation | async-start | bytes 262144 | tf_op jit(solution)/shard_map/all_to_all | solution.py:71
  36.6 1.5 copy.199
  38.1 1.5 copy.210
  40.7 2.0 collective-permute-start.5
  42.7 1.9 collective-permute-start.4
  44.6 3.6 %collective-permute-start.6 = (bf16[2,256,1,128]{3,1,2,0:T(8,128)(2,1)S(1)}, bf16[2,256,1,128]{3,1,2,0:T(8,128)(2,1)}, u32[]{:S(2)}, u32[]{:S(2)}) collective-permute-start(bf16[2,256,1,128]{3,1,2,0:T(8,128)(2,1)S(1)} %bitcast.450), channel_id=1, source_target_pairs={{4,0},{8,4},{12,8},{16,12},{20,16},{24,20},{28,24},{32,28},{36,32}... | collective-permute-start | bytes 393224 | tf_op jit(solution)/shard_map/ppermute | solution.py:16
  48.3 3.9 %collective-permute-start.7 = (bf16[2,256,1,128]{3,1,2,0:T(8,128)(2,1)S(1)}, bf16[2,256,1,128]{3,1,2,0:T(8,128)(2,1)}, u32[]{:S(2)}, u32[]{:S(2)}) collective-permute-start(bf16[2,256,1,128]{3,1,2,0:T(8,128)(2,1)S(1)} %bitcast.451), channel_id=1, source_target_pairs={{8,0},{12,4},{16,8},{20,12},{24,16},{28,20},{32,24},{36,28},{40,32... | collective-permute-start | bytes 393224 | tf_op jit(solution)/shard_map/ppermute | solution.py:16
  52.2 6.2 %collective-permute-start.1 = (bf16[256,1,128]{2,0,1:T(8,128)(2,1)S(1)}, bf16[256,1,128]{2,0,1:T(8,128)(2,1)S(1)}, u32[]{:S(2)}, u32[]{:S(2)}) collective-permute-start(bf16[256,1,128]{2,0,1:T(8,128)(2,1)S(1)} %bitcast.445), channel_id=1, source_target_pairs={{0,8},{4,12},{8,16},{12,20},{16,24},{20,28},{24,32},{28,36},{32,40... | collective-permute-start | bytes 196616 | tf_op jit(solution)/shard_map/ppermute | solution.py:16
  58.4 1.9 collective-permute-start
  60.4 3.6 %collective-permute-start.2 = (bf16[2,256,1,128]{3,1,2,0:T(8,128)(2,1)S(1)}, bf16[2,256,1,128]{3,1,2,0:T(8,128)(2,1)S(1)}, u32[]{:S(2)}, u32[]{:S(2)}) collective-permute-start(bf16[2,256,1,128]{3,1,2,0:T(8,128)(2,1)S(1)} %bitcast.453), channel_id=1, source_target_pairs={{4,0},{8,4},{12,8},{16,12},{20,16},{24,20},{28,24},{32,28},{36,32}... | collective-permute-start | bytes 393224 | tf_op jit(solution)/shard_map/ppermute | solution.py:16
  65.7 1.9 collective-permute-start.3
  72.1 5.1 %collective-permute-done.3 = bf16[2,256,1,128]{3,1,0,2:T(8,128)(2,1)S(1)} collective-permute-done((bf16[2,256,1,128]{3,1,0,2:T(8,128)(2,1)S(1)}, bf16[2,256,1,128]{3,1,0,2:T(8,128)(2,1)S(1)}, u32[]{:S(2)}, u32[]{:S(2)}) %collective-permute-start.3) | collective-permute-done | bytes 131104 | tf_op jit(solution)/shard_map/ppermute | solution.py:16
  77.2 31.2 %while.17 = (s32[]{:T(128)}, bf16[2,2,256,1,4,128]{2,5,4,1,3,0:T(8,128)(2,1)S(1)}, bf16[2,2,256,1,4,128]{5,2,4,1,3,0:T(8,128)(2,1)}, f32[2,2,768,1,128]{2,4,1,3,...) while((s32[]{:T(128)}, ...), condition=%wide.region_8.9_spmd.clone, body=%wide.region_4.8_spmd.clone.sunk | while | flops 2452549632 | bytes 86355816 | solution.py:136
  77.3 1.2 and_bitcast_fusion.2
  78.4 1.6 fusion.82
  80.0 1.7 exponential_reduce_fusion.2
  81.8 2.0 %fusion.87 = f32[2,2,768,1,128]{2,4,1,3,0:T(8,128)S(1)} fusion(f32[2,2,768,1,128]{2,4,1,3,0:T(8,128)S(1)} %copy-done.2, s32[]{:T(128)} %get-tuple-element.391, bf16[2,2,256,1,4,128]{2,5,4,0,1,3:T(8,128)(2,1)S(1)} %get-tuple-element.414, f32[2,256,4,768]{3,1,2,0:T(8,128)S(1)} %get-tuple-element.372, f32[2,256,4]{1,2,0:T(4,128)S(1)} %bitcast.459, ...), kind=kOutput, calls=%fused_computation.15.clone.1 | convolution fusion | flops 408944640 | bytes 8004608 | tf_op jit(solution)/shard_map/while/body/eval_jaxpr/hqgrk,hqgrd->hkgd/dot_general | solution.py:51
  83.9 1.1 copy-done.3
  85.0 2.2 %bitcast_dynamic-update-slice_fusion.6 = (bf16[2,2,256,1,4,128]{2,5,4,1,3,0:T(8,128)(2,1)S(1)}, bf16[2,256,4,128]{1,3,2,0:T(8,128)(2,1)S(1)}) fusion(bf16[2,2,256,1,4,128]{2,5,4,1,3,0:T(8,128)(2,1)S(1)} %get-tuple-element.392, s32[]{:T(128)} %get-tuple-element.391, bf16[2,768,1,128]{3,1,0,2:T(8,128)(2,1)S(1)} %copy-done.8, ...), kind=kOutput, calls=%fused_computation.31.clone.1 | convolution fusion | flops 409206784 | bytes 8134660 | tf_op jit(solution)/shard_map/while/body/eval_jaxpr/hqgrk,hkgd->hqgrd/dot_general | solution.py:33
  87.4 2.7 %fusion.84 = bf16[2,256,4,768]{3,1,2,0:T(8,128)(2,1)S(1)} fusion(f32[2,256,4,768]{3,1,2,0:T(8,128)S(1)} %get-tuple-element.372, f32[2,256,4]{1,2,0:T(4,128)S(1)} %fusion.83, f32[2,256,4]{1,2,0:T(4,128)S(1)} %bitcast.461, pred[2,256,768]{2,1,0:T(8,128)(4,1)S(1)} %and_bitcast_fusion.2, bf16[2,2,256,1,4,128]{2,5,4,0,1,3:T(8,128)(2,1)S(1)} %get-tuple-element.414, ...), kind=kOutput, calls=%fused_computation.11.clone.1 | convolution fusion | flops 412090368 | bytes 10764292 | tf_op jit(solution)/shard_map/while/body/eval_jaxpr/hqgrd,hkgd->hqgrk/dot_general | solution.py:39
  92.9 1.2 and_bitcast_fusion.2
  94.1 1.6 fusion.82
  95.7 1.7 exponential_reduce_fusion.2
  97.4 2.0 %fusion.87 = f32[2,2,768,1,128]{2,4,1,3,0:T(8,128)S(1)} fusion(f32[2,2,768,1,128]{2,4,1,3,0:T(8,128)S(1)} %copy-done.2, s32[]{:T(128)} %get-tuple-element.391, bf16[2,2,256,1,4,128]{2,5,4,0,1,3:T(8,128)(2,1)S(1)} %get-tuple-element.414, f32[2,256,4,768]{3,1,2,0:T(8,128)S(1)} %get-tuple-element.372, f32[2,256,4]{1,2,0:T(4,128)S(1)} %bitcast.459, ...), kind=kOutput, calls=%fused_computation.15.clone.1 | convolution fusion | flops 408944640 | bytes 8004608 | tf_op jit(solution)/shard_map/while/body/eval_jaxpr/hqgrk,hqgrd->hkgd/dot_general | solution.py:51
  100.6 2.2 %bitcast_dynamic-update-slice_fusion.6 = (bf16[2,2,256,1,4,128]{2,5,4,1,3,0:T(8,128)(2,1)S(1)}, bf16[2,256,4,128]{1,3,2,0:T(8,128)(2,1)S(1)}) fusion(bf16[2,2,256,1,4,128]{2,5,4,1,3,0:T(8,128)(2,1)S(1)} %get-tuple-element.392, s32[]{:T(128)} %get-tuple-element.391, bf16[2,768,1,128]{3,1,0,2:T(8,128)(2,1)S(1)} %copy-done.8, ...), kind=kOutput, calls=%fused_computation.31.clone.1 | convolution fusion | flops 409206784 | bytes 8134660 | tf_op jit(solution)/shard_map/while/body/eval_jaxpr/hqgrk,hkgd->hqgrd/dot_general | solution.py:33
  103.0 2.7 %fusion.84 = bf16[2,256,4,768]{3,1,2,0:T(8,128)(2,1)S(1)} fusion(f32[2,256,4,768]{3,1,2,0:T(8,128)S(1)} %get-tuple-element.372, f32[2,256,4]{1,2,0:T(4,128)S(1)} %fusion.83, f32[2,256,4]{1,2,0:T(4,128)S(1)} %bitcast.461, pred[2,256,768]{2,1,0:T(8,128)(4,1)S(1)} %and_bitcast_fusion.2, bf16[2,2,256,1,4,128]{2,5,4,0,1,3:T(8,128)(2,1)S(1)} %get-tuple-element.414, ...), kind=kOutput, calls=%fused_computation.11.clone.1 | convolution fusion | flops 412090368 | bytes 10764292 | tf_op jit(solution)/shard_map/while/body/eval_jaxpr/hqgrd,hkgd->hqgrk/dot_general | solution.py:39
  108.5 1.9 reduce_sum.57
  110.7 1.6 reduce_sum.56
  116.2 1.9 collective-permute-start.14
  119.1 3.1 %collective-permute-start.15 = (f32[2,256,1,128]{3,1,2,0:T(8,128)S(1)}, f32[2,256,1,128]{3,1,2,0:T(8,128)S(1)}, u32[]{:S(2)}, u32[]{:S(2)}) collective-permute-start(f32[2,256,1,128]{3,1,2,0:T(8,128)S(1)} %pad_maximum_fusion.3), channel_id=1, source_target_pairs={{0,8},{4,12},{8,16},{12,20},{16,24},{20,28},{24,32},{28,36},{32,40... | collective-permute-start | bytes 786440 | tf_op jit(solution)/shard_map/ppermute | solution.py:16
  122.2 3.4 %collective-permute-start.12 = (f32[256,1,128]{2,0,1:T(8,128)S(1)}, f32[256,1,128]{2,0,1:T(8,128)S(1)}, u32[]{:S(2)}, u32[]{:S(2)}) collective-permute-start(f32[256,1,128]{2,0,1:T(8,128)S(1)} %get-tuple-element.260), channel_id=1, source_target_pairs={{4,0},{8,4},{12,8},{16,12},{20,16},{24,20},{28,24},{32,28},{36,32}... | collective-permute-start | bytes 393224 | tf_op jit(solution)/shard_map/ppermute | solution.py:16
  125.5 2.9 %collective-permute-start.13 = (f32[256,1,128]{2,0,1:T(8,128)S(1)}, f32[256,1,128]{2,0,1:T(8,128)S(1)}, u32[]{:S(2)}, u32[]{:S(2)}) collective-permute-start(f32[256,1,128]{2,0,1:T(8,128)S(1)} %get-tuple-element.263), channel_id=1, source_target_pairs={{8,0},{12,4},{16,8},{20,12},{24,16},{28,20},{32,24},{36,28},{40,32... | collective-permute-start | bytes 393224 | tf_op jit(solution)/shard_map/ppermute | solution.py:16
  129.2 1.6 pad_maximum_fusion
  130.8 1.9 collective-permute-start.10
  132.8 1.6 pad_maximum_fusion.1
  134.4 3.6 %collective-permute-start.8 = (f32[256,1,128]{2,0,1:T(8,128)}, f32[256,1,128]{2,0,1:T(8,128)}, u32[]{:S(2)}, u32[]{:S(2)}) collective-permute-start(f32[256,1,128]{2,0,1:T(8,128)} %get-tuple-element.264), channel_id=1, source_target_pairs={{4,0},{8,4},{12,8},{16,12},{20,16},{24,20},{28,24},{32,28},{36,32}... | collective-permute-start | bytes 393224 | tf_op jit(solution)/shard_map/ppermute | solution.py:16
  138.0 1.9 collective-permute-start.9
  140.0 11.5 %collective-permute-start.11 = (f32[2,256,1,128]{3,1,0,2:T(8,128)}, f32[2,256,1,128]{3,1,0,2:T(8,128)}, u32[]{:S(2)}, u32[]{:S(2)}) collective-permute-start(f32[2,256,1,128]{3,1,0,2:T(8,128)} %pad_maximum_fusion.1), channel_id=1, source_target_pairs={{0,8},{4,12},{8,16},{12,20},{16,24},{20,28},{24,32},{28,36},{32,40... | collective-permute-start | bytes 786440 | tf_op jit(solution)/shard_map/ppermute | solution.py:16
  152.4 12.0 %all-to-all-start.3 = ((bf16[2,256,1,128]{3,0,2,1:T(2,128)(2,1)}), bf16[2,256,1,128]{3,0,2,1:T(2,128)(2,1)S(1)}, u32[]{:S(2)}, u32[]{:S(2)}) async-start(bf16[2,256,1,128]{3,0,2,1:T(2,128)(2,1)} %copy.241), calls=%async_computation.3 | async-start | bytes 262144 | tf_op jit(solution)/shard_map/all_to_all | solution.py:180
  165.5 1.1 fusion.49
  167.4 12.0 %all-to-all-done.3 = bf16[2,256,1,128]{3,0,2,1:T(2,128)(2,1)S(1)} async-done(((bf16[2,256,1,128]{3,0,2,1:T(2,128)(2,1)}), bf16[2,256,1,128]{3,0,2,1:T(2,128)(2,1)S(1)}, u32[]{:S(2)}, u32[]{:S(2)}) %all-to-all-start.3) | async-done | bytes 131104 | tf_op jit(solution)/shard_map/all_to_all | solution.py:180
  179.4 3.3 %all-to-all-start.2 = ((bf16[2,256,1,128]{3,0,2,1:T(2,128)(2,1)}), bf16[2,256,1,128]{3,0,2,1:T(2,128)(2,1)S(1)}, u32[]{:S(2)}, u32[]{:S(2)}) async-start(bf16[2,256,1,128]{3,0,2,1:T(2,128)(2,1)} %copy.232), calls=%async_computation.2 | async-start | bytes 262144 | tf_op jit(solution)/shard_map/all_to_all | solution.py:179
  183.5 1.5 reshape_reshape.14
  185.0 2.0 %copy.217 = bf16[2,256,1,2,4,128]{5,4,3,1,0,2:T(4,128)(2,1)S(1)} copy(bf16[2,256,1,2,4,128]{5,1,4,0,2,3:T(8,128)(2,1)} %bitcast.439) | data formatting | bytes 2097152 | tf_op jit(solution)/shard_map/transpose | solution.py:140
  187.1 1.5 reshape_reshape.15
  189.5 7.8 %all-to-all-done.2 = bf16[2,256,1,128]{3,0,2,1:T(2,128)(2,1)S(1)} async-done(((bf16[2,256,1,128]{3,0,2,1:T(2,128)(2,1)}), bf16[2,256,1,128]{3,0,2,1:T(2,128)(2,1)S(1)}, u32[]{:S(2)}, u32[]{:S(2)}) %all-to-all-start.2) | async-done | bytes 131104 | tf_op jit(solution)/shard_map/all_to_all | solution.py:179
  (140 shorter events, 32.0 us)
Async XLA Ops:
  2.3 29.5 %all-to-all-start.1 = ((bf16[2,64,4,128]{3,1,0,2:T(8,128)(2,1)}), bf16[2,64,4,128]{3,1,0,2:T(8,128)(2,1)S(1)}, u32[]{:S(2)}, u32[]{:S(2)}) async-start(bf16[2,64,4,128]{3,1,0,2:T(8,128)(2,1)} %copy.206), calls=%async_computation.1 | async-start | bytes 262144 | tf_op jit(solution)/shard_map/all_to_all | solution.py:72
  18.9 17.6 %copy-start.9 = (s32[2,256]{1,0:T(2,128)}, s32[2,256]{1,0:T(2,128)S(1)}, u32[]{:S(2)}) copy-start(s32[2,256]{1,0:T(2,128)S(1)} %iota_add_fusion) | copy-start | bytes 6148
  31.8 20.4 %all-to-all-start = ((bf16[2,64,4,128]{3,1,0,2:T(8,128)(2,1)}), bf16[2,64,4,128]{3,1,0,2:T(8,128)(2,1)S(1)}, u32[]{:S(2)}, u32[]{:S(2)}) async-start(bf16[2,64,4,128]{3,1,0,2:T(8,128)(2,1)} %copy.200), calls=%async_computation | async-start | bytes 262144 | tf_op jit(solution)/shard_map/all_to_all | solution.py:71
  40.7 17.7 %collective-permute-start.5 = (bf16[256,1,128]{2,0,1:T(8,128)(2,1)S(1)}, bf16[256,1,128]{2,0,1:T(8,128)(2,1)S(1)}, u32[]{:S(2)}, u32[]{:S(2)}) collective-permute-start(bf16[256,1,128]{2,0,1:T(8,128)(2,1)S(1)} %bitcast.441), channel_id=1, source_target_pairs={{0,8},{4,12},{8,16},{12,20},{16,24},{20,28},{24,32},{28,36},{32,40... | collective-permute-start | bytes 196616 | tf_op jit(solution)/shard_map/ppermute | solution.py:16
  42.7 17.7 %collective-permute-start.4 = (bf16[256,1,128]{2,0,1:T(8,128)(2,1)S(1)}, bf16[256,1,128]{2,0,1:T(8,128)(2,1)}, u32[]{:S(2)}, u32[]{:S(2)}) collective-permute-start(bf16[256,1,128]{2,0,1:T(8,128)(2,1)S(1)} %bitcast.442), channel_id=1, source_target_pairs={{0,4},{4,8},{8,12},{12,16},{16,20},{20,24},{24,28},{28,32},{32,36}... | collective-permute-start | bytes 196616 | tf_op jit(solution)/shard_map/ppermute | solution.py:16
  44.6 23.1 %collective-permute-start.6 = (bf16[2,256,1,128]{3,1,2,0:T(8,128)(2,1)S(1)}, bf16[2,256,1,128]{3,1,2,0:T(8,128)(2,1)}, u32[]{:S(2)}, u32[]{:S(2)}) collective-permute-start(bf16[2,256,1,128]{3,1,2,0:T(8,128)(2,1)S(1)} %bitcast.450), channel_id=1, source_target_pairs={{4,0},{8,4},{12,8},{16,12},{20,16},{24,20},{28,24},{32,28},{36,32}... | collective-permute-start | bytes 393224 | tf_op jit(solution)/shard_map/ppermute | solution.py:16
  48.3 20.4 %collective-permute-start.7 = (bf16[2,256,1,128]{3,1,2,0:T(8,128)(2,1)S(1)}, bf16[2,256,1,128]{3,1,2,0:T(8,128)(2,1)}, u32[]{:S(2)}, u32[]{:S(2)}) collective-permute-start(bf16[2,256,1,128]{3,1,2,0:T(8,128)(2,1)S(1)} %bitcast.451), channel_id=1, source_target_pairs={{8,0},{12,4},{16,8},{20,12},{24,16},{28,20},{32,24},{36,28},{40,32... | collective-permute-start | bytes 393224 | tf_op jit(solution)/shard_map/ppermute | solution.py:16
  52.2 13.5 %collective-permute-start.1 = (bf16[256,1,128]{2,0,1:T(8,128)(2,1)S(1)}, bf16[256,1,128]{2,0,1:T(8,128)(2,1)S(1)}, u32[]{:S(2)}, u32[]{:S(2)}) collective-permute-start(bf16[256,1,128]{2,0,1:T(8,128)(2,1)S(1)} %bitcast.445), channel_id=1, source_target_pairs={{0,8},{4,12},{8,16},{12,20},{16,24},{20,28},{24,32},{28,36},{32,40... | collective-permute-start | bytes 196616 | tf_op jit(solution)/shard_map/ppermute | solution.py:16
  58.4 9.3 %collective-permute-start = (bf16[256,1,128]{2,0,1:T(8,128)(2,1)S(1)}, bf16[256,1,128]{2,0,1:T(8,128)(2,1)S(1)}, u32[]{:S(2)}, u32[]{:S(2)}) collective-permute-start(bf16[256,1,128]{2,0,1:T(8,128)(2,1)S(1)} %bitcast.446), channel_id=1, source_target_pairs={{0,4},{4,8},{8,12},{12,16},{16,20},{20,24},{24,28},{28,32},{32,36}... | collective-permute-start | bytes 196616 | tf_op jit(solution)/shard_map/ppermute | solution.py:16
  60.4 9.1 %collective-permute-start.2 = (bf16[2,256,1,128]{3,1,2,0:T(8,128)(2,1)S(1)}, bf16[2,256,1,128]{3,1,2,0:T(8,128)(2,1)S(1)}, u32[]{:S(2)}, u32[]{:S(2)}) collective-permute-start(bf16[2,256,1,128]{3,1,2,0:T(8,128)(2,1)S(1)} %bitcast.453), channel_id=1, source_target_pairs={{4,0},{8,4},{12,8},{16,12},{20,16},{24,20},{28,24},{32,28},{36,32}... | collective-permute-start | bytes 393224 | tf_op jit(solution)/shard_map/ppermute | solution.py:16
  65.7 11.4 %collective-permute-start.3 = (bf16[2,256,1,128]{3,1,0,2:T(8,128)(2,1)S(1)}, bf16[2,256,1,128]{3,1,0,2:T(8,128)(2,1)S(1)}, u32[]{:S(2)}, u32[]{:S(2)}) collective-permute-start(bf16[2,256,1,128]{3,1,0,2:T(8,128)(2,1)S(1)} %bitcast.454), channel_id=1, source_target_pairs={{8,0},{12,4},{16,8},{20,12},{24,16},{28,20},{32,24},{36,28},{40,32... | collective-permute-start | bytes 393224 | tf_op jit(solution)/shard_map/ppermute | solution.py:16
  78.4 3.4 %copy-start.2 = (f32[2,2,768,1,128]{2,4,1,3,0:T(8,128)S(1)}, f32[2,2,768,1,128]{2,4,1,3,0:T(8,128)}, u32[]{:S(2)}) copy-start(f32[2,2,768,1,128]{2,4,1,3,0:T(8,128)} %get-tuple-element.395) | copy-start | bytes 4718596 | tf_op jit(solution)/shard_map/while
  81.8 3.2 %copy-start.8 = (bf16[2,768,1,128]{3,1,0,2:T(8,128)(2,1)S(1)}, bf16[2,768,1,128]{3,1,0,2:T(8,128)(2,1)}, u32[]{:S(2)}) copy-start(bf16[2,768,1,128]{3,1,0,2:T(8,128)(2,1)} %get-tuple-element.413) | copy-start | bytes 1179652 | tf_op jit(solution)/shard_map/while
  83.9 1.1 copy-start.3
  87.2 2.9 %copy-start = (f32[2,2,768,1,128]{2,4,1,3,0:T(8,128)S(1)}, f32[2,2,768,1,128]{2,4,1,3,0:T(8,128)}, u32[]{:S(2)}) copy-start(f32[2,2,768,1,128]{2,4,1,3,0:T(8,128)} %get-tuple-element.394) | copy-start | bytes 4718596 | tf_op jit(solution)/shard_map/while
  87.4 3.4 %copy-start.6 = (bf16[2,2,256,1,4,128]{5,2,4,1,3,0:T(8,128)(2,1)S(1)}, bf16[2,2,256,1,4,128]{5,2,4,1,3,0:T(8,128)(2,1)}, u32[]{:S(2)}) copy-start(bf16[2,2,256,1,4,128]{5,2,4,1,3,0:T(8,128)(2,1)} %get-tuple-element.393) | copy-start | bytes 3145732 | tf_op jit(solution)/shard_map/while
  90.7 1.2 copy-start.1
  91.9 1.0 copy-start.7
  94.0 3.4 %copy-start.2 = (f32[2,2,768,1,128]{2,4,1,3,0:T(8,128)S(1)}, f32[2,2,768,1,128]{2,4,1,3,0:T(8,128)}, u32[]{:S(2)}) copy-start(f32[2,2,768,1,128]{2,4,1,3,0:T(8,128)} %get-tuple-element.395) | copy-start | bytes 4718596 | tf_op jit(solution)/shard_map/while
  97.4 3.2 %copy-start.8 = (bf16[2,768,1,128]{3,1,0,2:T(8,128)(2,1)S(1)}, bf16[2,768,1,128]{3,1,0,2:T(8,128)(2,1)}, u32[]{:S(2)}) copy-start(bf16[2,768,1,128]{3,1,0,2:T(8,128)(2,1)} %get-tuple-element.413) | copy-start | bytes 1179652 | tf_op jit(solution)/shard_map/while
  99.5 1.1 copy-start.3
  102.8 2.9 %copy-start = (f32[2,2,768,1,128]{2,4,1,3,0:T(8,128)S(1)}, f32[2,2,768,1,128]{2,4,1,3,0:T(8,128)}, u32[]{:S(2)}) copy-start(f32[2,2,768,1,128]{2,4,1,3,0:T(8,128)} %get-tuple-element.394) | copy-start | bytes 4718596 | tf_op jit(solution)/shard_map/while
  103.0 3.4 %copy-start.6 = (bf16[2,2,256,1,4,128]{5,2,4,1,3,0:T(8,128)(2,1)S(1)}, bf16[2,2,256,1,4,128]{5,2,4,1,3,0:T(8,128)(2,1)}, u32[]{:S(2)}) copy-start(bf16[2,2,256,1,4,128]{5,2,4,1,3,0:T(8,128)(2,1)} %get-tuple-element.393) | copy-start | bytes 3145732 | tf_op jit(solution)/shard_map/while
  106.3 1.2 copy-start.1
  107.5 1.0 copy-start.7
  108.5 1.9 copy-start.4
  108.5 5.2 %copy-start.10 = (pred[5]{0:T(512)(128)(4,1)S(1)}, pred[5]{0:T(512)(128)(4,1)}, u32[]{:S(2)}) copy-start(pred[5]{0:T(512)(128)(4,1)} %get-tuple-element.281) | copy-start | bytes 19
  108.5 5.2 %copy-start.11 = (pred[5]{0:T(512)(128)(4,1)S(1)}, pred[5]{0:T(512)(128)(4,1)}, u32[]{:S(2)}) copy-start(pred[5]{0:T(512)(128)(4,1)} %get-tuple-element.282) | copy-start | bytes 19
  114.8 18.0 %slice-start = ((f32[5,256,1,128]{3,1,0,2:T(8,128)}), f32[1,256,1,128]{3,1,0,2:T(8,128)S(1)}, s32[]{:S(2)}) async-start(f32[5,256,1,128]{3,1,0,2:T(8,128)} %bitcast_add_fusion), calls=%async_computation.4 | async-start | bytes 262144 | tf_op jit(solution)/shard_map/slice | solution.py:169
  115.1 67.6 %copy-start.5 = (bf16[2,2,256,1,4,128]{2,5,4,1,3,0:T(8,128)(2,1)S(1)}, bf16[2,2,256,1,4,128]{2,5,4,1,3,0:T(8,128)(2,1)}, u32[]{:S(2)}) copy-start(bf16[2,2,256,1,4,128]{2,5,4,1,3,0:T(8,128)(2,1)} %copy-done.4) | copy-start | bytes 3145732
  116.2 23.8 %collective-permute-start.14 = (f32[2,256,1,128]{3,1,2,0:T(8,128)S(1)}, f32[2,256,1,128]{3,1,2,0:T(8,128)S(1)}, u32[]{:S(2)}, u32[]{:S(2)}) collective-permute-start(f32[2,256,1,128]{3,1,2,0:T(8,128)S(1)} %pad_maximum_fusion.2), channel_id=1, source_target_pairs={{0,4},{4,8},{8,12},{12,16},{16,20},{20,24},{24,28},{28,32},{32,36}... | collective-permute-start | bytes 786440 | tf_op jit(solution)/shard_map/ppermute | solution.py:16
  119.1 32.5 %collective-permute-start.15 = (f32[2,256,1,128]{3,1,2,0:T(8,128)S(1)}, f32[2,256,1,128]{3,1,2,0:T(8,128)S(1)}, u32[]{:S(2)}, u32[]{:S(2)}) collective-permute-start(f32[2,256,1,128]{3,1,2,0:T(8,128)S(1)} %pad_maximum_fusion.3), channel_id=1, source_target_pairs={{0,8},{4,12},{8,16},{12,20},{16,24},{20,28},{24,32},{28,36},{32,40... | collective-permute-start | bytes 786440 | tf_op jit(solution)/shard_map/ppermute | solution.py:16
  122.2 12.2 %collective-permute-start.12 = (f32[256,1,128]{2,0,1:T(8,128)S(1)}, f32[256,1,128]{2,0,1:T(8,128)S(1)}, u32[]{:S(2)}, u32[]{:S(2)}) collective-permute-start(f32[256,1,128]{2,0,1:T(8,128)S(1)} %get-tuple-element.260), channel_id=1, source_target_pairs={{4,0},{8,4},{12,8},{16,12},{20,16},{24,20},{28,24},{32,28},{36,32}... | collective-permute-start | bytes 393224 | tf_op jit(solution)/shard_map/ppermute | solution.py:16
  125.5 12.5 %collective-permute-start.13 = (f32[256,1,128]{2,0,1:T(8,128)S(1)}, f32[256,1,128]{2,0,1:T(8,128)S(1)}, u32[]{:S(2)}, u32[]{:S(2)}) collective-permute-start(f32[256,1,128]{2,0,1:T(8,128)S(1)} %get-tuple-element.263), channel_id=1, source_target_pairs={{8,0},{12,4},{16,8},{20,12},{24,16},{28,20},{32,24},{36,28},{40,32... | collective-permute-start | bytes 393224 | tf_op jit(solution)/shard_map/ppermute | solution.py:16
  130.8 33.6 %collective-permute-start.10 = (f32[2,256,1,128]{3,1,2,0:T(8,128)}, f32[2,256,1,128]{3,1,2,0:T(8,128)}, u32[]{:S(2)}, u32[]{:S(2)}) collective-permute-start(f32[2,256,1,128]{3,1,2,0:T(8,128)} %pad_maximum_fusion), channel_id=1, source_target_pairs={{0,4},{4,8},{8,12},{12,16},{16,20},{20,24},{24,28},{28,32},{32,36}... | collective-permute-start | bytes 786440 | tf_op jit(solution)/shard_map/ppermute | solution.py:16
  134.4 31.0 %collective-permute-start.8 = (f32[256,1,128]{2,0,1:T(8,128)}, f32[256,1,128]{2,0,1:T(8,128)}, u32[]{:S(2)}, u32[]{:S(2)}) collective-permute-start(f32[256,1,128]{2,0,1:T(8,128)} %get-tuple-element.264), channel_id=1, source_target_pairs={{4,0},{8,4},{12,8},{16,12},{20,16},{24,20},{28,24},{32,28},{36,32}... | collective-permute-start | bytes 393224 | tf_op jit(solution)/shard_map/ppermute | solution.py:16
  138.0 27.4 %collective-permute-start.9 = (f32[256,1,128]{2,0,1:T(8,128)}, f32[256,1,128]{2,0,1:T(8,128)}, u32[]{:S(2)}, u32[]{:S(2)}) collective-permute-start(f32[256,1,128]{2,0,1:T(8,128)} %get-tuple-element.266), channel_id=1, source_target_pairs={{8,0},{12,4},{16,8},{20,12},{24,16},{28,20},{32,24},{36,28},{40,32... | collective-permute-start | bytes 393224 | tf_op jit(solution)/shard_map/ppermute | solution.py:16
  140.0 24.5 %collective-permute-start.11 = (f32[2,256,1,128]{3,1,0,2:T(8,128)}, f32[2,256,1,128]{3,1,0,2:T(8,128)}, u32[]{:S(2)}, u32[]{:S(2)}) collective-permute-start(f32[2,256,1,128]{3,1,0,2:T(8,128)} %pad_maximum_fusion.1), channel_id=1, source_target_pairs={{0,8},{4,12},{8,16},{12,20},{16,24},{20,28},{24,32},{28,36},{32,40... | collective-permute-start | bytes 786440 | tf_op jit(solution)/shard_map/ppermute | solution.py:16
  152.4 27.0 %all-to-all-start.3 = ((bf16[2,256,1,128]{3,0,2,1:T(2,128)(2,1)}), bf16[2,256,1,128]{3,0,2,1:T(2,128)(2,1)S(1)}, u32[]{:S(2)}, u32[]{:S(2)}) async-start(bf16[2,256,1,128]{3,0,2,1:T(2,128)(2,1)} %copy.241), calls=%async_computation.3 | async-start | bytes 262144 | tf_op jit(solution)/shard_map/all_to_all | solution.py:180
  179.4 17.9 %all-to-all-start.2 = ((bf16[2,256,1,128]{3,0,2,1:T(2,128)(2,1)}), bf16[2,256,1,128]{3,0,2,1:T(2,128)(2,1)S(1)}, u32[]{:S(2)}, u32[]{:S(2)}) async-start(bf16[2,256,1,128]{3,0,2,1:T(2,128)(2,1)} %copy.232), calls=%async_computation.2 | async-start | bytes 262144 | tf_op jit(solution)/shard_map/all_to_all | solution.py:179
where the time goes:
time: 200 us; the launch traced here: 198 us
  starting transfers between devices  90 us (45%)
  waiting for transfers between devices  34.6 us (17%)
  other arithmetic  26.5 us (13%)
  local copies, waits for them, and re-layouts  25 us (12%)
  matrix products  20.4 us (10%)
    ppermute x16, starting transfers between devices, from_behind(): return lax.ppermute(block, axis, route)  55.4 us
    all_to_all x1, starting transfers between devices, local(): lax.all_to_all(value_split, 'tp', split_axis=2, concat_axis=1, tiled=True)  15.1 us
    all_to_all x1, starting transfers between devices, local(): lax.all_to_all(value_total, 'tp', split_axis=1, concat_axis=2, tiled=True)  12 us
    all_to_all x1, waiting for transfers between devices, local(): lax.all_to_all(value_total, 'tp', split_axis=1, concat_axis=2, tiled=True)  12 us
    all_to_all x1, waiting for transfers between devices, local(): lax.all_to_all(value_split, 'tp', split_axis=2, concat_axis=1, tiled=True)  9.78 us
    all_to_all x1, waiting for transfers between devices, local(): lax.all_to_all(key_total, 'tp', split_axis=1, concat_axis=2, tiled=True)  7.79 us
    dot_general x2, matrix products, attend_block(): jnp.einsum('hqgrd,hkgd->hqgrk', grad_part, value_rows, preferred_element_...  5.42 us
    ppermute x16, waiting for transfers between devices, from_behind(): return lax.ppermute(block, axis, route)  5.1 us
  transfers between devices with their start and end apart: 20, of which 4 were waited for; matrix products, arithmetic and copies ran while one was open for 16% of the time, Pallas kernels for 0%

commit v1 on v0

v1 whole, which is shorter than its diff:
```python
import functools
import math

import jax
import jax.numpy as jnp
from jax import lax
from jax.experimental import pallas as pl
from jax.experimental.pallas import tpu as pltpu
from jax.sharding import PartitionSpec as P

KV = 4
HD = 128
HEADS_STEP = 2
FACTOR = 1.0 / math.sqrt(HD)
LOG2E = math.log2(math.e)
OUT = -1e30
VMEM = pl.BlockSpec(memory_space=pltpu.VMEM)
FIRST, SECOND = 0, 1


def from_behind(block, axis, distance):
    devices = range(lax.axis_size(axis))
    route = [(i - distance, i) for i in devices if i - distance in devices]
    return lax.ppermute(block, axis, route)


def around(block, axis, distance):
    count = lax.axis_size(axis)
    return lax.ppermute(block, axis, [(i, (i + distance) % count) for i in range(count)])


def dot(a, b, contract):
    return lax.dot_general(a, b, (contract, ((), ())), preferred_element_type=jnp.float32)


def split_kernel(groups, k_ref, v_ref, *pieces):
    tp = lax.axis_index("tp")
    for step, piece in enumerate(pieces, 1):
        lanes = pl.ds(pl.multiple_of(lax.rem(tp + step, groups) * HD, HD), HD)
        piece[:, 0] = k_ref[:, 0, :, lanes]
        piece[:, 1] = v_ref[:, 0, :, lanes]


def join_kernel(groups, k_ref, v_ref, *refs):
    pieces, (both_ref, first_ref, second_ref) = refs[:-3], refs[-3:]
    tp = lax.axis_index("tp")
    rows = k_ref.shape[2]
    lanes = pl.ds(pl.multiple_of(tp * HD, HD), HD)
    place = pl.ds(pl.multiple_of(tp * rows, rows), rows)
    for kind, ref in enumerate((k_ref, v_ref)):
        for half, out in enumerate((first_ref, second_ref)):
            own = ref[half, 0, :, lanes]
            both_ref[half, kind, place, :] = own
            out[kind, place, :] = own
    for step, piece in enumerate(pieces, 1):
        place = pl.ds(pl.multiple_of(lax.rem(tp - step + groups, groups) * rows, rows), rows)
        both_ref[:, :, place, :] = piece[...]
        first_ref[:, place, :] = piece[FIRST]
        second_ref[:, place, :] = piece[SECOND]


def total_kernel(groups, own_ref, up1_ref, up2_ref, down1_ref, down2_ref, *pieces):
    tp = lax.axis_index("tp")
    rows = pieces[0].shape[2]
    for step, piece in enumerate(pieces):
        place = pl.ds(pl.multiple_of(lax.rem(tp + step, groups) * rows, rows), rows)
        for kind in range(2):
            first = (
                own_ref[FIRST, kind, place, :]
                + up1_ref[kind, place, :].astype(jnp.float32)
                + up2_ref[kind, place, :].astype(jnp.float32)
                + down1_ref[1, kind, place, :].astype(jnp.float32)
            )
            second = (
                own_ref[SECOND, kind, place, :]
                + down1_ref[0, kind, place, :].astype(jnp.float32)
                + down2_ref[kind, place, :].astype(jnp.float32)
            )
            piece[FIRST, kind] = first.astype(piece.dtype)
            piece[SECOND, kind] = second.astype(piece.dtype)


def place_kernel(groups, *refs):
    pieces, (k_ref, v_ref) = refs[:-2], refs[-2:]
    tp = lax.axis_index("tp")
    for step, piece in enumerate(pieces):
        lanes = pl.ds(pl.multiple_of(lax.rem(tp - step + groups, groups) * HD, HD), HD)
        k_ref[:, 0, :, lanes] = piece[:, 0]
        v_ref[:, 0, :, lanes] = piece[:, 1]


def blend(field, side):
    low = side // 2
    row = lax.broadcasted_iota(jnp.int32, (low, low), 0)
    column = lax.broadcasted_iota(jnp.int32, (low, low), 1)
    causal = column <= row
    old, own = field[:, :side], field[:, 2 * side :]
    top = jnp.concatenate(
        [jnp.where(causal, own[:low, :low], old[:low, :low]), old[:low, low:]], axis=1
    )
    bottom = jnp.concatenate(
        [own[low:, :low], jnp.where(causal, own[low:, low:], old[low:, low:])], axis=1
    )
    shared = jnp.concatenate([top, bottom], axis=0)
    return jnp.concatenate([shared, field[:, side : 2 * side]], axis=1)


def unblend(field, side):
    low = side // 2
    row = lax.broadcasted_iota(jnp.int32, (low, low), 0)
    column = lax.broadcasted_iota(jnp.int32, (low, low), 1)
    causal = column <= row
    bf = jnp.bfloat16
    none = jnp.zeros((low, low), bf)
    a, d = field[:low, :low], field[low:, low : 2 * low]
    b, c = field[:low, low : 2 * low].astype(bf), field[low:, :low].astype(bf)
    a_own, a_old = jnp.where(causal, a, 0.0).astype(bf), jnp.where(causal, 0.0, a).astype(bf)
    d_own, d_old = jnp.where(causal, d, 0.0).astype(bf), jnp.where(causal, 0.0, d).astype(bf)
    old = jnp.concatenate(
        [jnp.concatenate([a_old, b], axis=1), jnp.concatenate([none, d_old], axis=1)], axis=0
    )
    own = jnp.concatenate(
        [jnp.concatenate([a_own, none], axis=1), jnp.concatenate([c, d_own], axis=1)], axis=0
    )
    return jnp.concatenate([old, field[:, side:].astype(bf), own], axis=1)


def attend_kernel(
    contexts,
    len_ref,
    q_ref,
    g_ref,
    first_ref,
    second_ref,
    up1_ref,
    up2_ref,
    down1_ref,
    down2_ref,
    attn_ref,
    dq_ref,
    own_ref,
    sup1_ref,
    sup2_ref,
    sdown1_ref,
    sdown2_ref,
    k_ref,
    v_ref,
    bias_ref,
    dk_ref,
    dv_ref,
    fold_ref,
):
    side = q_ref.shape[2]
    cp = lax.axis_index("cp")
    last = contexts - 1
    turn, part = pl.program_id(0), pl.program_id(1)
    half = 1 - turn
    block = jnp.where(half == FIRST, cp, 2 * contexts - 1 - cp)
    bf = jnp.bfloat16

    def keep(oldest, middle, own):
        for kind, ref in enumerate((k_ref, v_ref)):
            ref[0:side, :] = oldest(kind)
            ref[side : 2 * side, :] = middle(kind)
            ref[2 * side :, :] = own(kind)

    @pl.when((part == 0) & (half == FIRST))
    def _():
        keep(lambda n: up2_ref[n], lambda n: up1_ref[n], lambda n: first_ref[n])

    @pl.when((part == 0) & (half == SECOND))
    def _():
        @pl.when(cp < last - 1)
        def _():
            keep(lambda n: down2_ref[n], lambda n: down1_ref[SECOND, n], lambda n: second_ref[n])

        @pl.when(cp == last - 1)
        def _():
            keep(
                lambda n: down1_ref[FIRST, n],
                lambda n: down1_ref[SECOND, n],
                lambda n: second_ref[n],
            )

        @pl.when(cp == last)
        def _():
            keep(lambda n: up1_ref[n], lambda n: first_ref[n], lambda n: second_ref[n])

    @pl.when(part == 0)
    def _():
        docs = len_ref.shape[1]
        lengths = jnp.broadcast_to(len_ref[...], (8, docs))
        before = lax.broadcasted_iota(jnp.int32, (docs, docs), 0)
        after = lax.broadcasted_iota(jnp.int32, (docs, docs), 1)
        upto = (before <= after).astype(jnp.float32).astype(bf)
        coarse = (lengths // 16).astype(jnp.float32).astype(bf)
        fine = (lengths % 16).astype(jnp.float32).astype(bf)
        over = ((1,), (0,))
        ends = (16.0 * dot(coarse, upto, over) + dot(fine, upto, over))[0:1, :]
        row = lax.broadcasted_iota(jnp.int32, (side, docs), 0)
        position = (row + block * side).astype(jnp.float32)
        begins = jnp.max(jnp.where(ends <= position, ends, 0.0), axis=1, keepdims=True)
        begins = begins - (block * side).astype(jnp.float32)
        row = lax.broadcasted_iota(jnp.int32, (side, side), 0)
        column = lax.broadcasted_iota(jnp.int32, (side, side), 1)
        key = column.astype(jnp.float32)
        shared = jnp.where(column <= row, key, key - 2.0 * side)
        bias_ref[:, :side] = jnp.where(shared >= begins, 0.0, OUT)
        bias_ref[:, side:] = jnp.where(key - side >= begins, 0.0, OUT)
        dk_ref[...] = jnp.zeros_like(dk_ref)
        dv_ref[...] = jnp.zeros_like(dv_ref)

    keys, values = k_ref[...], v_ref[...]
    along, across = ((1,), (1,)), ((1,), (0,))
    rows_q, rows_g, probs_all, ds_all = [], [], [], []
    for head in range(HEADS_STEP):
        lanes = slice(head * HD, (head + 1) * HD)
        q, g = q_ref[0, 0, :, lanes], g_ref[0, 0, :, lanes]
        scores = blend(dot(q, keys, along), side) * (FACTOR * LOG2E) + bias_ref[...]
        top = jnp.max(scores, axis=1, keepdims=True)
        raised = jnp.exp2(scores - top)
        probs = raised * (1.0 / jnp.sum(raised, axis=1, keepdims=True))
        probs_low = unblend(probs, side)
        attn = dot(probs_low, values, across).astype(bf)
        attn_ref[0, 0, :, lanes] = attn
        delta = jnp.sum(attn.astype(jnp.float32) * g.astype(jnp.float32), axis=1, keepdims=True)
        ds = unblend(probs * (blend(dot(g, values, along), side) - delta), side)
        dq_ref[0, 0, :, lanes] = (dot(ds, keys, across) * FACTOR).astype(bf)
        rows_q.append(q)
        rows_g.append(g)
        probs_all.append(probs_low)
        ds_all.append(ds)
    down = ((0,), (0,))
    dv_ref[...] += dot(jnp.concatenate(rows_g, 0), jnp.concatenate(probs_all, 0), down)
    dk_ref[...] += dot(jnp.concatenate(rows_q, 0), jnp.concatenate(ds_all, 0), down)

    @pl.when(part == pl.num_programs(1) - 1)
    def _():
        terms = (dk_ref[...].T * FACTOR, dv_ref[...].T)

        @pl.when(half == SECOND)
        def _():
            for kind, term in enumerate(terms):
                oldest, middle = term[:side], term[side : 2 * side]
                own_ref[SECOND, kind] = term[2 * side :]
                sdown1_ref[0, kind] = middle.astype(bf)
                sdown1_ref[1, kind] = jnp.where(cp == last - 1, oldest, 0.0).astype(bf)
                sdown2_ref[kind] = oldest.astype(bf)
                fold_ref[kind] = jnp.where(cp == last, term[: 2 * side], 0.0)

        @pl.when(half == FIRST)
        def _():
            for kind, term in enumerate(terms):
                own_ref[FIRST, kind] = term[2 * side :] + fold_ref[kind, side:, :]
                sup1_ref[kind] = (term[side : 2 * side] + fold_ref[kind, :side, :]).astype(bf)
                sup2_ref[kind] = term[:side].astype(bf)


def local(queries, keys, values, out_grad, doc_lengths):
    side, width = queries.shape[2], queries.shape[3]
    contexts, groups = lax.axis_size("cp"), lax.axis_size("tp")
    rows = keys.shape[2]
    bf = jnp.bfloat16
    shape = jax.ShapeDtypeStruct
    piece = shape((2, 2, rows, HD), bf)
    one = shape((2, side, HD), bf)
    two = shape((2, 2, side, HD), bf)

    sent = pl.pallas_call(
        functools.partial(split_kernel, groups),
        out_shape=[piece] * (groups - 1),
        in_specs=[VMEM] * 2,
        out_specs=[VMEM] * (groups - 1),
        name="split",
    )(keys, values)
    came = [around(block, "tp", step) for step, block in enumerate(sent, 1)]
    both, first, second = pl.pallas_call(
        functools.partial(join_kernel, groups),
        out_shape=[two, one, one],
        in_specs=[VMEM] * (groups + 1),
        out_specs=[VMEM] * 3,
        name="join",
    )(keys, values, *came)
    up1 = from_behind(first, "cp", 1)
    up2 = from_behind(first, "cp", 2)
    down1 = from_behind(both, "cp", -1)
    down2 = from_behind(second, "cp", -2)

    lanes = HEADS_STEP * HD
    wide = pl.BlockSpec((1, 1, side, lanes), lambda turn, part: (1 - turn, 0, 0, part))
    work = 2 * (width // HD) * side * 3 * side
    attn_out, q_grad, own, sup1, sup2, sdown1, sdown2 = pl.pallas_call(
        functools.partial(attend_kernel, contexts),
        grid=(2, width // lanes),
        out_shape=[
            shape(queries.shape, bf),
            shape(queries.shape, bf),
            shape((2, 2, side, HD), jnp.float32),
            one,
            one,
            two,
            one,
        ],
        in_specs=[VMEM, wide, wide] + [VMEM] * 6,
        out_specs=[wide, wide] + [VMEM] * 5,
        scratch_shapes=[
            pltpu.VMEM((3 * side, HD), bf),
            pltpu.VMEM((3 * side, HD), bf),
            pltpu.VMEM((side, 2 * side), jnp.float32),
            pltpu.VMEM((HD, 3 * side), jnp.float32),
            pltpu.VMEM((HD, 3 * side), jnp.float32),
            pltpu.VMEM((2, 2 * side, HD), jnp.float32),
        ],
        compiler_params=pltpu.CompilerParams(vmem_limit_bytes=40 * 2**20),
        cost_estimate=pl.CostEstimate(
            flops=12 * work * HD, bytes_accessed=8 * side * width * 2, transcendentals=work
        ),
        name="attend",
    )(doc_lengths[None, :], queries, out_grad, first, second, up1, up2, down1, down2)

    back_up1 = from_behind(sup1, "cp", -1)
    back_up2 = from_behind(sup2, "cp", -2)
    back_down1 = from_behind(sdown1, "cp", 1)
    back_down2 = from_behind(sdown2, "cp", 2)
    pieces = pl.pallas_call(
        functools.partial(total_kernel, groups),
        out_shape=[piece] * groups,
        in_specs=[VMEM] * 5,
        out_specs=[VMEM] * groups,
        name="total",
    )(own, back_up1, back_up2, back_down1, back_down2)
    returned = [pieces[0]] + [around(block, "tp", step) for step, block in enumerate(pieces[1:], 1)]
    k_grad, v_grad = pl.pallas_call(
        functools.partial(place_kernel, groups),
        out_shape=[shape(keys.shape, bf)] * 2,
        in_specs=[VMEM] * groups,
        out_specs=[VMEM] * 2,
        name="place",
    )(*returned)
    return (attn_out, q_grad, k_grad, v_grad)


def solution(mesh):
    heads, tokens = P(None, "cp", None, "tp"), P(None, "cp", "tp", None)
    return jax.shard_map(
        local,
        mesh=mesh,
        in_specs=(heads, tokens, tokens, heads, P()),
        out_specs=(heads, heads, tokens, tokens),
        check_vma=False,
    )
```

time: 200 us -> 140 us (0.70)
  the two profiles are of different devices: /device:TPU:30 before, /device:TPU:32 now
where the time goes in v1:
time: 140 us; the launch traced here: 139 us
  starting transfers between devices  76.8 us (55%)
  waiting for transfers between devices  28.4 us (20%)
  Pallas kernels  26.2 us (19%)
  local copies, waits for them, and re-layouts  7.08 us (5%)
    ppermute x6, starting transfers between devices, around(): lax.ppermute(block, axis, [(i, (i + distance) % count) for i in range(cou...  43.8 us
    ppermute x8, starting transfers between devices, from_behind(): return lax.ppermute(block, axis, route)  33 us
    pallas_call x1, Pallas kernels, local(): pl.pallas_call(functools.partial(attend_kernel, contexts), grid=(2, width...  19 us
    ppermute x8, waiting for transfers between devices, from_behind(): return lax.ppermute(block, axis, route)  16.5 us
    ppermute x6, waiting for transfers between devices, around(): lax.ppermute(block, axis, [(i, (i + distance) % count) for i in range(cou...  12 us
    unnamed x32, local copies, waits for them, and re-layouts  7.08 us
  transfers between devices with their start and end apart: 14, of which 7 were waited for; matrix products, arithmetic and copies ran while one was open for 0% of the time, Pallas kernels for 0%

profile of v1, /device:TPU:32, one launch (start us, length us, event | category | flops | bytes accessed | tf_op | source)
XLA Modules:
  0.0 139.4 jit_solution(1312873755296275162)
XLA Ops:
  0.6 1.7 %split.1 = (bf16[2,2,64,128]{3,2,1,0:T(8,128)(2,1)}, bf16[2,2,64,128]{3,2,1,0:T(8,128)(2,1)}, bf16[2,2,64,128]{3,2,1,0:T(8,128)(2,1)}) custom-call(bf16[2,1,64,512]{3,2,1,0:T(8,128)(2,1)} %k_ref.3, bf16[2,1,64,512]{3,2,1,0:T(8,128)(2,1)} %v_ref.3), custom_call_target="tpu_custom_call" | custom-call | tf_op jit(solution)/shard_map/split/pallas_call | solution.py:269
  2.3 9.1 %collective-permute-start = (bf16[2,2,64,128]{3,2,1,0:T(8,128)(2,1)}, bf16[2,2,64,128]{3,2,1,0:T(8,128)(2,1)S(1)}, u32[]{:S(2)}, u32[]{:S(2)}) collective-permute-start(bf16[2,2,64,128]{3,2,1,0:T(8,128)(2,1)} %get-tuple-element.23), channel_id=1, source_target_pairs={{0,1},{1,2},{2,3},{3,0},{4,5},{5,6},{6,7},{7,4},{8,9},{9,10},{10,1... | collective-permute-start | bytes 196616 | tf_op jit(solution)/shard_map/ppermute | solution.py:29
  11.4 10.0 %collective-permute-start.1 = (bf16[2,2,64,128]{3,2,1,0:T(8,128)(2,1)}, bf16[2,2,64,128]{3,2,1,0:T(8,128)(2,1)S(1)}, u32[]{:S(2)}, u32[]{:S(2)}) collective-permute-start(bf16[2,2,64,128]{3,2,1,0:T(8,128)(2,1)} %get-tuple-element.24), channel_id=1, source_target_pairs={{0,2},{1,3},{2,0},{3,1},{4,6},{5,7},{6,4},{7,5},{8,10},{9,11},{10,... | collective-permute-start | bytes 196616 | tf_op jit(solution)/shard_map/ppermute | solution.py:29
  21.4 5.5 %collective-permute-start.2 = (bf16[2,2,64,128]{3,2,1,0:T(8,128)(2,1)}, bf16[2,2,64,128]{3,2,1,0:T(8,128)(2,1)S(1)}, u32[]{:S(2)}, u32[]{:S(2)}) collective-permute-start(bf16[2,2,64,128]{3,2,1,0:T(8,128)(2,1)} %get-tuple-element.25), channel_id=1, source_target_pairs={{0,3},{1,0},{2,1},{3,2},{4,7},{5,4},{6,5},{7,6},{8,11},{9,8},{10,9... | collective-permute-start | bytes 196616 | tf_op jit(solution)/shard_map/ppermute | solution.py:29
  26.9 0.0 collective-permute-done.refs_0_
  26.9 0.0 copy-start.10
  26.9 0.0 collective-permute-done.1.refs_1_
  26.9 5.5 %collective-permute-done.2.refs_2_ = bf16[2,2,64,128]{3,2,1,0:T(8,128)(2,1)S(1)} collective-permute-done((bf16[2,2,64,128]{3,2,1,0:T(8,128)(2,1)}, bf16[2,2,64,128]{3,2,1,0:T(8,128)(2,1)S(1)}, u32[]{:S(2)}, u32[]{:S(2)}) %collective-permute-start.2) | collective-permute-done | bytes 65568 | tf_op jit(solution)/shard_map/ppermute | solution.py:29
  32.5 0.0 copy-done.10
  32.5 0.6 copy-done.12
  33.1 1.9 %join.1 = (bf16[2,2,256,128]{3,2,1,0:T(8,128)(2,1)}, bf16[2,256,128]{2,1,0:T(8,128)(2,1)}, bf16[2,256,128]{2,1,0:T(8,128)(2,1)}) custom-call(bf16[2,1,64,512]{3,2,1,0:T(8,128)(2,1)} %k_ref.3, bf16[2,1,64,512]{3,2,1,0:T(8,128)(2,1)} %v_ref.3, bf16[2,2,64,128]{3,2,1,0:T(8,128)(2,1)} %copy-done.10, bf16[2,2,64,128]{3,2,1,0:T(8,128)(2,1)} %copy-done.11, ...), custom_call_target="tpu_custom_call" | custom-call | tf_op jit(solution)/shard_map/join/pallas_call | solution.py:277
  35.0 9.6 %collective-permute-start.5 = (bf16[2,2,256,128]{3,2,1,0:T(8,128)(2,1)}, bf16[2,2,256,128]{3,2,1,0:T(8,128)(2,1)S(1)}, u32[]{:S(2)}, u32[]{:S(2)}) collective-permute-start(bf16[2,2,256,128]{3,2,1,0:T(8,128)(2,1)} %get-tuple-element.28), channel_id=1, source_target_pairs={{4,0},{8,4},{12,8},{16,12},{20,16},{24,20},{28,24},{32,28},{36,32}... | collective-permute-start | bytes 786440 | tf_op jit(solution)/shard_map/ppermute | solution.py:24
  44.6 2.7 %collective-permute-start.6 = (bf16[2,256,128]{2,1,0:T(8,128)(2,1)}, bf16[2,256,128]{2,1,0:T(8,128)(2,1)S(1)}, u32[]{:S(2)}, u32[]{:S(2)}) collective-permute-start(bf16[2,256,128]{2,1,0:T(8,128)(2,1)} %get-tuple-element.27.second_ref), channel_id=1, source_target_pairs={{8,0},{12,4},{16,8},{20,12},{24,16},{28,20},{32,24},{36,28},{40,32... | collective-permute-start | bytes 393224 | tf_op jit(solution)/shard_map/ppermute | solution.py:24
  47.4 0.0 copy-start.5
  47.4 3.1 %collective-permute-start.4 = (bf16[2,256,128]{2,1,0:T(8,128)(2,1)}, bf16[2,256,128]{2,1,0:T(8,128)(2,1)S(1)}, u32[]{:S(2)}, u32[]{:S(2)}) collective-permute-start(bf16[2,256,128]{2,1,0:T(8,128)(2,1)} %get-tuple-element.26.first_ref), channel_id=1, source_target_pairs={{0,8},{4,12},{8,16},{12,20},{16,24},{20,28},{24,32},{28,36},{32,40... | collective-permute-start | bytes 393224 | tf_op jit(solution)/shard_map/ppermute | solution.py:24
  50.5 1.9 %collective-permute-start.3 = (bf16[2,256,128]{2,1,0:T(8,128)(2,1)}, bf16[2,256,128]{2,1,0:T(8,128)(2,1)S(1)}, u32[]{:S(2)}, u32[]{:S(2)}) collective-permute-start(bf16[2,256,128]{2,1,0:T(8,128)(2,1)} %get-tuple-element.26.first_ref), channel_id=1, source_target_pairs={{0,4},{4,8},{8,12},{12,16},{16,20},{20,24},{24,28},{28,32},{32,36}... | collective-permute-start | bytes 393224 | tf_op jit(solution)/shard_map/ppermute | solution.py:24
  52.4 0.0 collective-permute-done.6.down2_ref
  52.4 6.5 %collective-permute-done.4.up2_ref = bf16[2,256,128]{2,1,0:T(8,128)(2,1)S(1)} collective-permute-done((bf16[2,256,128]{2,1,0:T(8,128)(2,1)}, bf16[2,256,128]{2,1,0:T(8,128)(2,1)S(1)}, u32[]{:S(2)}, u32[]{:S(2)}) %collective-permute-start.4) | collective-permute-done | bytes 131104 | tf_op jit(solution)/shard_map/ppermute | solution.py:24
  58.9 2.3 %collective-permute-done.3.up1_ref = bf16[2,256,128]{2,1,0:T(8,128)(2,1)S(1)} collective-permute-done((bf16[2,256,128]{2,1,0:T(8,128)(2,1)}, bf16[2,256,128]{2,1,0:T(8,128)(2,1)S(1)}, u32[]{:S(2)}, u32[]{:S(2)}) %collective-permute-start.3) | collective-permute-done | bytes 131104 | tf_op jit(solution)/shard_map/ppermute | solution.py:24
  61.2 0.0 collective-permute-done.5.down1_ref
  61.2 1.2 copy-done.1
  62.5 1.2 copy-done.2
  63.7 0.9 copy-done.3
  64.6 0.9 copy-done.4
  65.5 19.0 %attend.1 = (bf16[2,1,256,1024]{3,2,1,0:T(8,128)(2,1)}, bf16[2,1,256,1024]{3,2,1,0:T(8,128)(2,1)}, f32[2,2,256,128]{3,2,1,0:T(8,128)S(1)}, bf16[2,256,128]{2,1,0...) custom-call(s32[1,256]{1,0:T(1,128)S(1)} %bitcast.1, ...), custom_call_target="tpu_custom_call" | custom-call | flops 4831838208 | bytes 4194304 | tf_op jit(solution)/shard_map/attend/pallas_call | solution.py:292
  84.4 0.8 copy-done
  85.2 1.9 %collective-permute-start.9 = (bf16[2,2,256,128]{3,2,1,0:T(8,128)(2,1)S(1)}, bf16[2,2,256,128]{3,2,1,0:T(8,128)(2,1)S(1)}, u32[]{:S(2)}, u32[]{:S(2)}) collective-permute-start(bf16[2,2,256,128]{3,2,1,0:T(8,128)(2,1)S(1)} %get-tuple-element.34), channel_id=1, source_target_pairs={{0,4},{4,8},{8,12},{12,16},{16,20},{20,24},{24,28},{28,32},{32,36}... | collective-permute-start | bytes 786440 | tf_op jit(solution)/shard_map/ppermute | solution.py:24
  87.2 7.9 %collective-permute-start.7 = (bf16[2,256,128]{2,1,0:T(8,128)(2,1)S(1)}, bf16[2,256,128]{2,1,0:T(8,128)(2,1)S(1)}, u32[]{:S(2)}, u32[]{:S(2)}) collective-permute-start(bf16[2,256,128]{2,1,0:T(8,128)(2,1)S(1)} %get-tuple-element.32), channel_id=1, source_target_pairs={{4,0},{8,4},{12,8},{16,12},{20,16},{24,20},{28,24},{32,28},{36,32}... | collective-permute-start | bytes 393224 | tf_op jit(solution)/shard_map/ppermute | solution.py:24
  95.0 1.9 %collective-permute-start.8 = (bf16[2,256,128]{2,1,0:T(8,128)(2,1)S(1)}, bf16[2,256,128]{2,1,0:T(8,128)(2,1)S(1)}, u32[]{:S(2)}, u32[]{:S(2)}) collective-permute-start(bf16[2,256,128]{2,1,0:T(8,128)(2,1)S(1)} %get-tuple-element.33), channel_id=1, source_target_pairs={{8,0},{12,4},{16,8},{20,12},{24,16},{28,20},{32,24},{36,28},{40,32... | collective-permute-start | bytes 393224 | tf_op jit(solution)/shard_map/ppermute | solution.py:24
  97.0 3.9 %collective-permute-start.10 = (bf16[2,256,128]{2,1,0:T(8,128)(2,1)S(1)}, bf16[2,256,128]{2,1,0:T(8,128)(2,1)S(1)}, u32[]{:S(2)}, u32[]{:S(2)}) collective-permute-start(bf16[2,256,128]{2,1,0:T(8,128)(2,1)S(1)} %get-tuple-element.35), channel_id=1, source_target_pairs={{0,8},{4,12},{8,16},{12,20},{16,24},{20,28},{24,32},{28,36},{32,40... | collective-permute-start | bytes 393224 | tf_op jit(solution)/shard_map/ppermute | solution.py:24
  100.9 0.0 collective-permute-done.7.up1_ref
  100.9 0.0 copy-start.7
  100.9 1.0 collective-permute-done.8.up2_ref
  101.9 6.7 %collective-permute-done.10.down2_ref = bf16[2,256,128]{2,1,0:T(8,128)(2,1)S(1)} collective-permute-done((bf16[2,256,128]{2,1,0:T(8,128)(2,1)S(1)}, bf16[2,256,128]{2,1,0:T(8,128)(2,1)S(1)}, u32[]{:S(2)}, u32[]{:S(2)}) %collective-permute-start.10) | collective-permute-done | bytes 131104 | tf_op jit(solution)/shard_map/ppermute | solution.py:24
  108.6 0.0 collective-permute-done.9.down1_ref
  108.6 0.0 copy-done.8
  108.6 0.6 copy-done.9
  109.2 0.1 copy-done.6
  109.4 2.0 %total.1 = (bf16[2,2,64,128]{3,2,1,0:T(8,128)(2,1)}, bf16[2,2,64,128]{3,2,1,0:T(8,128)(2,1)}, bf16[2,2,64,128]{3,2,1,0:T(8,128)(2,1)}, bf16[2,2,64,128]{3,2,1,0:T(8,128)(2,1)}) custom-call(f32[2,2,256,128]{3,2,1,0:T(8,128)} %copy-done, bf16[2,256,128]{2,1,0:T(8,128)(2,1)} %copy-done.7, bf16[2,256,128]{2,1,0:T(8,128)(2,1)} %copy-done.8, ...), custom_call_target="tpu_custom_call" | custom-call | tf_op jit(solution)/shard_map/total/pallas_call | solution.py:325
  111.3 5.6 %collective-permute-start.11 = (bf16[2,2,64,128]{3,2,1,0:T(8,128)(2,1)}, bf16[2,2,64,128]{3,2,1,0:T(8,128)(2,1)S(1)}, u32[]{:S(2)}, u32[]{:S(2)}) collective-permute-start(bf16[2,2,64,128]{3,2,1,0:T(8,128)(2,1)} %get-tuple-element.37), channel_id=1, source_target_pairs={{0,1},{1,2},{2,3},{3,0},{4,5},{5,6},{6,7},{7,4},{8,9},{9,10},{10,1... | collective-permute-start | bytes 196616 | tf_op jit(solution)/shard_map/ppermute | solution.py:29
  116.9 7.9 %collective-permute-start.12 = (bf16[2,2,64,128]{3,2,1,0:T(8,128)(2,1)}, bf16[2,2,64,128]{3,2,1,0:T(8,128)(2,1)S(1)}, u32[]{:S(2)}, u32[]{:S(2)}) collective-permute-start(bf16[2,2,64,128]{3,2,1,0:T(8,128)(2,1)} %get-tuple-element.38), channel_id=1, source_target_pairs={{0,2},{1,3},{2,0},{3,1},{4,6},{5,7},{6,4},{7,5},{8,10},{9,11},{10,... | collective-permute-start | bytes 196616 | tf_op jit(solution)/shard_map/ppermute | solution.py:29
  124.9 5.7 %collective-permute-start.13 = (bf16[2,2,64,128]{3,2,1,0:T(8,128)(2,1)}, bf16[2,2,64,128]{3,2,1,0:T(8,128)(2,1)S(1)}, u32[]{:S(2)}, u32[]{:S(2)}) collective-permute-start(bf16[2,2,64,128]{3,2,1,0:T(8,128)(2,1)} %get-tuple-element.39), channel_id=1, source_target_pairs={{0,3},{1,0},{2,1},{3,2},{4,7},{5,4},{6,5},{7,6},{8,11},{9,8},{10,9... | collective-permute-start | bytes 196616 | tf_op jit(solution)/shard_map/ppermute | solution.py:29
  130.6 0.0 collective-permute-done.11.refs_1_
  130.6 6.0 %collective-permute-done.12.refs_2_ = bf16[2,2,64,128]{3,2,1,0:T(8,128)(2,1)S(1)} collective-permute-done((bf16[2,2,64,128]{3,2,1,0:T(8,128)(2,1)}, bf16[2,2,64,128]{3,2,1,0:T(8,128)(2,1)S(1)}, u32[]{:S(2)}, u32[]{:S(2)}) %collective-permute-start.12) | collective-permute-done | bytes 65568 | tf_op jit(solution)/shard_map/ppermute | solution.py:29
  136.7 0.4 collective-permute-done.13.refs_3_
  137.1 0.2 copy-done.14
  137.3 0.4 copy-done.15
  137.7 1.7 %place.1 = (bf16[2,1,64,512]{3,2,1,0:T(8,128)(2,1)}, bf16[2,1,64,512]{3,2,1,0:T(8,128)(2,1)}) custom-call(bf16[2,2,64,128]{3,2,1,0:T(8,128)(2,1)} %get-tuple-element.36.refs_0_, bf16[2,2,64,128]{3,2,1,0:T(8,128)(2,1)} %copy-done.13, bf16[2,2,64,128]{3,2,1,0:T(8,128)(2,1)} %copy-done.14, bf16[2,2,64,128]{3,2,1,0:T(8,128)(2,1)} %copy-done.15), custom_call_target="tpu_custom_call" | custom-call | tf_op jit(solution)/shard_map/place/pallas_call | solution.py:333
  (17 shorter events, 0.0 us)
Async XLA Ops:
  2.3 24.6 %collective-permute-start = (bf16[2,2,64,128]{3,2,1,0:T(8,128)(2,1)}, bf16[2,2,64,128]{3,2,1,0:T(8,128)(2,1)S(1)}, u32[]{:S(2)}, u32[]{:S(2)}) collective-permute-start(bf16[2,2,64,128]{3,2,1,0:T(8,128)(2,1)} %get-tuple-element.23), channel_id=1, source_target_pairs={{0,1},{1,2},{2,3},{3,0},{4,5},{5,6},{6,7},{7,4},{8,9},{9,10},{10,1... | collective-permute-start | bytes 196616 | tf_op jit(solution)/shard_map/ppermute | solution.py:29
  11.4 15.5 %collective-permute-start.1 = (bf16[2,2,64,128]{3,2,1,0:T(8,128)(2,1)}, bf16[2,2,64,128]{3,2,1,0:T(8,128)(2,1)S(1)}, u32[]{:S(2)}, u32[]{:S(2)}) collective-permute-start(bf16[2,2,64,128]{3,2,1,0:T(8,128)(2,1)} %get-tuple-element.24), channel_id=1, source_target_pairs={{0,2},{1,3},{2,0},{3,1},{4,6},{5,7},{6,4},{7,5},{8,10},{9,11},{10,... | collective-permute-start | bytes 196616 | tf_op jit(solution)/shard_map/ppermute | solution.py:29
  21.4 11.0 %collective-permute-start.2 = (bf16[2,2,64,128]{3,2,1,0:T(8,128)(2,1)}, bf16[2,2,64,128]{3,2,1,0:T(8,128)(2,1)S(1)}, u32[]{:S(2)}, u32[]{:S(2)}) collective-permute-start(bf16[2,2,64,128]{3,2,1,0:T(8,128)(2,1)} %get-tuple-element.25), channel_id=1, source_target_pairs={{0,3},{1,0},{2,1},{3,2},{4,7},{5,4},{6,5},{7,6},{8,11},{9,8},{10,9... | collective-permute-start | bytes 196616 | tf_op jit(solution)/shard_map/ppermute | solution.py:29
  26.9 5.6 %copy-start.10 = (bf16[2,2,64,128]{3,2,1,0:T(8,128)(2,1)}, bf16[2,2,64,128]{3,2,1,0:T(8,128)(2,1)S(1)}, u32[]{:S(2)}) copy-start(bf16[2,2,64,128]{3,2,1,0:T(8,128)(2,1)S(1)} %collective-permute-done.refs_0_) | copy-start | bytes 196612
  26.9 5.6 %copy-start.11 = (bf16[2,2,64,128]{3,2,1,0:T(8,128)(2,1)}, bf16[2,2,64,128]{3,2,1,0:T(8,128)(2,1)S(1)}, u32[]{:S(2)}) copy-start(bf16[2,2,64,128]{3,2,1,0:T(8,128)(2,1)S(1)} %collective-permute-done.1.refs_1_) | copy-start | bytes 196612
  32.5 0.6 copy-start.12
  35.0 26.2 %collective-permute-start.5 = (bf16[2,2,256,128]{3,2,1,0:T(8,128)(2,1)}, bf16[2,2,256,128]{3,2,1,0:T(8,128)(2,1)S(1)}, u32[]{:S(2)}, u32[]{:S(2)}) collective-permute-start(bf16[2,2,256,128]{3,2,1,0:T(8,128)(2,1)} %get-tuple-element.28), channel_id=1, source_target_pairs={{4,0},{8,4},{12,8},{16,12},{20,16},{24,20},{28,24},{32,28},{36,32}... | collective-permute-start | bytes 786440 | tf_op jit(solution)/shard_map/ppermute | solution.py:24
  44.6 7.8 %collective-permute-start.6 = (bf16[2,256,128]{2,1,0:T(8,128)(2,1)}, bf16[2,256,128]{2,1,0:T(8,128)(2,1)S(1)}, u32[]{:S(2)}, u32[]{:S(2)}) collective-permute-start(bf16[2,256,128]{2,1,0:T(8,128)(2,1)} %get-tuple-element.27.second_ref), channel_id=1, source_target_pairs={{8,0},{12,4},{16,8},{20,12},{24,16},{28,20},{32,24},{36,28},{40,32... | collective-permute-start | bytes 393224 | tf_op jit(solution)/shard_map/ppermute | solution.py:24
  47.4 13.8 %copy-start.5 = (s32[256]{0:T(256)S(1)}, s32[256]{0:T(256)}, u32[]{:S(2)}) copy-start(s32[256]{0:T(256)} %param.9) | copy-start | bytes 3076
  47.4 11.5 %collective-permute-start.4 = (bf16[2,256,128]{2,1,0:T(8,128)(2,1)}, bf16[2,256,128]{2,1,0:T(8,128)(2,1)S(1)}, u32[]{:S(2)}, u32[]{:S(2)}) collective-permute-start(bf16[2,256,128]{2,1,0:T(8,128)(2,1)} %get-tuple-element.26.first_ref), channel_id=1, source_target_pairs={{0,8},{4,12},{8,16},{12,20},{16,24},{20,28},{24,32},{28,36},{32,40... | collective-permute-start | bytes 393224 | tf_op jit(solution)/shard_map/ppermute | solution.py:24
  50.5 10.7 %collective-permute-start.3 = (bf16[2,256,128]{2,1,0:T(8,128)(2,1)}, bf16[2,256,128]{2,1,0:T(8,128)(2,1)S(1)}, u32[]{:S(2)}, u32[]{:S(2)}) collective-permute-start(bf16[2,256,128]{2,1,0:T(8,128)(2,1)} %get-tuple-element.26.first_ref), channel_id=1, source_target_pairs={{0,4},{4,8},{8,12},{12,16},{16,20},{20,24},{24,28},{28,32},{32,36}... | collective-permute-start | bytes 393224 | tf_op jit(solution)/shard_map/ppermute | solution.py:24
  61.2 1.2 copy-start.1
  62.5 1.2 copy-start.2
  63.7 0.9 copy-start.3
  64.6 0.9 copy-start.4
  84.4 0.8 copy-start
  85.2 23.3 %collective-permute-start.9 = (bf16[2,2,256,128]{3,2,1,0:T(8,128)(2,1)S(1)}, bf16[2,2,256,128]{3,2,1,0:T(8,128)(2,1)S(1)}, u32[]{:S(2)}, u32[]{:S(2)}) collective-permute-start(bf16[2,2,256,128]{3,2,1,0:T(8,128)(2,1)S(1)} %get-tuple-element.34), channel_id=1, source_target_pairs={{0,4},{4,8},{8,12},{12,16},{16,20},{20,24},{24,28},{28,32},{32,36}... | collective-permute-start | bytes 786440 | tf_op jit(solution)/shard_map/ppermute | solution.py:24
  87.2 13.7 %collective-permute-start.7 = (bf16[2,256,128]{2,1,0:T(8,128)(2,1)S(1)}, bf16[2,256,128]{2,1,0:T(8,128)(2,1)S(1)}, u32[]{:S(2)}, u32[]{:S(2)}) collective-permute-start(bf16[2,256,128]{2,1,0:T(8,128)(2,1)S(1)} %get-tuple-element.32), channel_id=1, source_target_pairs={{4,0},{8,4},{12,8},{16,12},{20,16},{24,20},{28,24},{32,28},{36,32}... | collective-permute-start | bytes 393224 | tf_op jit(solution)/shard_map/ppermute | solution.py:24
  95.0 6.9 %collective-permute-start.8 = (bf16[2,256,128]{2,1,0:T(8,128)(2,1)S(1)}, bf16[2,256,128]{2,1,0:T(8,128)(2,1)S(1)}, u32[]{:S(2)}, u32[]{:S(2)}) collective-permute-start(bf16[2,256,128]{2,1,0:T(8,128)(2,1)S(1)} %get-tuple-element.33), channel_id=1, source_target_pairs={{8,0},{12,4},{16,8},{20,12},{24,16},{28,20},{32,24},{36,28},{40,32... | collective-permute-start | bytes 393224 | tf_op jit(solution)/shard_map/ppermute | solution.py:24
  97.0 11.6 %collective-permute-start.10 = (bf16[2,256,128]{2,1,0:T(8,128)(2,1)S(1)}, bf16[2,256,128]{2,1,0:T(8,128)(2,1)S(1)}, u32[]{:S(2)}, u32[]{:S(2)}) collective-permute-start(bf16[2,256,128]{2,1,0:T(8,128)(2,1)S(1)} %get-tuple-element.35), channel_id=1, source_target_pairs={{0,8},{4,12},{8,16},{12,20},{16,24},{20,28},{24,32},{28,36},{32,40... | collective-permute-start | bytes 393224 | tf_op jit(solution)/shard_map/ppermute | solution.py:24
  100.9 7.7 %copy-start.7 = (bf16[2,256,128]{2,1,0:T(8,128)(2,1)}, bf16[2,256,128]{2,1,0:T(8,128)(2,1)S(1)}, u32[]{:S(2)}) copy-start(bf16[2,256,128]{2,1,0:T(8,128)(2,1)S(1)} %collective-permute-done.7.up1_ref) | copy-start | bytes 393220
  101.9 6.7 %copy-start.8 = (bf16[2,256,128]{2,1,0:T(8,128)(2,1)}, bf16[2,256,128]{2,1,0:T(8,128)(2,1)S(1)}, u32[]{:S(2)}) copy-start(bf16[2,256,128]{2,1,0:T(8,128)(2,1)S(1)} %collective-permute-done.8.up2_ref) | copy-start | bytes 393220
  108.6 0.7 copy-start.9
  108.6 0.8 copy-start.6
  111.3 19.3 %collective-permute-start.11 = (bf16[2,2,64,128]{3,2,1,0:T(8,128)(2,1)}, bf16[2,2,64,128]{3,2,1,0:T(8,128)(2,1)S(1)}, u32[]{:S(2)}, u32[]{:S(2)}) collective-permute-start(bf16[2,2,64,128]{3,2,1,0:T(8,128)(2,1)} %get-tuple-element.37), channel_id=1, source_target_pairs={{0,1},{1,2},{2,3},{3,0},{4,5},{5,6},{6,7},{7,4},{8,9},{9,10},{10,1... | collective-permute-start | bytes 196616 | tf_op jit(solution)/shard_map/ppermute | solution.py:29
  116.9 19.7 %collective-permute-start.12 = (bf16[2,2,64,128]{3,2,1,0:T(8,128)(2,1)}, bf16[2,2,64,128]{3,2,1,0:T(8,128)(2,1)S(1)}, u32[]{:S(2)}, u32[]{:S(2)}) collective-permute-start(bf16[2,2,64,128]{3,2,1,0:T(8,128)(2,1)} %get-tuple-element.38), channel_id=1, source_target_pairs={{0,2},{1,3},{2,0},{3,1},{4,6},{5,7},{6,4},{7,5},{8,10},{9,11},{10,... | collective-permute-start | bytes 196616 | tf_op jit(solution)/shard_map/ppermute | solution.py:29
  124.9 12.2 %collective-permute-start.13 = (bf16[2,2,64,128]{3,2,1,0:T(8,128)(2,1)}, bf16[2,2,64,128]{3,2,1,0:T(8,128)(2,1)S(1)}, u32[]{:S(2)}, u32[]{:S(2)}) collective-permute-start(bf16[2,2,64,128]{3,2,1,0:T(8,128)(2,1)} %get-tuple-element.39), channel_id=1, source_target_pairs={{0,3},{1,0},{2,1},{3,2},{4,7},{5,4},{6,5},{7,6},{8,11},{9,8},{10,9... | collective-permute-start | bytes 196616 | tf_op jit(solution)/shard_map/ppermute | solution.py:29
  130.6 6.4 %copy-start.13 = (bf16[2,2,64,128]{3,2,1,0:T(8,128)(2,1)}, bf16[2,2,64,128]{3,2,1,0:T(8,128)(2,1)S(1)}, u32[]{:S(2)}) copy-start(bf16[2,2,64,128]{3,2,1,0:T(8,128)(2,1)S(1)} %collective-permute-done.11.refs_1_) | copy-start | bytes 196612
  136.7 0.6 copy-start.14
  137.1 0.6 copy-start.15

commit v2 on v1

v2 whole, which is shorter than its diff:
```python
import functools
import math

import jax
import jax.numpy as jnp
from jax import lax
from jax.experimental import pallas as pl
from jax.experimental.pallas import tpu as pltpu
from jax.sharding import PartitionSpec as P

HD = 128
HEADS_STEP = 4
FACTOR = 1.0 / math.sqrt(HD)
LOG2E = math.log2(math.e)
OUT = -1e30
VMEM = pl.BlockSpec(memory_space=pltpu.VMEM)
HBM = pl.BlockSpec(memory_space=pltpu.HBM)
ANY = pl.BlockSpec(memory_space=pl.ANY)
SMALL = pltpu.CompilerParams(vmem_limit_bytes=4 * 2**20)


def device_at(place, contexts):
    return 2 * place if 2 * place < contexts else 2 * (contexts - 1 - place) + 1


def along_line(block, step):
    contexts = lax.axis_size("cp")
    places = range(contexts)
    route = [
        (device_at(i, contexts), device_at(i + step, contexts)) for i in places if i + step in places
    ]
    return lax.ppermute(block, "cp", route)


def to_partner(block):
    return lax.ppermute(block, "cp", [(i, i ^ 1) for i in range(lax.axis_size("cp"))])


def offset(step, core, groups):
    return jnp.where(core == 0, step, groups - step)


def around(block, step):
    contexts, groups = lax.axis_size("cp"), lax.axis_size("tp")
    route = []
    for i in range(contexts):
        turn = step if i % 2 == 0 else groups - step
        route += [(i * groups + t, i * groups + (t + turn) % groups) for t in range(groups)]
    return lax.ppermute(block, ("cp", "tp"), route)


def dot(a, b, contract):
    return lax.dot_general(a, b, (contract, ((), ())), preferred_element_type=jnp.float32)


def aligned(index, size):
    return pl.ds(pl.multiple_of(index * size, size), size)


def split_kernel(groups, k_ref, v_ref, k_pair_ref, v_pair_ref, *pieces):
    tp, core = lax.axis_index("tp"), lax.rem(lax.axis_index("cp"), 2)
    for step, piece in enumerate(pieces, 1):
        lanes = aligned(lax.rem(tp + offset(step, core, groups), groups), HD)
        for block, refs in enumerate(((k_ref, v_ref), (k_pair_ref, v_pair_ref))):
            for kind, ref in enumerate(refs):
                piece[block, kind] = ref[core, 0, :, lanes]


def join_kernel(groups, k_ref, v_ref, k_pair_ref, v_pair_ref, *refs):
    pieces, out_ref = refs[:-1], refs[-1]
    tp, core = lax.axis_index("tp"), lax.rem(lax.axis_index("cp"), 2)
    rows = k_ref.shape[2]
    for block, pair in enumerate(((k_ref, v_ref), (k_pair_ref, v_pair_ref))):
        for kind, ref in enumerate(pair):
            out_ref[kind, aligned(block * groups + tp, rows), :] = ref[core, 0, :, aligned(tp, HD)]
    for step, piece in enumerate(pieces, 1):
        source = lax.rem(tp - offset(step, core, groups) + groups, groups)
        for block in range(2):
            out_ref[:, aligned(block * groups + source, rows), :] = piece[block]


def total_kernel(groups, own_ref, came_ref, *pieces):
    tp, core = lax.axis_index("tp"), lax.rem(lax.axis_index("cp"), 2)
    rows = pieces[0].shape[2]
    for step, piece in enumerate(pieces):
        target = lax.rem(tp + offset(step, core, groups), groups)
        for block in range(2):
            place = aligned(block * groups + target, rows)
            total = own_ref[:, place, :] + came_ref[:, place, :].astype(jnp.float32)
            piece[block] = total.astype(piece.dtype)


def place_kernel(groups, *refs):
    pieces, outs = refs[:-3], refs[-2:]
    tp, core = lax.axis_index("tp"), lax.rem(lax.axis_index("cp"), 2)
    for step, piece in enumerate(pieces):
        lanes = aligned(lax.rem(tp - offset(step, core, groups) + groups, groups), HD)
        for block, out in enumerate(outs):
            out[:, :, lanes] = piece[block]


def finish_kernel(kept_ref, came_ref, k_ref, v_ref):
    core = lax.rem(lax.axis_index("cp"), 2)
    for kind, ref in enumerate((k_ref, v_ref)):
        ref[core, 0] = kept_ref[kind]
        ref[1 - core, 0] = came_ref[kind]


def pick_kernel(q_ref, g_ref, after_ref, own_ref, pair_ref, sems):
    core = lax.rem(lax.axis_index("cp"), 2)
    copies = []
    for kind, ref in enumerate((q_ref, g_ref)):
        copies.append(pltpu.make_async_copy(ref.at[1 - core, 0], pair_ref.at[kind], sems.at[kind]))
        copies.append(pltpu.make_async_copy(ref.at[core, 0], own_ref.at[kind], sems.at[2 + kind]))
    for copy in copies:
        copy.start()
    for copy in copies:
        copy.wait()


def fill_kernel(attn_in, dq_in, came_ref, after_ref, attn_ref, dq_ref, done_ref, sems):
    core = lax.rem(lax.axis_index("cp"), 2)
    copies = [
        pltpu.make_async_copy(came_ref.at[kind], ref.at[1 - core, 0], sems.at[kind])
        for kind, ref in enumerate((attn_ref, dq_ref))
    ]
    for copy in copies:
        copy.start()
    done_ref[...] = jnp.zeros_like(done_ref)
    for copy in copies:
        copy.wait()


def blend(field, side):
    low = side // 2
    row = lax.broadcasted_iota(jnp.int32, (low, low), 0)
    column = lax.broadcasted_iota(jnp.int32, (low, low), 1)
    causal = column <= row
    old, own = field[:, :side], field[:, 2 * side :]
    top = jnp.concatenate(
        [jnp.where(causal, own[:low, :low], old[:low, :low]), old[:low, low:]], axis=1
    )
    bottom = jnp.concatenate(
        [own[low:, :low], jnp.where(causal, own[low:, low:], old[low:, low:])], axis=1
    )
    shared = jnp.concatenate([top, bottom], axis=0)
    return jnp.concatenate([shared, field[:, side : 2 * side]], axis=1)


def unblend(field, side):
    low = side // 2
    row = lax.broadcasted_iota(jnp.int32, (low, low), 0)
    column = lax.broadcasted_iota(jnp.int32, (low, low), 1)
    causal = column <= row
    bf = jnp.bfloat16
    none = jnp.zeros((low, low), bf)
    a, d = field[:low, :low], field[low:, low : 2 * low]
    b, c = field[:low, low : 2 * low].astype(bf), field[low:, :low].astype(bf)
    a_own, a_old = jnp.where(causal, a, 0.0).astype(bf), jnp.where(causal, 0.0, a).astype(bf)
    d_own, d_old = jnp.where(causal, d, 0.0).astype(bf), jnp.where(causal, 0.0, d).astype(bf)
    old = jnp.concatenate(
        [jnp.concatenate([a_old, b], axis=1), jnp.concatenate([none, d_old], axis=1)], axis=0
    )
    own = jnp.concatenate(
        [jnp.concatenate([a_own, none], axis=1), jnp.concatenate([c, d_own], axis=1)], axis=0
    )
    return jnp.concatenate([old, field[:, side:].astype(bf), own], axis=1)


def attend_kernel(
    where_ref,
    len_ref,
    own_qg_ref,
    pair_qg_ref,
    behind_ref,
    here_ref,
    attn_ref,
    dq_ref,
    pair_ref,
    own_ref,
    halo_ref,
    k_ref,
    v_ref,
    kt_ref,
    vt_ref,
    bias_ref,
    dk_ref,
    dv_ref,
):
    side = own_qg_ref.shape[1]
    turn, part = pl.program_id(0), pl.program_id(1)
    bf = jnp.bfloat16

    @pl.when((turn == 0) & (part == 0))
    def _():
        for kind, (ref, turned) in enumerate(((k_ref, kt_ref), (v_ref, vt_ref))):
            ref[: 2 * side, :] = behind_ref[kind]
            ref[2 * side :, :] = here_ref[kind]
            turned[:, : 2 * side] = behind_ref[kind].T
            turned[:, 2 * side :] = here_ref[kind].T
        dk_ref[...] = jnp.zeros_like(dk_ref)
        dv_ref[...] = jnp.zeros_like(dv_ref)

    @pl.when(part == 0)
    def _():
        begin_block = (2 * where_ref[1] + turn) * side
        docs = len_ref.shape[1]
        lengths = jnp.broadcast_to(len_ref[...], (8, docs))
        before = lax.broadcasted_iota(jnp.int32, (docs, docs), 0)
        after = lax.broadcasted_iota(jnp.int32, (docs, docs), 1)
        upto = (before <= after).astype(jnp.float32).astype(bf)
        coarse = (lengths // 16).astype(jnp.float32).astype(bf)
        fine = (lengths % 16).astype(jnp.float32).astype(bf)
        over = ((1,), (0,))
        ends = (16.0 * dot(coarse, upto, over) + dot(fine, upto, over))[0:1, :]
        row = lax.broadcasted_iota(jnp.int32, (side, docs), 0)
        position = (row + begin_block).astype(jnp.float32)
        begins = jnp.max(jnp.where(ends <= position, ends, 0.0), axis=1, keepdims=True)
        begins = begins - begin_block.astype(jnp.float32)
        row = lax.broadcasted_iota(jnp.int32, (side, side), 0)
        column = lax.broadcasted_iota(jnp.int32, (side, side), 1)
        key = column.astype(jnp.float32)
        shared = jnp.where(column <= row, key, key - 2.0 * side)
        bias_ref[:, :side] = jnp.where(shared >= begins, 0.0, OUT)
        bias_ref[:, side:] = jnp.where(key - side >= begins, 0.0, OUT)

    window = pl.ds(pl.multiple_of(turn * side, side), 3 * side)
    over, down = ((1,), (0,)), ((0,), (0,))

    def run(take_q, take_g, give):
        def products(head):
            q, g = take_q(head), take_g(head)
            scores = dot(q, kt_ref[:, window], over)
            return q, g, scores, dot(g, vt_ref[:, window], over)

        def softmax(scores):
            scaled = blend(scores, side) * (FACTOR * LOG2E) + bias_ref[...]
            raised = jnp.exp2(scaled - jnp.max(scaled, axis=1, keepdims=True))
            return raised * (1.0 / jnp.sum(raised, axis=1, keepdims=True))

        def finish(head, q, g, probs_low, ds):
            give(1, head, (dot(ds, k_ref[window, :], over) * FACTOR).astype(bf))
            dv_ref[:, window] += dot(g, probs_low, down)
            dk_ref[:, window] += dot(q, ds, down)

        pending = None
        ahead = products(0)
        for head in range(HEADS_STEP):
            q, g, scores, dprobs = ahead
            if head + 1 < HEADS_STEP:
                ahead = products(head + 1)
            probs = softmax(scores)
            probs_low = unblend(probs, side)
            attn = dot(probs_low, v_ref[window, :], over).astype(bf)
            give(0, head, attn)
            if pending is not None:
                finish(*pending)
            delta = jnp.sum(
                attn.astype(jnp.float32) * g.astype(jnp.float32), axis=1, keepdims=True
            )
            ds = unblend(probs * (blend(dprobs, side) - delta), side)
            pending = (head, q, g, probs_low, ds)
        finish(*pending)

    def lanes(head):
        return slice(head * HD, (head + 1) * HD)

    def taker(ref, kind):
        return lambda head: ref[kind, :, aligned(part * HEADS_STEP + head, HD)]

    @pl.when(turn == 0)
    def _():
        outs = (attn_ref, dq_ref)

        def give(kind, head, value):
            outs[kind][0, 0, :, lanes(head)] = value

        run(taker(own_qg_ref, 0), taker(own_qg_ref, 1), give)

    @pl.when(turn == 1)
    def _():
        def give(kind, head, value):
            pair_ref[kind, :, lanes(head)] = value

        run(taker(pair_qg_ref, 0), taker(pair_qg_ref, 1), give)

    @pl.when((turn == 1) & (part == pl.num_programs(1) - 1))
    def _():
        for kind, (ref, factor) in enumerate(((dk_ref, FACTOR), (dv_ref, 1.0))):
            halo_ref[kind] = (ref[:, : 2 * side].T * factor).astype(bf)
            own_ref[kind] = ref[:, 2 * side :].T * factor


def local(queries, keys, values, out_grad, doc_lengths):
    side, width = queries.shape[2], queries.shape[3]
    contexts, groups = lax.axis_size("cp"), lax.axis_size("tp")
    rows = keys.shape[2]
    bf = jnp.bfloat16
    shape = jax.ShapeDtypeStruct
    piece = shape((2, 2, rows, HD), bf)
    cp = lax.axis_index("cp")
    core = cp % 2
    place = jnp.where(core == 0, cp // 2, contexts - 1 - cp // 2)

    local_kv = (keys, values, to_partner(keys), to_partner(values))
    sent = pl.pallas_call(
        functools.partial(split_kernel, groups),
        out_shape=[piece] * (groups - 1),
        in_specs=[VMEM] * 4,
        out_specs=[VMEM] * (groups - 1),
        compiler_params=SMALL,
        name="split",
    )(*local_kv)
    came = [around(block, step) for step, block in enumerate(sent, 1)]
    both = shape((2, side, width), bf)
    own_qg, for_pair = pl.pallas_call(
        pick_kernel,
        out_shape=[both] * 2,
        in_specs=[HBM, HBM, ANY],
        out_specs=[VMEM] * 2,
        scratch_shapes=[pltpu.SemaphoreType.DMA((4,))],
        compiler_params=SMALL,
        name="pick",
    )(queries, out_grad, came[0])
    pair_qg = to_partner(for_pair)
    here = pl.pallas_call(
        functools.partial(join_kernel, groups),
        out_shape=shape((2, 2 * side, HD), bf),
        in_specs=[VMEM] * (groups + 3),
        out_specs=VMEM,
        compiler_params=SMALL,
        name="join",
    )(*local_kv, *came)
    behind = along_line(here, 1)

    lanes = HEADS_STEP * HD
    parts = width // lanes
    own_turn = pl.BlockSpec(
        (1, 1, side, lanes), lambda j, n, at: (at[0], 0, 0, jnp.where(j == 0, n, parts - 1))
    )
    pair_out = pl.BlockSpec((2, side, lanes), lambda j, n, at: (0, 0, jnp.where(j == 0, 0, n)))
    work = 2 * (width // HD) * side * 3 * side
    attn_out, q_grad, for_pair, own, halo = pl.pallas_call(
        attend_kernel,
        grid_spec=pltpu.PrefetchScalarGridSpec(
            num_scalar_prefetch=1,
            grid=(2, parts),
            in_specs=[VMEM] * 5,
            out_specs=[own_turn, own_turn, pair_out, VMEM, VMEM],
            scratch_shapes=[
                pltpu.VMEM((4 * side, HD), bf),
                pltpu.VMEM((4 * side, HD), bf),
                pltpu.VMEM((HD, 4 * side), bf),
                pltpu.VMEM((HD, 4 * side), bf),
                pltpu.VMEM((side, 2 * side), jnp.float32),
                pltpu.VMEM((HD, 4 * side), jnp.float32),
                pltpu.VMEM((HD, 4 * side), jnp.float32),
            ],
        ),
        out_shape=[
            shape(queries.shape, bf),
            shape(queries.shape, bf),
            both,
            shape((2, 2 * side, HD), jnp.float32),
            shape((2, 2 * side, HD), bf),
        ],
        compiler_params=pltpu.CompilerParams(vmem_limit_bytes=32 * 2**20),
        cost_estimate=pl.CostEstimate(
            flops=12 * work * HD, bytes_accessed=8 * side * width * 2, transcendentals=work
        ),
        name="attend",
    )(
        jnp.stack([core, place]),
        doc_lengths[None, :],
        own_qg,
        pair_qg,
        behind,
        here,
    )

    came_halo = along_line(halo, -1)
    from_pair = to_partner(for_pair)
    pieces = pl.pallas_call(
        functools.partial(total_kernel, groups),
        out_shape=[piece] * groups,
        in_specs=[VMEM] * 2,
        out_specs=[VMEM] * groups,
        compiler_params=SMALL,
        name="total",
    )(own, came_halo)
    returned = [pieces[0]] + [around(block, step) for step, block in enumerate(pieces[1:], 1)]
    attn_out, q_grad, filled = pl.pallas_call(
        fill_kernel,
        out_shape=[shape(queries.shape, bf)] * 2 + [shape((8, HD), jnp.float32)],
        in_specs=[HBM, HBM, ANY, ANY],
        out_specs=[HBM, HBM, VMEM],
        scratch_shapes=[pltpu.SemaphoreType.DMA((2,))],
        input_output_aliases={0: 0, 1: 1},
        compiler_params=SMALL,
        name="fill",
    )(attn_out, q_grad, from_pair, returned[1])
    kept, for_pair = pl.pallas_call(
        functools.partial(place_kernel, groups),
        out_shape=[shape((2, rows, keys.shape[3]), bf)] * 2,
        in_specs=[VMEM] * groups + [ANY],
        out_specs=[VMEM] * 2,
        compiler_params=SMALL,
        name="place",
    )(*returned, filled)
    k_grad, v_grad = pl.pallas_call(
        finish_kernel,
        out_shape=[shape(keys.shape, bf)] * 2,
        in_specs=[VMEM] * 2,
        out_specs=[VMEM] * 2,
        compiler_params=SMALL,
        name="finish",
    )(kept, to_partner(for_pair))

    return (attn_out, q_grad, k_grad, v_grad)


def solution(mesh):
    heads, tokens = P(None, "cp", None, "tp"), P(None, "cp", "tp", None)
    return jax.shard_map(
        local,
        mesh=mesh,
        in_specs=(heads, tokens, tokens, heads, P()),
        out_specs=(heads, heads, tokens, tokens),
        check_vma=False,
    )
```

time: 140 us -> 119 us (0.85)
  the two profiles are of different devices: /device:TPU:32 before, /device:TPU:95 now
where the time goes in v2:
time: 119 us; the launch traced here: 118 us
  starting transfers between devices  72.9 us (61%)
  waiting for transfers between devices  23.9 us (20%)
  Pallas kernels  15.7 us (13%)
  local copies, waits for them, and re-layouts  4.94 us (4%)
    ppermute x6, starting transfers between devices, around(): return lax.ppermute(block, ('cp', 'tp'), route)  41.9 us
    ppermute x5, starting transfers between devices, to_partner(): lax.ppermute(block, 'cp', [(i, i ^ 1) for i in range(lax.axis_size('cp'))])  22.6 us
    pallas_call x1, Pallas kernels, local(): pl.pallas_call(attend_kernel, grid_spec=pltpu.PrefetchScalarGridSpec(num_...  13.6 us
    ppermute x2, waiting for transfers between devices, along_line(): return lax.ppermute(block, 'cp', route)  12.2 us
    ppermute x6, waiting for transfers between devices, around(): return lax.ppermute(block, ('cp', 'tp'), route)  9.28 us
    ppermute x2, starting transfers between devices, along_line(): return lax.ppermute(block, 'cp', route)  8.4 us
    unnamed x14, local copies, waits for them, and re-layouts  4.94 us
    ppermute x5, waiting for transfers between devices, to_partner(): lax.ppermute(block, 'cp', [(i, i ^ 1) for i in range(lax.axis_size('cp'))])  2.49 us
  transfers between devices with their start and end apart: 13, of which 8 were waited for; matrix products, arithmetic and copies ran while one was open for 0% of the time, Pallas kernels for 1%

profile of v2, /device:TPU:95, one launch (start us, length us, event | category | flops | bytes accessed | tf_op | source)
XLA Modules:
  0.0 118.4 jit_solution(7048198657536152178)
XLA Ops:
  0.6 2.6 %collective-permute-start = (bf16[2,1,64,512]{3,2,1,0:T(8,128)(2,1)}, bf16[2,1,64,512]{3,2,1,0:T(8,128)(2,1)S(1)}, u32[]{:S(2)}, u32[]{:S(2)}) collective-permute-start(bf16[2,1,64,512]{3,2,1,0:T(8,128)(2,1)} %k_ref.3), channel_id=1, source_target_pairs={{0,4},{4,0},{8,12},{12,8},{16,20},{20,16},{24,28},{28,24},{32,36},... | collective-permute-start | bytes 393224 | tf_op jit(solution)/shard_map/ppermute | solution.py:36
  3.2 1.9 %collective-permute-start.1 = (bf16[2,1,64,512]{3,2,1,0:T(8,128)(2,1)}, bf16[2,1,64,512]{3,2,1,0:T(8,128)(2,1)S(1)}, u32[]{:S(2)}, u32[]{:S(2)}) collective-permute-start(bf16[2,1,64,512]{3,2,1,0:T(8,128)(2,1)} %v_ref.3), channel_id=1, source_target_pairs={{0,4},{4,0},{8,12},{12,8},{16,20},{20,16},{24,28},{28,24},{32,36},... | collective-permute-start | bytes 393224 | tf_op jit(solution)/shard_map/ppermute | solution.py:36
  5.2 0.0 collective-permute-done.k_pair_ref
  5.2 1.5 %collective-permute-done.1.v_pair_ref = bf16[2,1,64,512]{3,2,1,0:T(8,128)(2,1)S(1)} collective-permute-done((bf16[2,1,64,512]{3,2,1,0:T(8,128)(2,1)}, bf16[2,1,64,512]{3,2,1,0:T(8,128)(2,1)S(1)}, u32[]{:S(2)}, u32[]{:S(2)}) %collective-permute-start.1) | collective-permute-done | bytes 131104 | tf_op jit(solution)/shard_map/ppermute | solution.py:36
  6.7 0.0 copy-start.2
  6.7 0.9 copy-done.2
  7.6 0.0 copy-start.4
  7.6 0.9 copy-done.4
  8.5 10.7 %collective-permute-start.2 = (bf16[2,2,64,128]{3,2,1,0:T(8,128)(2,1)S(1)}, bf16[2,2,64,128]{3,2,1,0:T(8,128)(2,1)S(1)}, u32[]{:S(2)}, u32[]{:S(2)}) collective-permute-start(bf16[2,2,64,128]{3,2,1,0:T(8,128)(2,1)S(1)} %get-tuple-element.25), channel_id=1, source_target_pairs={{0,1},{1,2},{2,3},{3,0},{4,7},{5,4},{6,5},{7,6},{8,9},{9,10},{10,1... | collective-permute-start | bytes 196616 | tf_op jit(solution)/shard_map/ppermute | solution.py:49
  19.2 1.3 %collective-permute-done.2.after_ref.refs_0_ = bf16[2,2,64,128]{3,2,1,0:T(8,128)(2,1)S(1)} collective-permute-done((bf16[2,2,64,128]{3,2,1,0:T(8,128)(2,1)S(1)}, bf16[2,2,64,128]{3,2,1,0:T(8,128)(2,1)S(1)}, u32[]{:S(2)}, u32[]{:S(2)}) %collective-permute-start.2) | collective-permute-done | bytes 65568 | tf_op jit(solution)/shard_map/ppermute | solution.py:49
  20.5 0.0 copy-start
  20.5 1.2 %copy-done = bf16[2,1,256,1024]{3,2,1,0:T(8,128)(2,1)S(1)} copy-done((bf16[2,1,256,1024]{3,2,1,0:T(8,128)(2,1)S(1)}, bf16[2,1,256,1024]{3,2,1,0:T(8,128)(2,1)}, u32[]{:S(2)}) %copy-start) | copy-done | bytes 1048600
  21.7 0.0 copy-start.1
  21.7 1.2 %copy-done.1 = bf16[2,1,256,1024]{3,2,1,0:T(8,128)(2,1)S(1)} copy-done((bf16[2,1,256,1024]{3,2,1,0:T(8,128)(2,1)S(1)}, bf16[2,1,256,1024]{3,2,1,0:T(8,128)(2,1)}, u32[]{:S(2)}) %copy-start.1) | copy-done | bytes 1048600
  23.0 0.0 copy-start.3
  23.0 0.0 copy-start.5
  23.0 0.2 pick.1
  23.2 4.8 %collective-permute-start.3 = (bf16[2,256,1024]{2,1,0:T(8,128)(2,1)S(1)}, bf16[2,256,1024]{2,1,0:T(8,128)(2,1)S(1)}, u32[]{:S(2)}, u32[]{:S(2)}) collective-permute-start(bf16[2,256,1024]{2,1,0:T(8,128)(2,1)S(1)} %get-tuple-element.27), channel_id=1, source_target_pairs={{0,4},{4,0},{8,12},{12,8},{16,20},{20,16},{24,28},{28,24},{32,36},... | collective-permute-start | bytes 3145736 | tf_op jit(solution)/shard_map/ppermute | solution.py:36
  27.9 9.5 %collective-permute-start.4 = (bf16[2,2,64,128]{3,2,1,0:T(8,128)(2,1)S(1)}, bf16[2,2,64,128]{3,2,1,0:T(8,128)(2,1)S(1)}, u32[]{:S(2)}, u32[]{:S(2)}) collective-permute-start(bf16[2,2,64,128]{3,2,1,0:T(8,128)(2,1)S(1)} %get-tuple-element.28), channel_id=1, source_target_pairs={{0,2},{1,3},{2,0},{3,1},{4,6},{5,7},{6,4},{7,5},{8,10},{9,11},{10,... | collective-permute-start | bytes 196616 | tf_op jit(solution)/shard_map/ppermute | solution.py:49
  37.4 5.0 %collective-permute-start.5 = (bf16[2,2,64,128]{3,2,1,0:T(8,128)(2,1)S(1)}, bf16[2,2,64,128]{3,2,1,0:T(8,128)(2,1)S(1)}, u32[]{:S(2)}, u32[]{:S(2)}) collective-permute-start(bf16[2,2,64,128]{3,2,1,0:T(8,128)(2,1)S(1)} %get-tuple-element.29), channel_id=1, source_target_pairs={{0,3},{1,0},{2,1},{3,2},{4,5},{5,6},{6,7},{7,4},{8,11},{9,8},{10,9... | collective-permute-start | bytes 196616 | tf_op jit(solution)/shard_map/ppermute | solution.py:49
  42.5 1.2 %collective-permute-done.4.refs_1_ = bf16[2,2,64,128]{3,2,1,0:T(8,128)(2,1)S(1)} collective-permute-done((bf16[2,2,64,128]{3,2,1,0:T(8,128)(2,1)S(1)}, bf16[2,2,64,128]{3,2,1,0:T(8,128)(2,1)S(1)}, u32[]{:S(2)}, u32[]{:S(2)}) %collective-permute-start.4) | collective-permute-done | bytes 65568 | tf_op jit(solution)/shard_map/ppermute | solution.py:49
  43.7 2.8 %collective-permute-done.5.refs_2_ = bf16[2,2,64,128]{3,2,1,0:T(8,128)(2,1)S(1)} collective-permute-done((bf16[2,2,64,128]{3,2,1,0:T(8,128)(2,1)S(1)}, bf16[2,2,64,128]{3,2,1,0:T(8,128)(2,1)S(1)}, u32[]{:S(2)}, u32[]{:S(2)}) %collective-permute-start.5) | collective-permute-done | bytes 65568 | tf_op jit(solution)/shard_map/ppermute | solution.py:49
  46.4 0.0 copy-done.3
  46.4 0.0 copy-done.5
  46.5 2.5 %collective-permute-start.6 = (bf16[2,512,128]{2,1,0:T(8,128)(2,1)S(1)}, bf16[2,512,128]{2,1,0:T(8,128)(2,1)}, u32[]{:S(2)}, u32[]{:S(2)}) collective-permute-start(bf16[2,512,128]{2,1,0:T(8,128)(2,1)S(1)} %join.1.here_ref), channel_id=1, source_target_pairs={{0,8},{8,16},{16,24},{24,32},{32,40},{40,48},{48,56},{56,64},{64,7... | collective-permute-start | bytes 786440 | tf_op jit(solution)/shard_map/ppermute | solution.py:32
  49.0 0.1 pad_add_fusion.where_ref
  49.1 8.9 %collective-permute-done.6.behind_ref = bf16[2,512,128]{2,1,0:T(8,128)(2,1)} collective-permute-done((bf16[2,512,128]{2,1,0:T(8,128)(2,1)S(1)}, bf16[2,512,128]{2,1,0:T(8,128)(2,1)}, u32[]{:S(2)}, u32[]{:S(2)}) %collective-permute-start.6) | collective-permute-done | bytes 262176 | tf_op jit(solution)/shard_map/ppermute | solution.py:32
  57.9 0.0 collective-permute-done.3.pair_qg_ref
  57.9 0.0 copy-start.6
  57.9 0.7 copy-done.6
  58.6 13.6 %attend.1 = (bf16[2,1,256,1024]{3,2,1,0:T(8,128)(2,1)}, bf16[2,1,256,1024]{3,2,1,0:T(8,128)(2,1)}, bf16[2,256,1024]{2,1,0:T(8,128)(2,1)S(1)}, f32[2,512,128]{2,1,0:T(8,128)S(1)}, bf16[2,512,128]{2,1,0:T(8,128)(2,1)S(1)}) custom-call(s32[2]{0:T(128)S(1)} %pad_add_fusion.where_ref, s32[1,256]{1,0:T(1,128)S(1)} %bitcast.3, ...), custom_call_target="tpu_custom_call" | custom-call | flops 4831838208 | bytes 4194304 | tf_op jit(solution)/shard_map/attend/pallas_call | solution.py:343
  72.3 2.5 %collective-permute-start.7 = (bf16[2,256,1024]{2,1,0:T(8,128)(2,1)S(1)}, bf16[2,256,1024]{2,1,0:T(8,128)(2,1)S(1)}, u32[]{:S(2)}, u32[]{:S(2)}) collective-permute-start(bf16[2,256,1024]{2,1,0:T(8,128)(2,1)S(1)} %get-tuple-element.32), channel_id=1, source_target_pairs={{0,4},{4,0},{8,12},{12,8},{16,20},{20,16},{24,28},{28,24},{32,36},... | collective-permute-start | bytes 3145736 | tf_op jit(solution)/shard_map/ppermute | solution.py:36
  74.7 5.9 %collective-permute-start.8 = (bf16[2,512,128]{2,1,0:T(8,128)(2,1)S(1)}, bf16[2,512,128]{2,1,0:T(8,128)(2,1)S(1)}, u32[]{:S(2)}, u32[]{:S(2)}) collective-permute-start(bf16[2,512,128]{2,1,0:T(8,128)(2,1)S(1)} %get-tuple-element.34), channel_id=1, source_target_pairs={{8,0},{16,8},{24,16},{32,24},{40,32},{48,40},{56,48},{64,56},{72,6... | collective-permute-start | bytes 786440 | tf_op jit(solution)/shard_map/ppermute | solution.py:32
  80.7 3.3 %collective-permute-done.8.came_ref = bf16[2,512,128]{2,1,0:T(8,128)(2,1)S(1)} collective-permute-done((bf16[2,512,128]{2,1,0:T(8,128)(2,1)S(1)}, bf16[2,512,128]{2,1,0:T(8,128)(2,1)S(1)}, u32[]{:S(2)}, u32[]{:S(2)}) %collective-permute-start.8) | collective-permute-done | bytes 262176 | tf_op jit(solution)/shard_map/ppermute | solution.py:32
  84.0 0.1 total.1
  84.0 6.5 %collective-permute-start.9 = (bf16[2,2,64,128]{3,2,1,0:T(8,128)(2,1)S(1)}, bf16[2,2,64,128]{3,2,1,0:T(8,128)(2,1)S(1)}, u32[]{:S(2)}, u32[]{:S(2)}) collective-permute-start(bf16[2,2,64,128]{3,2,1,0:T(8,128)(2,1)S(1)} %get-tuple-element.35), channel_id=1, source_target_pairs={{0,1},{1,2},{2,3},{3,0},{4,7},{5,4},{6,5},{7,6},{8,9},{9,10},{10,1... | collective-permute-start | bytes 196616 | tf_op jit(solution)/shard_map/ppermute | solution.py:49
  90.5 5.3 %collective-permute-start.10 = (bf16[2,2,64,128]{3,2,1,0:T(8,128)(2,1)S(1)}, bf16[2,2,64,128]{3,2,1,0:T(8,128)(2,1)S(1)}, u32[]{:S(2)}, u32[]{:S(2)}) collective-permute-start(bf16[2,2,64,128]{3,2,1,0:T(8,128)(2,1)S(1)} %get-tuple-element.39), channel_id=1, source_target_pairs={{0,2},{1,3},{2,0},{3,1},{4,6},{5,7},{6,4},{7,5},{8,10},{9,11},{10,... | collective-permute-start | bytes 196616 | tf_op jit(solution)/shard_map/ppermute | solution.py:49
  95.8 4.9 %collective-permute-start.11 = (bf16[2,2,64,128]{3,2,1,0:T(8,128)(2,1)S(1)}, bf16[2,2,64,128]{3,2,1,0:T(8,128)(2,1)S(1)}, u32[]{:S(2)}, u32[]{:S(2)}) collective-permute-start(bf16[2,2,64,128]{3,2,1,0:T(8,128)(2,1)S(1)} %get-tuple-element.40), channel_id=1, source_target_pairs={{0,3},{1,0},{2,1},{3,2},{4,5},{5,6},{6,7},{7,4},{8,11},{9,8},{10,9... | collective-permute-start | bytes 196616 | tf_op jit(solution)/shard_map/ppermute | solution.py:49
  100.7 0.0 collective-permute-done.9.after_ref.refs_1_
  100.8 0.0 collective-permute-done.7.came_ref
  100.8 1.0 fill.1
  101.8 4.0 %collective-permute-done.10.refs_2_ = bf16[2,2,64,128]{3,2,1,0:T(8,128)(2,1)S(1)} collective-permute-done((bf16[2,2,64,128]{3,2,1,0:T(8,128)(2,1)S(1)}, bf16[2,2,64,128]{3,2,1,0:T(8,128)(2,1)S(1)}, u32[]{:S(2)}, u32[]{:S(2)}) %collective-permute-start.10) | collective-permute-done | bytes 65568 | tf_op jit(solution)/shard_map/ppermute | solution.py:49
  105.8 0.0 collective-permute-done.11.refs_3_
  105.8 0.1 place.1
  105.8 10.9 %collective-permute-start.12 = (bf16[2,64,512]{2,1,0:T(8,128)(2,1)S(1)}, bf16[2,64,512]{2,1,0:T(8,128)(2,1)S(1)}, u32[]{:S(2)}, u32[]{:S(2)}) collective-permute-start(bf16[2,64,512]{2,1,0:T(8,128)(2,1)S(1)} %get-tuple-element.43), channel_id=1, source_target_pairs={{0,4},{4,0},{8,12},{12,8},{16,20},{20,16},{24,28},{28,24},{32,36},... | collective-permute-start | bytes 393224 | tf_op jit(solution)/shard_map/ppermute | solution.py:36
  116.7 1.0 collective-permute-done.12.came_ref
  117.7 0.7 finish.1
  (2 shorter events, 0.1 us)
Async XLA Ops:
  0.6 4.5 %collective-permute-start = (bf16[2,1,64,512]{3,2,1,0:T(8,128)(2,1)}, bf16[2,1,64,512]{3,2,1,0:T(8,128)(2,1)S(1)}, u32[]{:S(2)}, u32[]{:S(2)}) collective-permute-start(bf16[2,1,64,512]{3,2,1,0:T(8,128)(2,1)} %k_ref.3), channel_id=1, source_target_pairs={{0,4},{4,0},{8,12},{12,8},{16,20},{20,16},{24,28},{28,24},{32,36},... | collective-permute-start | bytes 393224 | tf_op jit(solution)/shard_map/ppermute | solution.py:36
  3.2 3.5 %collective-permute-start.1 = (bf16[2,1,64,512]{3,2,1,0:T(8,128)(2,1)}, bf16[2,1,64,512]{3,2,1,0:T(8,128)(2,1)S(1)}, u32[]{:S(2)}, u32[]{:S(2)}) collective-permute-start(bf16[2,1,64,512]{3,2,1,0:T(8,128)(2,1)} %v_ref.3), channel_id=1, source_target_pairs={{0,4},{4,0},{8,12},{12,8},{16,20},{20,16},{24,28},{28,24},{32,36},... | collective-permute-start | bytes 393224 | tf_op jit(solution)/shard_map/ppermute | solution.py:36
  6.7 0.9 copy-start.2
  7.6 0.9 copy-start.4
  8.5 12.0 %collective-permute-start.2 = (bf16[2,2,64,128]{3,2,1,0:T(8,128)(2,1)S(1)}, bf16[2,2,64,128]{3,2,1,0:T(8,128)(2,1)S(1)}, u32[]{:S(2)}, u32[]{:S(2)}) collective-permute-start(bf16[2,2,64,128]{3,2,1,0:T(8,128)(2,1)S(1)} %get-tuple-element.25), channel_id=1, source_target_pairs={{0,1},{1,2},{2,3},{3,0},{4,7},{5,4},{6,5},{7,6},{8,9},{9,10},{10,1... | collective-permute-start | bytes 196616 | tf_op jit(solution)/shard_map/ppermute | solution.py:49
  20.5 1.2 %copy-start = (bf16[2,1,256,1024]{3,2,1,0:T(8,128)(2,1)S(1)}, bf16[2,1,256,1024]{3,2,1,0:T(8,128)(2,1)}, u32[]{:S(2)}) copy-start(bf16[2,1,256,1024]{3,2,1,0:T(8,128)(2,1)} %q_ref.1) | copy-start | bytes 3145732
  21.7 1.2 %copy-start.1 = (bf16[2,1,256,1024]{3,2,1,0:T(8,128)(2,1)S(1)}, bf16[2,1,256,1024]{3,2,1,0:T(8,128)(2,1)}, u32[]{:S(2)}) copy-start(bf16[2,1,256,1024]{3,2,1,0:T(8,128)(2,1)} %g_ref.1) | copy-start | bytes 3145732
  23.0 23.5 %copy-start.3 = (bf16[2,1,64,512]{3,2,1,0:T(8,128)(2,1)S(1)}, bf16[2,1,64,512]{3,2,1,0:T(8,128)(2,1)}, u32[]{:S(2)}) copy-start(bf16[2,1,64,512]{3,2,1,0:T(8,128)(2,1)} %k_ref.3) | copy-start | bytes 393220
  23.0 23.5 %copy-start.5 = (bf16[2,1,64,512]{3,2,1,0:T(8,128)(2,1)S(1)}, bf16[2,1,64,512]{3,2,1,0:T(8,128)(2,1)}, u32[]{:S(2)}) copy-start(bf16[2,1,64,512]{3,2,1,0:T(8,128)(2,1)} %v_ref.3) | copy-start | bytes 393220
  23.2 34.8 %collective-permute-start.3 = (bf16[2,256,1024]{2,1,0:T(8,128)(2,1)S(1)}, bf16[2,256,1024]{2,1,0:T(8,128)(2,1)S(1)}, u32[]{:S(2)}, u32[]{:S(2)}) collective-permute-start(bf16[2,256,1024]{2,1,0:T(8,128)(2,1)S(1)} %get-tuple-element.27), channel_id=1, source_target_pairs={{0,4},{4,0},{8,12},{12,8},{16,20},{20,16},{24,28},{28,24},{32,36},... | collective-permute-start | bytes 3145736 | tf_op jit(solution)/shard_map/ppermute | solution.py:36
  27.9 15.8 %collective-permute-start.4 = (bf16[2,2,64,128]{3,2,1,0:T(8,128)(2,1)S(1)}, bf16[2,2,64,128]{3,2,1,0:T(8,128)(2,1)S(1)}, u32[]{:S(2)}, u32[]{:S(2)}) collective-permute-start(bf16[2,2,64,128]{3,2,1,0:T(8,128)(2,1)S(1)} %get-tuple-element.28), channel_id=1, source_target_pairs={{0,2},{1,3},{2,0},{3,1},{4,6},{5,7},{6,4},{7,5},{8,10},{9,11},{10,... | collective-permute-start | bytes 196616 | tf_op jit(solution)/shard_map/ppermute | solution.py:49
  37.4 9.0 %collective-permute-start.5 = (bf16[2,2,64,128]{3,2,1,0:T(8,128)(2,1)S(1)}, bf16[2,2,64,128]{3,2,1,0:T(8,128)(2,1)S(1)}, u32[]{:S(2)}, u32[]{:S(2)}) collective-permute-start(bf16[2,2,64,128]{3,2,1,0:T(8,128)(2,1)S(1)} %get-tuple-element.29), channel_id=1, source_target_pairs={{0,3},{1,0},{2,1},{3,2},{4,5},{5,6},{6,7},{7,4},{8,11},{9,8},{10,9... | collective-permute-start | bytes 196616 | tf_op jit(solution)/shard_map/ppermute | solution.py:49
  46.5 11.4 %collective-permute-start.6 = (bf16[2,512,128]{2,1,0:T(8,128)(2,1)S(1)}, bf16[2,512,128]{2,1,0:T(8,128)(2,1)}, u32[]{:S(2)}, u32[]{:S(2)}) collective-permute-start(bf16[2,512,128]{2,1,0:T(8,128)(2,1)S(1)} %join.1.here_ref), channel_id=1, source_target_pairs={{0,8},{8,16},{16,24},{24,32},{32,40},{40,48},{48,56},{56,64},{64,7... | collective-permute-start | bytes 786440 | tf_op jit(solution)/shard_map/ppermute | solution.py:32
  57.9 0.7 copy-start.6
  72.3 28.5 %collective-permute-start.7 = (bf16[2,256,1024]{2,1,0:T(8,128)(2,1)S(1)}, bf16[2,256,1024]{2,1,0:T(8,128)(2,1)S(1)}, u32[]{:S(2)}, u32[]{:S(2)}) collective-permute-start(bf16[2,256,1024]{2,1,0:T(8,128)(2,1)S(1)} %get-tuple-element.32), channel_id=1, source_target_pairs={{0,4},{4,0},{8,12},{12,8},{16,20},{20,16},{24,28},{28,24},{32,36},... | collective-permute-start | bytes 3145736 | tf_op jit(solution)/shard_map/ppermute | solution.py:36
  74.7 9.2 %collective-permute-start.8 = (bf16[2,512,128]{2,1,0:T(8,128)(2,1)S(1)}, bf16[2,512,128]{2,1,0:T(8,128)(2,1)S(1)}, u32[]{:S(2)}, u32[]{:S(2)}) collective-permute-start(bf16[2,512,128]{2,1,0:T(8,128)(2,1)S(1)} %get-tuple-element.34), channel_id=1, source_target_pairs={{8,0},{16,8},{24,16},{32,24},{40,32},{48,40},{56,48},{64,56},{72,6... | collective-permute-start | bytes 786440 | tf_op jit(solution)/shard_map/ppermute | solution.py:32
  84.0 16.7 %collective-permute-start.9 = (bf16[2,2,64,128]{3,2,1,0:T(8,128)(2,1)S(1)}, bf16[2,2,64,128]{3,2,1,0:T(8,128)(2,1)S(1)}, u32[]{:S(2)}, u32[]{:S(2)}) collective-permute-start(bf16[2,2,64,128]{3,2,1,0:T(8,128)(2,1)S(1)} %get-tuple-element.35), channel_id=1, source_target_pairs={{0,1},{1,2},{2,3},{3,0},{4,7},{5,4},{6,5},{7,6},{8,9},{9,10},{10,1... | collective-permute-start | bytes 196616 | tf_op jit(solution)/shard_map/ppermute | solution.py:49
  90.5 15.3 %collective-permute-start.10 = (bf16[2,2,64,128]{3,2,1,0:T(8,128)(2,1)S(1)}, bf16[2,2,64,128]{3,2,1,0:T(8,128)(2,1)S(1)}, u32[]{:S(2)}, u32[]{:S(2)}) collective-permute-start(bf16[2,2,64,128]{3,2,1,0:T(8,128)(2,1)S(1)} %get-tuple-element.39), channel_id=1, source_target_pairs={{0,2},{1,3},{2,0},{3,1},{4,6},{5,7},{6,4},{7,5},{8,10},{9,11},{10,... | collective-permute-start | bytes 196616 | tf_op jit(solution)/shard_map/ppermute | solution.py:49
  95.8 9.9 %collective-permute-start.11 = (bf16[2,2,64,128]{3,2,1,0:T(8,128)(2,1)S(1)}, bf16[2,2,64,128]{3,2,1,0:T(8,128)(2,1)S(1)}, u32[]{:S(2)}, u32[]{:S(2)}) collective-permute-start(bf16[2,2,64,128]{3,2,1,0:T(8,128)(2,1)S(1)} %get-tuple-element.40), channel_id=1, source_target_pairs={{0,3},{1,0},{2,1},{3,2},{4,5},{5,6},{6,7},{7,4},{8,11},{9,8},{10,9... | collective-permute-start | bytes 196616 | tf_op jit(solution)/shard_map/ppermute | solution.py:49
  105.8 11.8 %collective-permute-start.12 = (bf16[2,64,512]{2,1,0:T(8,128)(2,1)S(1)}, bf16[2,64,512]{2,1,0:T(8,128)(2,1)S(1)}, u32[]{:S(2)}, u32[]{:S(2)}) collective-permute-start(bf16[2,64,512]{2,1,0:T(8,128)(2,1)S(1)} %get-tuple-element.43), channel_id=1, source_target_pairs={{0,4},{4,0},{8,12},{12,8},{16,20},{20,16},{24,28},{28,24},{32,36},... | collective-permute-start | bytes 393224 | tf_op jit(solution)/shard_map/ppermute | solution.py:36

commit v3 on v2

v3 whole, which is shorter than its diff:
```python
import functools
import math

import jax
import jax.numpy as jnp
from jax import lax
from jax.experimental import pallas as pl
from jax.experimental.pallas import tpu as pltpu
from jax.sharding import PartitionSpec as P

HD = 128
FACTOR = 1.0 / math.sqrt(HD)
LOG2E = math.log2(math.e)
OUT = -1e30
VMEM = pl.BlockSpec(memory_space=pltpu.VMEM)
HBM = pl.BlockSpec(memory_space=pltpu.HBM)
ANY = pl.BlockSpec(memory_space=pl.ANY)
SMALL = pltpu.CompilerParams(vmem_limit_bytes=4 * 2**20)


def device_at(place, contexts):
    return 2 * place if 2 * place < contexts else 2 * (contexts - 1 - place) + 1


def along_line(block, step):
    contexts = lax.axis_size("cp")
    places = range(contexts)
    route = [
        (device_at(i, contexts), device_at(i + step, contexts)) for i in places if i + step in places
    ]
    return lax.ppermute(block, "cp", route)


def to_partner(block):
    return lax.ppermute(block, "cp", [(i, i ^ 1) for i in range(lax.axis_size("cp"))])


def offset(step, core, groups):
    return jnp.where(core == 0, step, groups - step)


def around(block, step):
    contexts, groups = lax.axis_size("cp"), lax.axis_size("tp")
    route = []
    for i in range(contexts):
        turn = step if i % 2 == 0 else groups - step
        route += [(i * groups + t, i * groups + (t + turn) % groups) for t in range(groups)]
    return lax.ppermute(block, ("cp", "tp"), route)


def dot(a, b, contract):
    return lax.dot_general(a, b, (contract, ((), ())), preferred_element_type=jnp.float32)


def aligned(index, size):
    return pl.ds(pl.multiple_of(index * size, size), size)


def split_kernel(groups, kv_ref, kv_pair_ref, *pieces):
    tp, core = lax.axis_index("tp"), lax.rem(lax.axis_index("cp"), 2)
    for step, piece in enumerate(pieces, 1):
        lanes = aligned(lax.rem(tp + offset(step, core, groups), groups), HD)
        for block, ref in enumerate((kv_ref, kv_pair_ref)):
            for kind in range(2):
                piece[block, kind] = ref[kind, core, 0, :, lanes]


def join_kernel(groups, kv_ref, kv_pair_ref, *refs):
    pieces, out_ref = refs[:-2], refs[-1]
    tp, core = lax.axis_index("tp"), lax.rem(lax.axis_index("cp"), 2)
    rows = kv_ref.shape[3]
    for block, ref in enumerate((kv_ref, kv_pair_ref)):
        place = aligned(block * groups + tp, rows)
        for kind in range(2):
            out_ref[kind, place, :] = ref[kind, core, 0, :, aligned(tp, HD)]
    for step, piece in enumerate(pieces, 1):
        source = lax.rem(tp - offset(step, core, groups) + groups, groups)
        for block in range(2):
            out_ref[:, aligned(block * groups + source, rows), :] = piece[block]


def total_kernel(groups, own_ref, came_ref, *pieces):
    tp, core = lax.axis_index("tp"), lax.rem(lax.axis_index("cp"), 2)
    rows = pieces[0].shape[2]
    for step, piece in enumerate(pieces):
        target = lax.rem(tp + offset(step, core, groups), groups)
        for block in range(2):
            place = aligned(block * groups + target, rows)
            total = own_ref[:, place, :] + came_ref[:, place, :].astype(jnp.float32)
            piece[block] = total.astype(piece.dtype)


def place_kernel(groups, *refs):
    pieces, outs = refs[:-3], refs[-2:]
    tp, core = lax.axis_index("tp"), lax.rem(lax.axis_index("cp"), 2)
    for step, piece in enumerate(pieces):
        lanes = aligned(lax.rem(tp - offset(step, core, groups) + groups, groups), HD)
        for block, out in enumerate(outs):
            out[:, :, lanes] = piece[block]


def finish_kernel(kept_ref, came_ref, k_ref, v_ref):
    core = lax.rem(lax.axis_index("cp"), 2)
    for kind, ref in enumerate((k_ref, v_ref)):
        ref[core, 0] = kept_ref[kind]
        ref[1 - core, 0] = came_ref[kind]


def prepare_kernel(contexts, q_ref, g_ref, len_ref, qg_ref, bias_ref, sems):
    chip, core = lax.axis_index("cp") // 2, lax.rem(lax.axis_index("cp"), 2)
    copies = []
    for kind, ref in enumerate((q_ref, g_ref)):
        for turn, half in enumerate((1 - core, core)):
            copies.append(
                pltpu.make_async_copy(
                    ref.at[half, 0], qg_ref.at[kind, turn], sems.at[2 * kind + turn]
                )
            )
    for copy in copies:
        copy.start()

    bf = jnp.bfloat16
    side, docs = bias_ref.shape[1], len_ref.shape[1]
    up, back = chip, contexts - 1 - chip
    blocks = (2 * jnp.where(core == 0, back, up) + 1, 2 * jnp.where(core == 0, up, back))
    lengths = jnp.broadcast_to(len_ref[...], (8, docs))
    before = lax.broadcasted_iota(jnp.int32, (docs, docs), 0)
    after = lax.broadcasted_iota(jnp.int32, (docs, docs), 1)
    upto = (before <= after).astype(jnp.float32).astype(bf)
    coarse = (lengths // 16).astype(jnp.float32).astype(bf)
    fine = (lengths % 16).astype(jnp.float32).astype(bf)
    over = ((1,), (0,))
    ends = (16.0 * dot(coarse, upto, over) + dot(fine, upto, over))[0:1, :]
    row = lax.broadcasted_iota(jnp.int32, (side, side), 0)
    column = lax.broadcasted_iota(jnp.int32, (side, side), 1)
    key = column.astype(jnp.float32)
    shared = jnp.where(column <= row, key, key - 2.0 * side)
    for turn, block in enumerate(blocks):
        first = block * side
        position = lax.broadcasted_iota(jnp.int32, (side, docs), 0) + first
        begins = jnp.where(ends <= position.astype(jnp.float32), ends, 0.0)
        begins = jnp.max(begins, axis=1, keepdims=True) - first.astype(jnp.float32)
        bias_ref[turn, :, :side] = jnp.where(shared >= begins, 0.0, OUT)
        bias_ref[turn, :, side:] = jnp.where(key - side >= begins, 0.0, OUT)

    for copy in copies:
        copy.wait()


def merge_kernel(mine_ref, came_ref, halo_ref, own_ref):
    side = mine_ref.shape[1] // 3
    for kind in range(2):
        mine = [mine_ref[kind, n * side : (n + 1) * side, :] for n in range(3)]
        came = [
            came_ref[kind, n * side : (n + 1) * side, :].astype(jnp.float32) for n in range(3)
        ]
        halo_ref[kind, :side, :] = mine[0].astype(halo_ref.dtype)
        halo_ref[kind, side:, :] = (mine[1] + came[0]).astype(halo_ref.dtype)
        own_ref[kind, :side, :] = mine[2] + came[1]
        own_ref[kind, side:, :] = came[2]


def fill_kernel(*refs):
    parts, (after_ref, attn_ref, dq_ref, done_ref, sems) = refs[:4], refs[4:]
    core = lax.rem(lax.axis_index("cp"), 2)
    copies = []
    for kind, ref in enumerate((attn_ref, dq_ref)):
        for turn, half in enumerate((1 - core, core)):
            n = 2 * kind + turn
            copies.append(pltpu.make_async_copy(parts[n], ref.at[half, 0], sems.at[n]))
    for copy in copies:
        copy.start()
    done_ref[...] = jnp.zeros_like(done_ref)
    for copy in copies:
        copy.wait()


def blend(field, side):
    low = side // 2
    row = lax.broadcasted_iota(jnp.int32, (low, low), 0)
    column = lax.broadcasted_iota(jnp.int32, (low, low), 1)
    causal = column <= row
    old, own = field[:, :side], field[:, 2 * side :]
    top = jnp.concatenate(
        [jnp.where(causal, own[:low, :low], old[:low, :low]), old[:low, low:]], axis=1
    )
    bottom = jnp.concatenate(
        [own[low:, :low], jnp.where(causal, own[low:, low:], old[low:, low:])], axis=1
    )
    shared = jnp.concatenate([top, bottom], axis=0)
    return jnp.concatenate([shared, field[:, side : 2 * side]], axis=1)


def unblend(field, side):
    low = side // 2
    row = lax.broadcasted_iota(jnp.int32, (low, low), 0)
    column = lax.broadcasted_iota(jnp.int32, (low, low), 1)
    causal = column <= row
    bf = jnp.bfloat16
    none = jnp.zeros((low, low), bf)
    a, d = field[:low, :low], field[low:, low : 2 * low]
    b, c = field[:low, low : 2 * low].astype(bf), field[low:, :low].astype(bf)
    a_own, a_old = jnp.where(causal, a, 0.0).astype(bf), jnp.where(causal, 0.0, a).astype(bf)
    d_own, d_old = jnp.where(causal, d, 0.0).astype(bf), jnp.where(causal, 0.0, d).astype(bf)
    old = jnp.concatenate(
        [jnp.concatenate([a_old, b], axis=1), jnp.concatenate([none, d_old], axis=1)], axis=0
    )
    own = jnp.concatenate(
        [jnp.concatenate([a_own, none], axis=1), jnp.concatenate([c, d_own], axis=1)], axis=0
    )
    return jnp.concatenate([old, field[:, side:].astype(bf), own], axis=1)


def line_window(behind_ref, here_ref, kind, turn, side):
    if turn == 0:
        parts = (behind_ref[kind, side:, :], here_ref[kind])
    else:
        parts = (behind_ref[kind], here_ref[kind, :side, :])
    return jnp.concatenate(parts, axis=0)


def attend_kernel(
    turn, qg_ref, behind_ref, here_ref, bias_ref, attn_ref, ds_ref, grad_ref, kt_ref, vt_ref, dk_ref, dv_ref
):
    side, heads = attn_ref.shape[0], ds_ref.shape[0]
    bf = jnp.bfloat16
    over, down = ((1,), (0,)), ((0,), (0,))
    values = line_window(behind_ref, here_ref, 1, turn, side)
    kt_ref[...] = line_window(behind_ref, here_ref, 0, turn, side).T
    vt_ref[...] = values.T

    def lanes(head):
        return slice(head * HD, (head + 1) * HD)

    def products(head):
        q, g = qg_ref[0, turn, :, lanes(head)], qg_ref[1, turn, :, lanes(head)]
        return q, g, dot(q, kt_ref[...], over), dot(g, vt_ref[...], over)

    def softmax(scores):
        scaled = blend(scores, side) * (FACTOR * LOG2E) + bias_ref[turn]
        raised = jnp.exp2(scaled - jnp.max(scaled, axis=1, keepdims=True))
        return raised * (1.0 / jnp.sum(raised, axis=1, keepdims=True))

    def finish(head, q, g, probs_low, ds):
        ds_ref[head] = ds
        value_term, key_term = dot(g, probs_low, down), dot(q, ds, down)
        if head == 0:
            dv_ref[...], dk_ref[...] = value_term, key_term
        else:
            dv_ref[...] += value_term
            dk_ref[...] += key_term

    pending = None
    ahead = products(0)
    for head in range(heads):
        q, g, scores, dprobs = ahead
        if head + 1 < heads:
            ahead = products(head + 1)
        probs = softmax(scores)
        probs_low = unblend(probs, side)
        attn = dot(probs_low, values, over).astype(bf)
        attn_ref[:, lanes(head)] = attn
        if pending is not None:
            finish(*pending)
        delta = jnp.sum(attn.astype(jnp.float32) * g.astype(jnp.float32), axis=1, keepdims=True)
        ds = unblend(probs * (blend(dprobs, side) - delta), side)
        pending = (head, q, g, probs_low, ds)
    finish(*pending)
    grad_ref[0] = (dk_ref[...].T * FACTOR).astype(grad_ref.dtype)
    grad_ref[1] = dv_ref[...].T.astype(grad_ref.dtype)


def query_kernel(*refs):
    inputs, outs = refs[:-2], refs[-2:]
    for turn, out in enumerate(outs):
        ds_ref, behind_ref, here_ref = inputs[3 * turn : 3 * turn + 3]
        heads, side = ds_ref.shape[0], ds_ref.shape[1]
        keys = line_window(behind_ref, here_ref, 0, turn, side)
        for head in range(heads):
            dq = dot(ds_ref[head], keys, ((1,), (0,))) * FACTOR
            out[:, head * HD : (head + 1) * HD] = dq.astype(out.dtype)


def local(queries, keys, values, out_grad, doc_lengths):
    side, width = queries.shape[2], queries.shape[3]
    contexts, groups = lax.axis_size("cp"), lax.axis_size("tp")
    rows = keys.shape[2]
    bf = jnp.bfloat16
    shape = jax.ShapeDtypeStruct
    piece = shape((2, 2, rows, HD), bf)

    kv = jnp.stack([keys, values])
    local_kv = (kv, to_partner(kv))
    sent = pl.pallas_call(
        functools.partial(split_kernel, groups),
        out_shape=[piece] * (groups - 1),
        in_specs=[VMEM] * 2,
        out_specs=[VMEM] * (groups - 1),
        compiler_params=SMALL,
        name="split",
    )(*local_kv)
    came = [around(block, step) for step, block in enumerate(sent, 1)]
    qg, bias = pl.pallas_call(
        functools.partial(prepare_kernel, contexts),
        out_shape=[shape((2, 2, side, width), bf), shape((2, side, 2 * side), jnp.float32)],
        in_specs=[HBM, HBM, VMEM],
        out_specs=[VMEM] * 2,
        scratch_shapes=[pltpu.SemaphoreType.DMA((4,))],
        compiler_params=SMALL,
        cost_estimate=pl.CostEstimate(
            flops=0, bytes_accessed=16 * side * width, transcendentals=0
        ),
        name="prepare",
    )(queries, out_grad, doc_lengths[None, :])
    here = pl.pallas_call(
        functools.partial(join_kernel, groups),
        out_shape=shape((2, 2 * side, HD), bf),
        in_specs=[VMEM] * (groups + 1) + [ANY],
        out_specs=VMEM,
        compiler_params=SMALL,
        name="join",
    )(*local_kv, *came, bias)
    behind = along_line(here, 1)
    here_pair, behind_pair = to_partner(here), to_partner(behind)
    heads = width // HD
    work = heads * side * 3 * side
    half = shape((side, width), bf)
    reach = (2, 3 * side, HD)

    def attend(turn, grad_type, *line):
        return pl.pallas_call(
            functools.partial(attend_kernel, turn),
            in_specs=[VMEM] * 4,
            out_specs=[VMEM] * 3,
            scratch_shapes=[pltpu.VMEM((HD, 3 * side), bf)] * 2
            + [pltpu.VMEM((HD, 3 * side), jnp.float32)] * 2,
            out_shape=[half, shape((heads, side, 3 * side), bf), shape(reach, grad_type)],
            compiler_params=pltpu.CompilerParams(vmem_limit_bytes=32 * 2**20),
            cost_estimate=pl.CostEstimate(
                flops=10 * work * HD, bytes_accessed=6 * side * width, transcendentals=work
            ),
            name="attend",
        )(qg, *line, bias)

    attn_pair, ds_pair, grad_pair = attend(0, bf, behind_pair, here_pair)
    came_grad = to_partner(grad_pair)
    attn_own, ds_own, grad_own = attend(1, jnp.float32, behind, here)
    halo, own = pl.pallas_call(
        merge_kernel,
        out_shape=[shape((2, 2 * side, HD), bf), shape((2, 2 * side, HD), jnp.float32)],
        in_specs=[VMEM] * 2,
        out_specs=[VMEM] * 2,
        compiler_params=SMALL,
        name="merge",
    )(grad_own, came_grad)
    came_halo = along_line(halo, -1)
    dq_pair, dq_own = pl.pallas_call(
        query_kernel,
        out_shape=[half, half],
        in_specs=[VMEM] * 6,
        out_specs=[VMEM] * 2,
        compiler_params=pltpu.CompilerParams(vmem_limit_bytes=16 * 2**20),
        cost_estimate=pl.CostEstimate(
            flops=4 * work * HD, bytes_accessed=4 * work, transcendentals=0
        ),
        name="query",
    )(ds_pair, behind_pair, here_pair, ds_own, behind, here)

    pieces = pl.pallas_call(
        functools.partial(total_kernel, groups),
        out_shape=[piece] * groups,
        in_specs=[VMEM] * 2,
        out_specs=[VMEM] * groups,
        compiler_params=SMALL,
        name="total",
    )(own, came_halo)
    returned = [pieces[0]] + [around(block, step) for step, block in enumerate(pieces[1:], 1)]
    attn_out, q_grad, filled = pl.pallas_call(
        fill_kernel,
        out_shape=[shape(queries.shape, bf)] * 2 + [shape((8, HD), jnp.float32)],
        in_specs=[VMEM] * 4 + [ANY],
        out_specs=[HBM, HBM, VMEM],
        scratch_shapes=[pltpu.SemaphoreType.DMA((4,))],
        compiler_params=SMALL,
        cost_estimate=pl.CostEstimate(
            flops=0, bytes_accessed=16 * side * width, transcendentals=0
        ),
        name="fill",
    )(attn_pair, attn_own, dq_pair, dq_own, returned[1])
    kept, for_pair = pl.pallas_call(
        functools.partial(place_kernel, groups),
        out_shape=[shape((2, rows, keys.shape[3]), bf)] * 2,
        in_specs=[VMEM] * groups + [ANY],
        out_specs=[VMEM] * 2,
        compiler_params=SMALL,
        name="place",
    )(*returned, filled)
    k_grad, v_grad = pl.pallas_call(
        finish_kernel,
        out_shape=[shape(keys.shape, bf)] * 2,
        in_specs=[VMEM] * 2,
        out_specs=[VMEM] * 2,
        compiler_params=SMALL,
        name="finish",
    )(kept, to_partner(for_pair))

    return (attn_out, q_grad, k_grad, v_grad)


def solution(mesh):
    heads, tokens = P(None, "cp", None, "tp"), P(None, "cp", "tp", None)
    return jax.shard_map(
        local,
        mesh=mesh,
        in_specs=(heads, tokens, tokens, heads, P()),
        out_specs=(heads, heads, tokens, tokens),
        check_vma=False,
    )
```

time: 119 us -> 102 us (0.86)
  the two profiles are of different devices: /device:TPU:95 before, /device:TPU:63 now
where the time goes in v3:
time: 102 us; the launch traced here: 101 us
  starting transfers between devices  63.1 us (62%)
  waiting for transfers between devices  19.7 us (19%)
  Pallas kernels  13.2 us (13%)
  local copies, waits for them, and re-layouts  3.12 us (3%)
    ppermute x6, starting transfers between devices, around(): return lax.ppermute(block, ('cp', 'tp'), route)  38.6 us
    ppermute x5, starting transfers between devices, to_partner(): lax.ppermute(block, 'cp', [(i, i ^ 1) for i in range(lax.axis_size('cp'))])  16.7 us
    pallas_call x2, Pallas kernels, attend(): pl.pallas_call(functools.partial(attend_kernel, turn), in_specs=[VMEM] *...  8.63 us
    ppermute x2, waiting for transfers between devices, along_line(): return lax.ppermute(block, 'cp', route)  8.07 us
    ppermute x6, waiting for transfers between devices, around(): return lax.ppermute(block, ('cp', 'tp'), route)  7.98 us
    ppermute x2, starting transfers between devices, along_line(): return lax.ppermute(block, 'cp', route)  7.82 us
    ppermute x5, waiting for transfers between devices, to_partner(): lax.ppermute(block, 'cp', [(i, i ^ 1) for i in range(lax.axis_size('cp'))])  3.6 us
    unnamed x6, local copies, waits for them, and re-layouts  3.12 us
  transfers between devices with their start and end apart: 13, of which 8 were waited for; matrix products, arithmetic and copies ran while one was open for 0% of the time, Pallas kernels for 8%

profile of v3, /device:TPU:63, one launch (start us, length us, event | category | flops | bytes accessed | tf_op | source)
XLA Modules:
  0.0 101.0 jit_solution(17167694150384532029)
XLA Ops:
  0.6 1.0 pad_maximum_fusion.kv_ref
  1.6 2.6 %collective-permute-start = (bf16[2,2,1,64,512]{4,3,2,1,0:T(8,128)(2,1)S(1)}, bf16[2,2,1,64,512]{4,3,2,1,0:T(8,128)(2,1)S(1)}, u32[]{:S(2)}, u32[]{:S(2)}) collective-permute-start(bf16[2,2,1,64,512]{4,3,2,1,0:T(8,128)(2,1)S(1)} %pad_maximum_fusion.kv_ref), channel_id=1, source_target_pairs={{0,4},{4,0},{8,12},{12,8},{16,20},{20,16},{24,28},{28,24},{32,36},... | collective-permute-start | bytes 786440 | tf_op jit(solution)/shard_map/ppermute | solution.py:35
  4.2 1.1 %collective-permute-done.kv_pair_ref = bf16[2,2,1,64,512]{4,3,2,1,0:T(8,128)(2,1)S(1)} collective-permute-done((bf16[2,2,1,64,512]{4,3,2,1,0:T(8,128)(2,1)S(1)}, bf16[2,2,1,64,512]{4,3,2,1,0:T(8,128)(2,1)S(1)}, u32[]{:S(2)}, u32[]{:S(2)}) %collective-permute-start) | collective-permute-done | bytes 262176 | tf_op jit(solution)/shard_map/ppermute | solution.py:35
  5.4 11.6 %collective-permute-start.1 = (bf16[2,2,64,128]{3,2,1,0:T(8,128)(2,1)S(1)}, bf16[2,2,64,128]{3,2,1,0:T(8,128)(2,1)S(1)}, u32[]{:S(2)}, u32[]{:S(2)}) collective-permute-start(bf16[2,2,64,128]{3,2,1,0:T(8,128)(2,1)S(1)} %get-tuple-element.31), channel_id=1, source_target_pairs={{0,1},{1,2},{2,3},{3,0},{4,7},{5,4},{6,5},{7,6},{8,9},{9,10},{10,1... | collective-permute-start | bytes 196616 | tf_op jit(solution)/shard_map/ppermute | solution.py:48
  17.0 4.9 %collective-permute-start.2 = (bf16[2,2,64,128]{3,2,1,0:T(8,128)(2,1)S(1)}, bf16[2,2,64,128]{3,2,1,0:T(8,128)(2,1)S(1)}, u32[]{:S(2)}, u32[]{:S(2)}) collective-permute-start(bf16[2,2,64,128]{3,2,1,0:T(8,128)(2,1)S(1)} %get-tuple-element.32), channel_id=1, source_target_pairs={{0,2},{1,3},{2,0},{3,1},{4,6},{5,7},{6,4},{7,5},{8,10},{9,11},{10,... | collective-permute-start | bytes 196616 | tf_op jit(solution)/shard_map/ppermute | solution.py:48
  21.9 7.3 %collective-permute-start.3 = (bf16[2,2,64,128]{3,2,1,0:T(8,128)(2,1)S(1)}, bf16[2,2,64,128]{3,2,1,0:T(8,128)(2,1)S(1)}, u32[]{:S(2)}, u32[]{:S(2)}) collective-permute-start(bf16[2,2,64,128]{3,2,1,0:T(8,128)(2,1)S(1)} %get-tuple-element.33), channel_id=1, source_target_pairs={{0,3},{1,0},{2,1},{3,2},{4,5},{5,6},{6,7},{7,4},{8,11},{9,8},{10,9... | collective-permute-start | bytes 196616 | tf_op jit(solution)/shard_map/ppermute | solution.py:48
  29.2 0.0 copy-start
  29.2 1.2 %copy-done = bf16[2,1,256,1024]{3,2,1,0:T(8,128)(2,1)S(1)} copy-done((bf16[2,1,256,1024]{3,2,1,0:T(8,128)(2,1)S(1)}, bf16[2,1,256,1024]{3,2,1,0:T(8,128)(2,1)}, u32[]{:S(2)}) %copy-start) | copy-done | bytes 1048600
  30.4 0.0 copy-start.1
  30.4 1.2 %copy-done.1 = bf16[2,1,256,1024]{3,2,1,0:T(8,128)(2,1)S(1)} copy-done((bf16[2,1,256,1024]{3,2,1,0:T(8,128)(2,1)S(1)}, bf16[2,1,256,1024]{3,2,1,0:T(8,128)(2,1)}, u32[]{:S(2)}) %copy-start.1) | copy-done | bytes 1048600
  31.6 0.0 copy-start.2
  31.6 0.7 copy-done.2
  32.3 0.5 prepare.1
  32.8 0.0 collective-permute-done.1.refs_0_
  32.8 0.0 collective-permute-done.2.refs_1_
  32.8 2.2 %collective-permute-done.3.refs_2_ = bf16[2,2,64,128]{3,2,1,0:T(8,128)(2,1)S(1)} collective-permute-done((bf16[2,2,64,128]{3,2,1,0:T(8,128)(2,1)S(1)}, bf16[2,2,64,128]{3,2,1,0:T(8,128)(2,1)S(1)}, u32[]{:S(2)}, u32[]{:S(2)}) %collective-permute-start.3) | collective-permute-done | bytes 65568 | tf_op jit(solution)/shard_map/ppermute | solution.py:48
  35.0 2.5 %collective-permute-start.4 = (bf16[2,512,128]{2,1,0:T(8,128)(2,1)S(1)}, bf16[2,512,128]{2,1,0:T(8,128)(2,1)S(1)}, u32[]{:S(2)}, u32[]{:S(2)}) collective-permute-start(bf16[2,512,128]{2,1,0:T(8,128)(2,1)S(1)} %join.1.here_ref.refs_5_), channel_id=1, source_target_pairs={{0,8},{8,16},{16,24},{24,32},{32,40},{40,48},{48,56},{56,64},{64,7... | collective-permute-start | bytes 786440 | tf_op jit(solution)/shard_map/ppermute | solution.py:31
  37.5 4.1 %collective-permute-start.6 = (bf16[2,512,128]{2,1,0:T(8,128)(2,1)S(1)}, bf16[2,512,128]{2,1,0:T(8,128)(2,1)S(1)}, u32[]{:S(2)}, u32[]{:S(2)}) collective-permute-start(bf16[2,512,128]{2,1,0:T(8,128)(2,1)S(1)} %join.1.here_ref.refs_5_), channel_id=1, source_target_pairs={{0,4},{4,0},{8,12},{12,8},{16,20},{20,16},{24,28},{28,24},{32,36},... | collective-permute-start | bytes 786440 | tf_op jit(solution)/shard_map/ppermute | solution.py:35
  41.6 4.8 %collective-permute-done.4.behind_ref.refs_4_ = bf16[2,512,128]{2,1,0:T(8,128)(2,1)S(1)} collective-permute-done((bf16[2,512,128]{2,1,0:T(8,128)(2,1)S(1)}, bf16[2,512,128]{2,1,0:T(8,128)(2,1)S(1)}, u32[]{:S(2)}, u32[]{:S(2)}) %collective-permute-start.4) | collective-permute-done | bytes 262176 | tf_op jit(solution)/shard_map/ppermute | solution.py:31
  46.4 1.9 %collective-permute-start.5 = (bf16[2,512,128]{2,1,0:T(8,128)(2,1)S(1)}, bf16[2,512,128]{2,1,0:T(8,128)(2,1)S(1)}, u32[]{:S(2)}, u32[]{:S(2)}) collective-permute-start(bf16[2,512,128]{2,1,0:T(8,128)(2,1)S(1)} %collective-permute-done.4.behind_ref.refs_4_), channel_id=1, source_target_pairs={{0,4},{4,0},{8,12},{12,8},{16,20},{20,16},{24,28},{28,24},{32,36},... | collective-permute-start | bytes 786440 | tf_op jit(solution)/shard_map/ppermute | solution.py:35
  48.3 0.0 collective-permute-done.6.here_ref.refs_2_
  48.3 1.5 %collective-permute-done.5.behind_ref.refs_1_ = bf16[2,512,128]{2,1,0:T(8,128)(2,1)S(1)} collective-permute-done((bf16[2,512,128]{2,1,0:T(8,128)(2,1)S(1)}, bf16[2,512,128]{2,1,0:T(8,128)(2,1)S(1)}, u32[]{:S(2)}, u32[]{:S(2)}) %collective-permute-start.5) | collective-permute-done | bytes 262176 | tf_op jit(solution)/shard_map/ppermute | solution.py:35
  49.8 4.3 %attend.2 = (bf16[256,1024]{1,0:T(8,128)(2,1)S(1)}, bf16[8,256,768]{2,1,0:T(8,128)(2,1)S(1)}, bf16[2,768,128]{2,1,0:T(8,128)(2,1)S(1)}) custom-call(bf16[2,2,256,1024]{3,2,1,0:T(8,128)(2,1)S(1)} %get-tuple-element.30.qg_ref, bf16[2,512,128]{2,1,0:T(8,128)(2,1)S(1)} %collective-permute-done.5.behind_ref.refs_1_, ...), custom_call_target="tpu_custom_call" | custom-call | flops 2013265920 | bytes 1572864 | tf_op jit(solution)/shard_map/attend/pallas_call | solution.py:331
  54.1 2.0 %collective-permute-start.7 = (bf16[2,768,128]{2,1,0:T(8,128)(2,1)S(1)}, bf16[2,768,128]{2,1,0:T(8,128)(2,1)S(1)}, u32[]{:S(2)}, u32[]{:S(2)}) collective-permute-start(bf16[2,768,128]{2,1,0:T(8,128)(2,1)S(1)} %get-tuple-element.42), channel_id=1, source_target_pairs={{0,4},{4,0},{8,12},{12,8},{16,20},{20,16},{24,28},{28,24},{32,36},... | collective-permute-start | bytes 1179656 | tf_op jit(solution)/shard_map/ppermute | solution.py:35
  56.2 4.3 %attend.3 = (bf16[256,1024]{1,0:T(8,128)(2,1)S(1)}, bf16[8,256,768]{2,1,0:T(8,128)(2,1)S(1)}, f32[2,768,128]{2,1,0:T(8,128)S(1)}) custom-call(bf16[2,2,256,1024]{3,2,1,0:T(8,128)(2,1)S(1)} %get-tuple-element.30.qg_ref, bf16[2,512,128]{2,1,0:T(8,128)(2,1)S(1)} %collective-permute-done.4.behind_ref.refs_4_, bf16[2,512,128]{2,1,0:T(8,128)(2,1)S(1)} %join.1.here_ref.refs_5_, ...), custom_call_target="tpu_custom_call" | custom-call | flops 2013265920 | bytes 1572864 | tf_op jit(solution)/shard_map/attend/pallas_call | solution.py:331
  60.5 0.0 collective-permute-done.7.came_ref
  60.5 0.1 merge.1
  60.6 5.4 %collective-permute-start.8 = (bf16[2,512,128]{2,1,0:T(8,128)(2,1)S(1)}, bf16[2,512,128]{2,1,0:T(8,128)(2,1)S(1)}, u32[]{:S(2)}, u32[]{:S(2)}) collective-permute-start(bf16[2,512,128]{2,1,0:T(8,128)(2,1)S(1)} %get-tuple-element.44), channel_id=1, source_target_pairs={{8,0},{16,8},{24,16},{32,24},{40,32},{48,40},{56,48},{64,56},{72,6... | collective-permute-start | bytes 786440 | tf_op jit(solution)/shard_map/ppermute | solution.py:31
  66.0 3.3 %collective-permute-done.8.came_ref = bf16[2,512,128]{2,1,0:T(8,128)(2,1)S(1)} collective-permute-done((bf16[2,512,128]{2,1,0:T(8,128)(2,1)S(1)}, bf16[2,512,128]{2,1,0:T(8,128)(2,1)S(1)}, u32[]{:S(2)}, u32[]{:S(2)}) %collective-permute-start.8) | collective-permute-done | bytes 262176 | tf_op jit(solution)/shard_map/ppermute | solution.py:31
  69.3 5.5 %collective-permute-start.9 = (bf16[2,2,64,128]{3,2,1,0:T(8,128)(2,1)S(1)}, bf16[2,2,64,128]{3,2,1,0:T(8,128)(2,1)S(1)}, u32[]{:S(2)}, u32[]{:S(2)}) collective-permute-start(bf16[2,2,64,128]{3,2,1,0:T(8,128)(2,1)S(1)} %get-tuple-element.45), channel_id=1, source_target_pairs={{0,1},{1,2},{2,3},{3,0},{4,7},{5,4},{6,5},{7,6},{8,9},{9,10},{10,1... | collective-permute-start | bytes 196616 | tf_op jit(solution)/shard_map/ppermute | solution.py:48
  74.8 6.0 %collective-permute-start.10 = (bf16[2,2,64,128]{3,2,1,0:T(8,128)(2,1)S(1)}, bf16[2,2,64,128]{3,2,1,0:T(8,128)(2,1)S(1)}, u32[]{:S(2)}, u32[]{:S(2)}) collective-permute-start(bf16[2,2,64,128]{3,2,1,0:T(8,128)(2,1)S(1)} %get-tuple-element.49), channel_id=1, source_target_pairs={{0,2},{1,3},{2,0},{3,1},{4,6},{5,7},{6,4},{7,5},{8,10},{9,11},{10,... | collective-permute-start | bytes 196616 | tf_op jit(solution)/shard_map/ppermute | solution.py:48
  80.9 3.3 %collective-permute-start.11 = (bf16[2,2,64,128]{3,2,1,0:T(8,128)(2,1)S(1)}, bf16[2,2,64,128]{3,2,1,0:T(8,128)(2,1)S(1)}, u32[]{:S(2)}, u32[]{:S(2)}) collective-permute-start(bf16[2,2,64,128]{3,2,1,0:T(8,128)(2,1)S(1)} %get-tuple-element.50), channel_id=1, source_target_pairs={{0,3},{1,0},{2,1},{3,2},{4,5},{5,6},{6,7},{7,4},{8,11},{9,8},{10,9... | collective-permute-start | bytes 196616 | tf_op jit(solution)/shard_map/ppermute | solution.py:48
  84.2 1.8 %query.1 = (bf16[256,1024]{1,0:T(8,128)(2,1)S(1)}, bf16[256,1024]{1,0:T(8,128)(2,1)S(1)}) custom-call(bf16[8,256,768]{2,1,0:T(8,128)(2,1)S(1)} %get-tuple-element.37.refs_0_, bf16[2,512,128]{2,1,0:T(8,128)(2,1)S(1)} %collective-permute-done.5.behind_ref.refs_1_, bf16[2,512,128]{2,1,0:T(8,128)(2,1)S(1)} %collective-permute-done.6.here_ref.refs_2_, ...), custom_call_target="tpu_custom_call" | custom-call | flops 805306368 | bytes 6291456 | tf_op jit(solution)/shard_map/query/pallas_call | solution.py:357
  86.0 0.0 collective-permute-done.9.refs_4_.refs_1_
  86.0 1.4 %fill.1 = (bf16[2,1,256,1024]{3,2,1,0:T(8,128)(2,1)}, bf16[2,1,256,1024]{3,2,1,0:T(8,128)(2,1)}, f32[8,128]{1,0:T(8,128)S(1)}) custom-call(bf16[256,1024]{1,0:T(8,128)(2,1)S(1)} %get-tuple-element.35.refs_0_, bf16[256,1024]{1,0:T(8,128)(2,1)S(1)} %get-tuple-element.36.refs_1_, bf16[256,1024]{1,0:T(8,128)(2,1)S(1)} %get-tuple-element.39.refs_2_, ...), custom_call_target="tpu_custom_call" | custom-call | bytes 4194304 | tf_op jit(solution)/shard_map/fill/pallas_call | solution.py:378
  87.4 1.7 %collective-permute-done.10.refs_2_ = bf16[2,2,64,128]{3,2,1,0:T(8,128)(2,1)S(1)} collective-permute-done((bf16[2,2,64,128]{3,2,1,0:T(8,128)(2,1)S(1)}, bf16[2,2,64,128]{3,2,1,0:T(8,128)(2,1)S(1)}, u32[]{:S(2)}, u32[]{:S(2)}) %collective-permute-start.10) | collective-permute-done | bytes 65568 | tf_op jit(solution)/shard_map/ppermute | solution.py:48
  89.1 4.0 %collective-permute-done.11.refs_3_ = bf16[2,2,64,128]{3,2,1,0:T(8,128)(2,1)S(1)} collective-permute-done((bf16[2,2,64,128]{3,2,1,0:T(8,128)(2,1)S(1)}, bf16[2,2,64,128]{3,2,1,0:T(8,128)(2,1)S(1)}, u32[]{:S(2)}, u32[]{:S(2)}) %collective-permute-start.11) | collective-permute-done | bytes 65568 | tf_op jit(solution)/shard_map/ppermute | solution.py:48
  93.2 0.1 place.1
  93.2 6.1 %collective-permute-start.12 = (bf16[2,64,512]{2,1,0:T(8,128)(2,1)S(1)}, bf16[2,64,512]{2,1,0:T(8,128)(2,1)S(1)}, u32[]{:S(2)}, u32[]{:S(2)}) collective-permute-start(bf16[2,64,512]{2,1,0:T(8,128)(2,1)S(1)} %get-tuple-element.53), channel_id=1, source_target_pairs={{0,4},{4,0},{8,12},{12,8},{16,20},{20,16},{24,28},{28,24},{32,36},... | collective-permute-start | bytes 393224 | tf_op jit(solution)/shard_map/ppermute | solution.py:35
  99.3 1.0 collective-permute-done.12.came_ref
  100.3 0.7 finish.1
  (3 shorter events, 0.1 us)
Async XLA Ops:
  1.6 3.7 %collective-permute-start = (bf16[2,2,1,64,512]{4,3,2,1,0:T(8,128)(2,1)S(1)}, bf16[2,2,1,64,512]{4,3,2,1,0:T(8,128)(2,1)S(1)}, u32[]{:S(2)}, u32[]{:S(2)}) collective-permute-start(bf16[2,2,1,64,512]{4,3,2,1,0:T(8,128)(2,1)S(1)} %pad_maximum_fusion.kv_ref), channel_id=1, source_target_pairs={{0,4},{4,0},{8,12},{12,8},{16,20},{20,16},{24,28},{28,24},{32,36},... | collective-permute-start | bytes 786440 | tf_op jit(solution)/shard_map/ppermute | solution.py:35
  5.4 27.4 %collective-permute-start.1 = (bf16[2,2,64,128]{3,2,1,0:T(8,128)(2,1)S(1)}, bf16[2,2,64,128]{3,2,1,0:T(8,128)(2,1)S(1)}, u32[]{:S(2)}, u32[]{:S(2)}) collective-permute-start(bf16[2,2,64,128]{3,2,1,0:T(8,128)(2,1)S(1)} %get-tuple-element.31), channel_id=1, source_target_pairs={{0,1},{1,2},{2,3},{3,0},{4,7},{5,4},{6,5},{7,6},{8,9},{9,10},{10,1... | collective-permute-start | bytes 196616 | tf_op jit(solution)/shard_map/ppermute | solution.py:48
  17.0 15.8 %collective-permute-start.2 = (bf16[2,2,64,128]{3,2,1,0:T(8,128)(2,1)S(1)}, bf16[2,2,64,128]{3,2,1,0:T(8,128)(2,1)S(1)}, u32[]{:S(2)}, u32[]{:S(2)}) collective-permute-start(bf16[2,2,64,128]{3,2,1,0:T(8,128)(2,1)S(1)} %get-tuple-element.32), channel_id=1, source_target_pairs={{0,2},{1,3},{2,0},{3,1},{4,6},{5,7},{6,4},{7,5},{8,10},{9,11},{10,... | collective-permute-start | bytes 196616 | tf_op jit(solution)/shard_map/ppermute | solution.py:48
  21.9 13.1 %collective-permute-start.3 = (bf16[2,2,64,128]{3,2,1,0:T(8,128)(2,1)S(1)}, bf16[2,2,64,128]{3,2,1,0:T(8,128)(2,1)S(1)}, u32[]{:S(2)}, u32[]{:S(2)}) collective-permute-start(bf16[2,2,64,128]{3,2,1,0:T(8,128)(2,1)S(1)} %get-tuple-element.33), channel_id=1, source_target_pairs={{0,3},{1,0},{2,1},{3,2},{4,5},{5,6},{6,7},{7,4},{8,11},{9,8},{10,9... | collective-permute-start | bytes 196616 | tf_op jit(solution)/shard_map/ppermute | solution.py:48
  29.2 1.2 %copy-start = (bf16[2,1,256,1024]{3,2,1,0:T(8,128)(2,1)S(1)}, bf16[2,1,256,1024]{3,2,1,0:T(8,128)(2,1)}, u32[]{:S(2)}) copy-start(bf16[2,1,256,1024]{3,2,1,0:T(8,128)(2,1)} %q_ref.1) | copy-start | bytes 3145732
  30.4 1.2 %copy-start.1 = (bf16[2,1,256,1024]{3,2,1,0:T(8,128)(2,1)S(1)}, bf16[2,1,256,1024]{3,2,1,0:T(8,128)(2,1)}, u32[]{:S(2)}) copy-start(bf16[2,1,256,1024]{3,2,1,0:T(8,128)(2,1)} %g_ref.1) | copy-start | bytes 3145732
  31.6 0.7 copy-start.2
  35.0 11.3 %collective-permute-start.4 = (bf16[2,512,128]{2,1,0:T(8,128)(2,1)S(1)}, bf16[2,512,128]{2,1,0:T(8,128)(2,1)S(1)}, u32[]{:S(2)}, u32[]{:S(2)}) collective-permute-start(bf16[2,512,128]{2,1,0:T(8,128)(2,1)S(1)} %join.1.here_ref.refs_5_), channel_id=1, source_target_pairs={{0,8},{8,16},{16,24},{24,32},{32,40},{40,48},{48,56},{56,64},{64,7... | collective-permute-start | bytes 786440 | tf_op jit(solution)/shard_map/ppermute | solution.py:31
  37.5 10.8 %collective-permute-start.6 = (bf16[2,512,128]{2,1,0:T(8,128)(2,1)S(1)}, bf16[2,512,128]{2,1,0:T(8,128)(2,1)S(1)}, u32[]{:S(2)}, u32[]{:S(2)}) collective-permute-start(bf16[2,512,128]{2,1,0:T(8,128)(2,1)S(1)} %join.1.here_ref.refs_5_), channel_id=1, source_target_pairs={{0,4},{4,0},{8,12},{12,8},{16,20},{20,16},{24,28},{28,24},{32,36},... | collective-permute-start | bytes 786440 | tf_op jit(solution)/shard_map/ppermute | solution.py:35
  46.4 3.4 %collective-permute-start.5 = (bf16[2,512,128]{2,1,0:T(8,128)(2,1)S(1)}, bf16[2,512,128]{2,1,0:T(8,128)(2,1)S(1)}, u32[]{:S(2)}, u32[]{:S(2)}) collective-permute-start(bf16[2,512,128]{2,1,0:T(8,128)(2,1)S(1)} %collective-permute-done.4.behind_ref.refs_4_), channel_id=1, source_target_pairs={{0,4},{4,0},{8,12},{12,8},{16,20},{20,16},{24,28},{28,24},{32,36},... | collective-permute-start | bytes 786440 | tf_op jit(solution)/shard_map/ppermute | solution.py:35
  54.1 6.4 %collective-permute-start.7 = (bf16[2,768,128]{2,1,0:T(8,128)(2,1)S(1)}, bf16[2,768,128]{2,1,0:T(8,128)(2,1)S(1)}, u32[]{:S(2)}, u32[]{:S(2)}) collective-permute-start(bf16[2,768,128]{2,1,0:T(8,128)(2,1)S(1)} %get-tuple-element.42), channel_id=1, source_target_pairs={{0,4},{4,0},{8,12},{12,8},{16,20},{20,16},{24,28},{28,24},{32,36},... | collective-permute-start | bytes 1179656 | tf_op jit(solution)/shard_map/ppermute | solution.py:35
  60.6 8.7 %collective-permute-start.8 = (bf16[2,512,128]{2,1,0:T(8,128)(2,1)S(1)}, bf16[2,512,128]{2,1,0:T(8,128)(2,1)S(1)}, u32[]{:S(2)}, u32[]{:S(2)}) collective-permute-start(bf16[2,512,128]{2,1,0:T(8,128)(2,1)S(1)} %get-tuple-element.44), channel_id=1, source_target_pairs={{8,0},{16,8},{24,16},{32,24},{40,32},{48,40},{56,48},{64,56},{72,6... | collective-permute-start | bytes 786440 | tf_op jit(solution)/shard_map/ppermute | solution.py:31
  69.3 16.7 %collective-permute-start.9 = (bf16[2,2,64,128]{3,2,1,0:T(8,128)(2,1)S(1)}, bf16[2,2,64,128]{3,2,1,0:T(8,128)(2,1)S(1)}, u32[]{:S(2)}, u32[]{:S(2)}) collective-permute-start(bf16[2,2,64,128]{3,2,1,0:T(8,128)(2,1)S(1)} %get-tuple-element.45), channel_id=1, source_target_pairs={{0,1},{1,2},{2,3},{3,0},{4,7},{5,4},{6,5},{7,6},{8,9},{9,10},{10,1... | collective-permute-start | bytes 196616 | tf_op jit(solution)/shard_map/ppermute | solution.py:48
  74.8 14.3 %collective-permute-start.10 = (bf16[2,2,64,128]{3,2,1,0:T(8,128)(2,1)S(1)}, bf16[2,2,64,128]{3,2,1,0:T(8,128)(2,1)S(1)}, u32[]{:S(2)}, u32[]{:S(2)}) collective-permute-start(bf16[2,2,64,128]{3,2,1,0:T(8,128)(2,1)S(1)} %get-tuple-element.49), channel_id=1, source_target_pairs={{0,2},{1,3},{2,0},{3,1},{4,6},{5,7},{6,4},{7,5},{8,10},{9,11},{10,... | collective-permute-start | bytes 196616 | tf_op jit(solution)/shard_map/ppermute | solution.py:48
  80.9 12.3 %collective-permute-start.11 = (bf16[2,2,64,128]{3,2,1,0:T(8,128)(2,1)S(1)}, bf16[2,2,64,128]{3,2,1,0:T(8,128)(2,1)S(1)}, u32[]{:S(2)}, u32[]{:S(2)}) collective-permute-start(bf16[2,2,64,128]{3,2,1,0:T(8,128)(2,1)S(1)} %get-tuple-element.50), channel_id=1, source_target_pairs={{0,3},{1,0},{2,1},{3,2},{4,5},{5,6},{6,7},{7,4},{8,11},{9,8},{10,9... | collective-permute-start | bytes 196616 | tf_op jit(solution)/shard_map/ppermute | solution.py:48
  93.2 7.1 %collective-permute-start.12 = (bf16[2,64,512]{2,1,0:T(8,128)(2,1)S(1)}, bf16[2,64,512]{2,1,0:T(8,128)(2,1)S(1)}, u32[]{:S(2)}, u32[]{:S(2)}) collective-permute-start(bf16[2,64,512]{2,1,0:T(8,128)(2,1)S(1)} %get-tuple-element.53), channel_id=1, source_target_pairs={{0,4},{4,0},{8,12},{12,8},{16,20},{20,16},{24,28},{28,24},{32,36},... | collective-permute-start | bytes 393224 | tf_op jit(solution)/shard_map/ppermute | solution.py:35

commit v4 on v3

--- a/solution.py
+++ b/solution.py
@@ -18,21 +18,34 @@
 SMALL = pltpu.CompilerParams(vmem_limit_bytes=4 * 2**20)
 
 
-def device_at(place, contexts):
-    return 2 * place if 2 * place < contexts else 2 * (contexts - 1 - place) + 1
-
-
-def along_line(block, step):
+def far_x(i, contexts):
+    if i % 2:
+        return i - 2
+    return i + 2 if i + 2 < contexts else i + 1
+
+
+def across_y(i, contexts):
+    if i % 2:
+        return min(i + 1, contexts - 1)
+    return i - 1
+
+
+def far_y(i, contexts):
+    if i % 2:
+        return i + 2 if i + 2 < contexts else i - 1
+    return i - 2
+
+
+def near_x(i, contexts):
+    return i ^ 1
+
+
+def move(block, target, back=False):
     contexts = lax.axis_size("cp")
-    places = range(contexts)
-    route = [
-        (device_at(i, contexts), device_at(i + step, contexts)) for i in places if i + step in places
-    ]
+    route = [(i, target(i, contexts)) for i in range(contexts) if target(i, contexts) >= 0]
+    if back:
+        route = [(there, here) for here, there in route]
     return lax.ppermute(block, "cp", route)
-
-
-def to_partner(block):
-    return lax.ppermute(block, "cp", [(i, i ^ 1) for i in range(lax.axis_size("cp"))])
 
 
 def offset(step, core, groups):
@@ -56,38 +69,39 @@
     return pl.ds(pl.multiple_of(index * size, size), size)
 
 
-def split_kernel(groups, kv_ref, kv_pair_ref, *pieces):
+def split_kernel(groups, kv_ref, *pieces):
     tp, core = lax.axis_index("tp"), lax.rem(lax.axis_index("cp"), 2)
     for step, piece in enumerate(pieces, 1):
         lanes = aligned(lax.rem(tp + offset(step, core, groups), groups), HD)
-        for block, ref in enumerate((kv_ref, kv_pair_ref)):
-            for kind in range(2):
-                piece[block, kind] = ref[kind, core, 0, :, lanes]
-
-
-def join_kernel(groups, kv_ref, kv_pair_ref, *refs):
-    pieces, out_ref = refs[:-2], refs[-1]
+        for kind in range(2):
+            for block, half in enumerate((core, 1 - core)):
+                piece[block, kind] = kv_ref[kind, half, 0, :, lanes]
+
+
+def join_kernel(groups, kv_ref, *refs):
+    pieces, outs = refs[:-3], refs[-2:]
     tp, core = lax.axis_index("tp"), lax.rem(lax.axis_index("cp"), 2)
     rows = kv_ref.shape[3]
-    for block, ref in enumerate((kv_ref, kv_pair_ref)):
-        place = aligned(block * groups + tp, rows)
-        for kind in range(2):
-            out_ref[kind, place, :] = ref[kind, core, 0, :, aligned(tp, HD)]
+    for kind in range(2):
+        for half, out in zip((core, 1 - core), outs):
+            out[kind, aligned(tp, rows), :] = kv_ref[kind, half, 0, :, aligned(tp, HD)]
     for step, piece in enumerate(pieces, 1):
         source = lax.rem(tp - offset(step, core, groups) + groups, groups)
-        for block in range(2):
-            out_ref[:, aligned(block * groups + source, rows), :] = piece[block]
-
-
-def total_kernel(groups, own_ref, came_ref, *pieces):
+        for block, out in enumerate(outs):
+            out[:, aligned(source, rows), :] = piece[block]
+
+
+def total_kernel(groups, *refs):
+    terms, pieces = refs[:6], refs[6:]
     tp, core = lax.axis_index("tp"), lax.rem(lax.axis_index("cp"), 2)
     rows = pieces[0].shape[2]
     for step, piece in enumerate(pieces):
-        target = lax.rem(tp + offset(step, core, groups), groups)
+        place = aligned(lax.rem(tp + offset(step, core, groups), groups), rows)
         for block in range(2):
-            place = aligned(block * groups + target, rows)
-            total = own_ref[:, place, :] + came_ref[:, place, :].astype(jnp.float32)
-            piece[block] = total.astype(piece.dtype)
+            own, *came = [ref[:, place, :] for ref in terms[3 * block : 3 * block + 3]]
+            for term in came:
+                own = own + term.astype(jnp.float32)
+            piece[block] = own.astype(piece.dtype)
 
 
 def place_kernel(groups, *refs):
@@ -95,22 +109,17 @@
     tp, core = lax.axis_index("tp"), lax.rem(lax.axis_index("cp"), 2)
     for step, piece in enumerate(pieces):
         lanes = aligned(lax.rem(tp - offset(step, core, groups) + groups, groups), HD)
-        for block, out in enumerate(outs):
-            out[:, :, lanes] = piece[block]
-
-
-def finish_kernel(kept_ref, came_ref, k_ref, v_ref):
-    core = lax.rem(lax.axis_index("cp"), 2)
-    for kind, ref in enumerate((k_ref, v_ref)):
-        ref[core, 0] = kept_ref[kind]
-        ref[1 - core, 0] = came_ref[kind]
+        for block, half in enumerate((core, 1 - core)):
+            for kind, out in enumerate(outs):
+                out[half, 0, :, lanes] = piece[block, kind]
 
 
 def prepare_kernel(contexts, q_ref, g_ref, len_ref, qg_ref, bias_ref, sems):
-    chip, core = lax.axis_index("cp") // 2, lax.rem(lax.axis_index("cp"), 2)
+    cp = lax.axis_index("cp")
+    core = lax.rem(cp, 2)
     copies = []
     for kind, ref in enumerate((q_ref, g_ref)):
-        for turn, half in enumerate((1 - core, core)):
+        for turn, half in enumerate((core, 1 - core)):
             copies.append(
                 pltpu.make_async_copy(
                     ref.at[half, 0], qg_ref.at[kind, turn], sems.at[2 * kind + turn]
@@ -121,8 +130,8 @@
 
     bf = jnp.bfloat16
     side, docs = bias_ref.shape[1], len_ref.shape[1]
-    up, back = chip, contexts - 1 - chip
-    blocks = (2 * jnp.where(core == 0, back, up) + 1, 2 * jnp.where(core == 0, up, back))
+    up, back = cp, 2 * contexts - 1 - cp
+    blocks = (jnp.where(core == 0, up, back), jnp.where(core == 0, back, up))
     lengths = jnp.broadcast_to(len_ref[...], (8, docs))
     before = lax.broadcasted_iota(jnp.int32, (docs, docs), 0)
     after = lax.broadcasted_iota(jnp.int32, (docs, docs), 1)
@@ -147,25 +156,12 @@
         copy.wait()
 
 
-def merge_kernel(mine_ref, came_ref, halo_ref, own_ref):
-    side = mine_ref.shape[1] // 3
-    for kind in range(2):
-        mine = [mine_ref[kind, n * side : (n + 1) * side, :] for n in range(3)]
-        came = [
-            came_ref[kind, n * side : (n + 1) * side, :].astype(jnp.float32) for n in range(3)
-        ]
-        halo_ref[kind, :side, :] = mine[0].astype(halo_ref.dtype)
-        halo_ref[kind, side:, :] = (mine[1] + came[0]).astype(halo_ref.dtype)
-        own_ref[kind, :side, :] = mine[2] + came[1]
-        own_ref[kind, side:, :] = came[2]
-
-
 def fill_kernel(*refs):
     parts, (after_ref, attn_ref, dq_ref, done_ref, sems) = refs[:4], refs[4:]
     core = lax.rem(lax.axis_index("cp"), 2)
     copies = []
     for kind, ref in enumerate((attn_ref, dq_ref)):
-        for turn, half in enumerate((1 - core, core)):
+        for turn, half in enumerate((core, 1 - core)):
             n = 2 * kind + turn
             copies.append(pltpu.make_async_copy(parts[n], ref.at[half, 0], sems.at[n]))
     for copy in copies:
@@ -211,22 +207,31 @@
     return jnp.concatenate([old, field[:, side:].astype(bf), own], axis=1)
 
 
-def line_window(behind_ref, here_ref, kind, turn, side):
-    if turn == 0:
-        parts = (behind_ref[kind, side:, :], here_ref[kind])
-    else:
-        parts = (behind_ref[kind], here_ref[kind, :side, :])
-    return jnp.concatenate(parts, axis=0)
-
-
 def attend_kernel(
-    turn, qg_ref, behind_ref, here_ref, bias_ref, attn_ref, ds_ref, grad_ref, kt_ref, vt_ref, dk_ref, dv_ref
+    turn,
+    qg_ref,
+    oldest_ref,
+    middle_ref,
+    here_ref,
+    bias_ref,
+    attn_ref,
+    ds_ref,
+    to_oldest_ref,
+    to_middle_ref,
+    own_ref,
+    kt_ref,
+    vt_ref,
+    dk_ref,
+    dv_ref,
 ):
     side, heads = attn_ref.shape[0], ds_ref.shape[0]
     bf = jnp.bfloat16
     over, down = ((1,), (0,)), ((0,), (0,))
-    values = line_window(behind_ref, here_ref, 1, turn, side)
-    kt_ref[...] = line_window(behind_ref, here_ref, 0, turn, side).T
+    keys, values = [
+        jnp.concatenate([oldest_ref[kind], middle_ref[kind], here_ref[kind]], axis=0)
+        for kind in range(2)
+    ]
+    kt_ref[...] = keys.T
     vt_ref[...] = values.T
 
     def lanes(head):
@@ -266,16 +271,18 @@
         ds = unblend(probs * (blend(dprobs, side) - delta), side)
         pending = (head, q, g, probs_low, ds)
     finish(*pending)
-    grad_ref[0] = (dk_ref[...].T * FACTOR).astype(grad_ref.dtype)
-    grad_ref[1] = dv_ref[...].T.astype(grad_ref.dtype)
+    for kind, (ref, factor) in enumerate(((dk_ref, FACTOR), (dv_ref, 1.0))):
+        for n, out in enumerate((to_oldest_ref, to_middle_ref, own_ref)):
+            term = ref[:, n * side : (n + 1) * side].T * factor
+            out[kind] = term.astype(out.dtype)
 
 
 def query_kernel(*refs):
     inputs, outs = refs[:-2], refs[-2:]
     for turn, out in enumerate(outs):
-        ds_ref, behind_ref, here_ref = inputs[3 * turn : 3 * turn + 3]
-        heads, side = ds_ref.shape[0], ds_ref.shape[1]
-        keys = line_window(behind_ref, here_ref, 0, turn, side)
+        ds_ref, *blocks = inputs[4 * turn : 4 * turn + 4]
+        heads = ds_ref.shape[0]
+        keys = jnp.concatenate([ref[0] for ref in blocks], axis=0)
         for head in range(heads):
             dq = dot(ds_ref[head], keys, ((1,), (0,))) * FACTOR
             out[:, head * HD : (head + 1) * HD] = dq.astype(out.dtype)
@@ -290,15 +297,14 @@
     piece = shape((2, 2, rows, HD), bf)
 
     kv = jnp.stack([keys, values])
-    local_kv = (kv, to_partner(kv))
     sent = pl.pallas_call(
         functools.partial(split_kernel, groups),
         out_shape=[piece] * (groups - 1),
-        in_specs=[VMEM] * 2,
+        in_specs=[VMEM],
         out_specs=[VMEM] * (groups - 1),
         compiler_params=SMALL,
         name="split",
-    )(*local_kv)
+    )(kv)
     came = [around(block, step) for step, block in enumerate(sent, 1)]
     qg, bias = pl.pallas_call(
         functools.partial(prepare_kernel, contexts),
@@ -312,29 +318,36 @@
         ),
         name="prepare",
     )(queries, out_grad, doc_lengths[None, :])
-    here = pl.pallas_call(
+    block = shape((2, side, HD), bf)
+    x, y = pl.pallas_call(
         functools.partial(join_kernel, groups),
-        out_shape=shape((2, 2 * side, HD), bf),
-        in_specs=[VMEM] * (groups + 1) + [ANY],
-        out_specs=VMEM,
+        out_shape=[block] * 2,
+        in_specs=[VMEM] * groups + [ANY],
+        out_specs=[VMEM] * 2,
         compiler_params=SMALL,
         name="join",
-    )(*local_kv, *came, bias)
-    behind = along_line(here, 1)
-    here_pair, behind_pair = to_partner(here), to_partner(behind)
+    )(kv, *came, bias)
+    x_line = (move(x, far_x), move(y, across_y), x)
+    y_line = (move(y, far_y), move(x, near_x), y)
+
     heads = width // HD
     work = heads * side * 3 * side
     half = shape((side, width), bf)
-    reach = (2, 3 * side, HD)
-
-    def attend(turn, grad_type, *line):
+
+    def attend(turn, *line):
         return pl.pallas_call(
             functools.partial(attend_kernel, turn),
-            in_specs=[VMEM] * 4,
-            out_specs=[VMEM] * 3,
+            in_specs=[VMEM] * 5,
+            out_specs=[VMEM] * 5,
             scratch_shapes=[pltpu.VMEM((HD, 3 * side), bf)] * 2
             + [pltpu.VMEM((HD, 3 * side), jnp.float32)] * 2,
-            out_shape=[half, shape((heads, side, 3 * side), bf), shape(reach, grad_type)],
+            out_shape=[
+                half,
+                shape((heads, side, 3 * side), bf),
+                block,
+                block,
+                shape((2, side, HD), jnp.float32),
+            ],
             compiler_params=pltpu.CompilerParams(vmem_limit_bytes=32 * 2**20),
             cost_estimate=pl.CostEstimate(
                 flops=10 * work * HD, bytes_accessed=6 * side * width, transcendentals=work
@@ -342,38 +355,36 @@
             name="attend",
         )(qg, *line, bias)
 
-    attn_pair, ds_pair, grad_pair = attend(0, bf, behind_pair, here_pair)
-    came_grad = to_partner(grad_pair)
-    attn_own, ds_own, grad_own = attend(1, jnp.float32, behind, here)
-    halo, own = pl.pallas_call(
-        merge_kernel,
-        out_shape=[shape((2, 2 * side, HD), bf), shape((2, 2 * side, HD), jnp.float32)],
-        in_specs=[VMEM] * 2,
-        out_specs=[VMEM] * 2,
-        compiler_params=SMALL,
-        name="merge",
-    )(grad_own, came_grad)
-    came_halo = along_line(halo, -1)
-    dq_pair, dq_own = pl.pallas_call(
+    attn_x, ds_x, to_far_x, to_across_y, own_x = attend(0, *x_line)
+    attn_y, ds_y, to_far_y, to_near_x, own_y = attend(1, *y_line)
+    terms = (
+        own_x,
+        move(to_far_x, far_x, back=True),
+        move(to_near_x, near_x, back=True),
+        own_y,
+        move(to_across_y, across_y, back=True),
+        move(to_far_y, far_y, back=True),
+    )
+    dq_x, dq_y = pl.pallas_call(
         query_kernel,
         out_shape=[half, half],
-        in_specs=[VMEM] * 6,
+        in_specs=[VMEM] * 8,
         out_specs=[VMEM] * 2,
         compiler_params=pltpu.CompilerParams(vmem_limit_bytes=16 * 2**20),
         cost_estimate=pl.CostEstimate(
             flops=4 * work * HD, bytes_accessed=4 * work, transcendentals=0
         ),
         name="query",
-    )(ds_pair, behind_pair, here_pair, ds_own, behind, here)
+    )(ds_x, *x_line, ds_y, *y_line)
 
     pieces = pl.pallas_call(
         functools.partial(total_kernel, groups),
         out_shape=[piece] * groups,
-        in_specs=[VMEM] * 2,
+        in_specs=[VMEM] * 6,
         out_specs=[VMEM] * groups,
         compiler_params=SMALL,
         name="total",
-    )(own, came_halo)
+    )(*terms)
     returned = [pieces[0]] + [around(block, step) for step, block in enumerate(pieces[1:], 1)]
     attn_out, q_grad, filled = pl.pallas_call(
         fill_kernel,
@@ -386,24 +397,15 @@
             flops=0, bytes_accessed=16 * side * width, transcendentals=0
         ),
         name="fill",
-    )(attn_pair, attn_own, dq_pair, dq_own, returned[1])
-    kept, for_pair = pl.pallas_call(
+    )(attn_x, attn_y, dq_x, dq_y, returned[1])
+    k_grad, v_grad = pl.pallas_call(
         functools.partial(place_kernel, groups),
-        out_shape=[shape((2, rows, keys.shape[3]), bf)] * 2,
+        out_shape=[shape(keys.shape, bf)] * 2,
         in_specs=[VMEM] * groups + [ANY],
         out_specs=[VMEM] * 2,
         compiler_params=SMALL,
         name="place",
     )(*returned, filled)
-    k_grad, v_grad = pl.pallas_call(
-        finish_kernel,
-        out_shape=[shape(keys.shape, bf)] * 2,
-        in_specs=[VMEM] * 2,
-        out_specs=[VMEM] * 2,
-        compiler_params=SMALL,
-        name="finish",
-    )(kept, to_partner(for_pair))
-
     return (attn_out, q_grad, k_grad, v_grad)
 
 

time: 102 us -> 101 us (level)
  the two profiles are of different devices: /device:TPU:63 before, /device:TPU:64 now
where the time goes in v4:
time: 101 us
  starting transfers between devices  66.3 us (66%)
  waiting for transfers between devices  16 us (16%)
  Pallas kernels  13.2 us (13%)
  local copies, waits for them, and re-layouts  3.12 us (3%)
    ppermute x6, starting transfers between devices, around(): return lax.ppermute(block, ('cp', 'tp'), route)  39.5 us
    ppermute x8, starting transfers between devices, move(): return lax.ppermute(block, 'cp', route)  26.8 us
    ppermute x8, waiting for transfers between devices, move(): return lax.ppermute(block, 'cp', route)  9.14 us
    pallas_call x2, Pallas kernels, attend(): pl.pallas_call(functools.partial(attend_kernel, turn), in_specs=[VMEM] *...  8.65 us
    ppermute x6, waiting for transfers between devices, around(): return lax.ppermute(block, ('cp', 'tp'), route)  6.89 us
    unnamed x6, local copies, waits for them, and re-layouts  3.12 us
  transfers between devices with their start and end apart: 14, of which 4 were waited for; matrix products, arithmetic and copies ran while one was open for 0% of the time, Pallas kernels for 12%

profile of v4, /device:TPU:64, one launch (start us, length us, event | category | flops | bytes accessed | tf_op | source)
XLA Modules:
  0.0 100.6 jit_solution(8543006234686169637)
XLA Ops:
  0.6 1.0 pad_maximum_fusion.kv_ref
  1.6 0.1 split.1
  1.7 9.1 %collective-permute-start = (bf16[2,2,64,128]{3,2,1,0:T(8,128)(2,1)S(1)}, bf16[2,2,64,128]{3,2,1,0:T(8,128)(2,1)S(1)}, u32[]{:S(2)}, u32[]{:S(2)}) collective-permute-start(bf16[2,2,64,128]{3,2,1,0:T(8,128)(2,1)S(1)} %get-tuple-element.33), channel_id=1, source_target_pairs={{0,1},{1,2},{2,3},{3,0},{4,7},{5,4},{6,5},{7,6},{8,9},{9,10},{10,1... | collective-permute-start | bytes 196616 | tf_op jit(solution)/shard_map/ppermute | solution.py:61
  10.8 9.1 %collective-permute-start.1 = (bf16[2,2,64,128]{3,2,1,0:T(8,128)(2,1)S(1)}, bf16[2,2,64,128]{3,2,1,0:T(8,128)(2,1)S(1)}, u32[]{:S(2)}, u32[]{:S(2)}) collective-permute-start(bf16[2,2,64,128]{3,2,1,0:T(8,128)(2,1)S(1)} %get-tuple-element.34), channel_id=1, source_target_pairs={{0,2},{1,3},{2,0},{3,1},{4,6},{5,7},{6,4},{7,5},{8,10},{9,11},{10,... | collective-permute-start | bytes 196616 | tf_op jit(solution)/shard_map/ppermute | solution.py:61
  19.9 5.5 %collective-permute-start.2 = (bf16[2,2,64,128]{3,2,1,0:T(8,128)(2,1)S(1)}, bf16[2,2,64,128]{3,2,1,0:T(8,128)(2,1)S(1)}, u32[]{:S(2)}, u32[]{:S(2)}) collective-permute-start(bf16[2,2,64,128]{3,2,1,0:T(8,128)(2,1)S(1)} %get-tuple-element.35), channel_id=1, source_target_pairs={{0,3},{1,0},{2,1},{3,2},{4,5},{5,6},{6,7},{7,4},{8,11},{9,8},{10,9... | collective-permute-start | bytes 196616 | tf_op jit(solution)/shard_map/ppermute | solution.py:61
  25.4 0.0 copy-start
  25.4 1.2 %copy-done = bf16[2,1,256,1024]{3,2,1,0:T(8,128)(2,1)S(1)} copy-done((bf16[2,1,256,1024]{3,2,1,0:T(8,128)(2,1)S(1)}, bf16[2,1,256,1024]{3,2,1,0:T(8,128)(2,1)}, u32[]{:S(2)}) %copy-start) | copy-done | bytes 1048600
  26.6 0.0 copy-start.1
  26.6 1.2 %copy-done.1 = bf16[2,1,256,1024]{3,2,1,0:T(8,128)(2,1)S(1)} copy-done((bf16[2,1,256,1024]{3,2,1,0:T(8,128)(2,1)S(1)}, bf16[2,1,256,1024]{3,2,1,0:T(8,128)(2,1)}, u32[]{:S(2)}) %copy-start.1) | copy-done | bytes 1048600
  27.8 0.0 copy-start.2
  27.8 0.7 copy-done.2
  28.5 0.5 prepare.1
  29.0 0.0 collective-permute-done.refs_0_
  29.0 0.0 collective-permute-done.1.refs_1_
  29.0 2.9 %collective-permute-done.2.refs_2_ = bf16[2,2,64,128]{3,2,1,0:T(8,128)(2,1)S(1)} collective-permute-done((bf16[2,2,64,128]{3,2,1,0:T(8,128)(2,1)S(1)}, bf16[2,2,64,128]{3,2,1,0:T(8,128)(2,1)S(1)}, u32[]{:S(2)}, u32[]{:S(2)}) %collective-permute-start.2) | collective-permute-done | bytes 65568 | tf_op jit(solution)/shard_map/ppermute | solution.py:61
  32.0 3.1 %collective-permute-start.3 = (bf16[2,256,128]{2,1,0:T(8,128)(2,1)S(1)}, bf16[2,256,128]{2,1,0:T(8,128)(2,1)S(1)}, u32[]{:S(2)}, u32[]{:S(2)}) collective-permute-start(bf16[2,256,128]{2,1,0:T(8,128)(2,1)S(1)} %get-tuple-element.37.here_ref.refs_3_), channel_id=1, source_target_pairs={{0,8},{8,16},{12,4},{16,24},{20,12},{24,32},{28,20},{32,40},{36,28... | collective-permute-start | bytes 393224 | tf_op jit(solution)/shard_map/ppermute | solution.py:48
  35.1 5.2 %collective-permute-start.4 = (bf16[2,256,128]{2,1,0:T(8,128)(2,1)S(1)}, bf16[2,256,128]{2,1,0:T(8,128)(2,1)S(1)}, u32[]{:S(2)}, u32[]{:S(2)}) collective-permute-start(bf16[2,256,128]{2,1,0:T(8,128)(2,1)S(1)} %get-tuple-element.38.here_ref.refs_7_), channel_id=1, source_target_pairs={{4,8},{8,4},{12,16},{16,12},{20,24},{24,20},{28,32},{32,28},{36,40... | collective-permute-start | bytes 393224 | tf_op jit(solution)/shard_map/ppermute | solution.py:48
  40.4 1.9 %collective-permute-start.6 = (bf16[2,256,128]{2,1,0:T(8,128)(2,1)S(1)}, bf16[2,256,128]{2,1,0:T(8,128)(2,1)S(1)}, u32[]{:S(2)}, u32[]{:S(2)}) collective-permute-start(bf16[2,256,128]{2,1,0:T(8,128)(2,1)S(1)} %get-tuple-element.37.here_ref.refs_3_), channel_id=1, source_target_pairs={{0,4},{4,0},{8,12},{12,8},{16,20},{20,16},{24,28},{28,24},{32,36},... | collective-permute-start | bytes 393224 | tf_op jit(solution)/shard_map/ppermute | solution.py:48
  42.3 4.9 %collective-permute-start.5 = (bf16[2,256,128]{2,1,0:T(8,128)(2,1)S(1)}, bf16[2,256,128]{2,1,0:T(8,128)(2,1)S(1)}, u32[]{:S(2)}, u32[]{:S(2)}) collective-permute-start(bf16[2,256,128]{2,1,0:T(8,128)(2,1)S(1)} %get-tuple-element.38.here_ref.refs_7_), channel_id=1, source_target_pairs={{4,12},{8,0},{12,20},{16,8},{20,28},{24,16},{28,36},{32,24},{36,44... | collective-permute-start | bytes 393224 | tf_op jit(solution)/shard_map/ppermute | solution.py:48
  47.3 0.0 collective-permute-done.3.oldest_ref.refs_1_
  47.3 0.0 collective-permute-done.4.middle_ref.refs_2_
  47.3 4.3 %attend.2 = (bf16[256,1024]{1,0:T(8,128)(2,1)S(1)}, bf16[8,256,768]{2,1,0:T(8,128)(2,1)S(1)}, bf16[2,256,128]{2,1,0:T(8,128)(2,1)S(1)}, bf16[2,256,128]{2,1,0:T(8,128)(2,1)S(1)}, f32[2,256,128]{2,1,0:T(8,128)S(1)}) custom-call(bf16[2,2,256,1024]{3,2,1,0:T(8,128)(2,1)S(1)} %get-tuple-element.32.qg_ref, ...), custom_call_target="tpu_custom_call" | custom-call | flops 2013265920 | bytes 1572864 | tf_op jit(solution)/shard_map/attend/pallas_call | solution.py:338
  51.6 2.7 %collective-permute-start.7 = (bf16[2,256,128]{2,1,0:T(8,128)(2,1)S(1)}, bf16[2,256,128]{2,1,0:T(8,128)(2,1)S(1)}, u32[]{:S(2)}, u32[]{:S(2)}) collective-permute-start(bf16[2,256,128]{2,1,0:T(8,128)(2,1)S(1)} %get-tuple-element.46), channel_id=1, source_target_pairs={{8,0},{16,8},{4,12},{24,16},{12,20},{32,24},{20,28},{40,32},{28,36... | collective-permute-start | bytes 393224 | tf_op jit(solution)/shard_map/ppermute | solution.py:48
  54.3 5.1 %collective-permute-start.9 = (bf16[2,256,128]{2,1,0:T(8,128)(2,1)S(1)}, bf16[2,256,128]{2,1,0:T(8,128)(2,1)S(1)}, u32[]{:S(2)}, u32[]{:S(2)}) collective-permute-start(bf16[2,256,128]{2,1,0:T(8,128)(2,1)S(1)} %get-tuple-element.49), channel_id=1, source_target_pairs={{8,4},{4,8},{16,12},{12,16},{24,20},{20,24},{32,28},{28,32},{40,36... | collective-permute-start | bytes 393224 | tf_op jit(solution)/shard_map/ppermute | solution.py:48
  59.4 0.0 collective-permute-done.6.middle_ref.refs_6_
  59.4 0.0 collective-permute-done.5.oldest_ref.refs_5_
  59.4 4.3 %attend.3 = (bf16[256,1024]{1,0:T(8,128)(2,1)S(1)}, bf16[8,256,768]{2,1,0:T(8,128)(2,1)S(1)}, bf16[2,256,128]{2,1,0:T(8,128)(2,1)S(1)}, bf16[2,256,128]{2,1,0:T(8,128)(2,1)S(1)}, f32[2,256,128]{2,1,0:T(8,128)S(1)}) custom-call(bf16[2,2,256,1024]{3,2,1,0:T(8,128)(2,1)S(1)} %get-tuple-element.32.qg_ref, ...), custom_call_target="tpu_custom_call" | custom-call | flops 2013265920 | bytes 1572864 | tf_op jit(solution)/shard_map/attend/pallas_call | solution.py:338
  63.8 1.9 %collective-permute-start.8 = (bf16[2,256,128]{2,1,0:T(8,128)(2,1)S(1)}, bf16[2,256,128]{2,1,0:T(8,128)(2,1)S(1)}, u32[]{:S(2)}, u32[]{:S(2)}) collective-permute-start(bf16[2,256,128]{2,1,0:T(8,128)(2,1)S(1)} %get-tuple-element.47), channel_id=1, source_target_pairs={{4,0},{0,4},{12,8},{8,12},{20,16},{16,20},{28,24},{24,28},{36,32},... | collective-permute-start | bytes 393224 | tf_op jit(solution)/shard_map/ppermute | solution.py:48
  65.7 1.9 %collective-permute-start.10 = (bf16[2,256,128]{2,1,0:T(8,128)(2,1)S(1)}, bf16[2,256,128]{2,1,0:T(8,128)(2,1)S(1)}, u32[]{:S(2)}, u32[]{:S(2)}) collective-permute-start(bf16[2,256,128]{2,1,0:T(8,128)(2,1)S(1)} %get-tuple-element.50), channel_id=1, source_target_pairs={{12,4},{0,8},{20,12},{8,16},{28,20},{16,24},{36,28},{24,32},{44,36... | collective-permute-start | bytes 393224 | tf_op jit(solution)/shard_map/ppermute | solution.py:48
  67.6 0.0 collective-permute-done.7.refs_1_
  67.6 0.0 collective-permute-done.9.refs_4_
  67.6 0.0 collective-permute-done.8.refs_2_
  67.6 9.1 %collective-permute-done.10.refs_5_ = bf16[2,256,128]{2,1,0:T(8,128)(2,1)S(1)} collective-permute-done((bf16[2,256,128]{2,1,0:T(8,128)(2,1)S(1)}, bf16[2,256,128]{2,1,0:T(8,128)(2,1)S(1)}, u32[]{:S(2)}, u32[]{:S(2)}) %collective-permute-start.10) | collective-permute-done | bytes 131104 | tf_op jit(solution)/shard_map/ppermute | solution.py:48
  76.8 0.1 total.1
  76.8 6.5 %collective-permute-start.11 = (bf16[2,2,64,128]{3,2,1,0:T(8,128)(2,1)S(1)}, bf16[2,2,64,128]{3,2,1,0:T(8,128)(2,1)S(1)}, u32[]{:S(2)}, u32[]{:S(2)}) collective-permute-start(bf16[2,2,64,128]{3,2,1,0:T(8,128)(2,1)S(1)} %get-tuple-element.51), channel_id=1, source_target_pairs={{0,1},{1,2},{2,3},{3,0},{4,7},{5,4},{6,5},{7,6},{8,9},{9,10},{10,1... | collective-permute-start | bytes 196616 | tf_op jit(solution)/shard_map/ppermute | solution.py:61
  83.3 5.1 %collective-permute-start.12 = (bf16[2,2,64,128]{3,2,1,0:T(8,128)(2,1)S(1)}, bf16[2,2,64,128]{3,2,1,0:T(8,128)(2,1)S(1)}, u32[]{:S(2)}, u32[]{:S(2)}) collective-permute-start(bf16[2,2,64,128]{3,2,1,0:T(8,128)(2,1)S(1)} %get-tuple-element.55), channel_id=1, source_target_pairs={{0,2},{1,3},{2,0},{3,1},{4,6},{5,7},{6,4},{7,5},{8,10},{9,11},{10,... | collective-permute-start | bytes 196616 | tf_op jit(solution)/shard_map/ppermute | solution.py:61
  88.4 4.3 %collective-permute-start.13 = (bf16[2,2,64,128]{3,2,1,0:T(8,128)(2,1)S(1)}, bf16[2,2,64,128]{3,2,1,0:T(8,128)(2,1)S(1)}, u32[]{:S(2)}, u32[]{:S(2)}) collective-permute-start(bf16[2,2,64,128]{3,2,1,0:T(8,128)(2,1)S(1)} %get-tuple-element.56), channel_id=1, source_target_pairs={{0,3},{1,0},{2,1},{3,2},{4,5},{5,6},{6,7},{7,4},{8,11},{9,8},{10,9... | collective-permute-start | bytes 196616 | tf_op jit(solution)/shard_map/ppermute | solution.py:61
  92.7 1.8 %query.1 = (bf16[256,1024]{1,0:T(8,128)(2,1)S(1)}, bf16[256,1024]{1,0:T(8,128)(2,1)S(1)}) custom-call(bf16[8,256,768]{2,1,0:T(8,128)(2,1)S(1)} %get-tuple-element.41.refs_0_, bf16[2,256,128]{2,1,0:T(8,128)(2,1)S(1)} %collective-permute-done.3.oldest_ref.refs_1_, bf16[2,256,128]{2,1,0:T(8,128)(2,1)S(1)} %collective-permute-done.4.middle_ref.refs_2_, ...), custom_call_target="tpu_custom_call" | custom-call | flops 805306368 | bytes 6291456 | tf_op jit(solution)/shard_map/query/pallas_call | solution.py:368
  94.5 0.0 collective-permute-done.11.refs_4_.refs_1_
  94.5 1.4 %fill.1 = (bf16[2,1,256,1024]{3,2,1,0:T(8,128)(2,1)}, bf16[2,1,256,1024]{3,2,1,0:T(8,128)(2,1)}, f32[8,128]{1,0:T(8,128)S(1)}) custom-call(bf16[256,1024]{1,0:T(8,128)(2,1)S(1)} %get-tuple-element.39.refs_0_, bf16[256,1024]{1,0:T(8,128)(2,1)S(1)} %get-tuple-element.40.refs_1_, bf16[256,1024]{1,0:T(8,128)(2,1)S(1)} %get-tuple-element.43.refs_2_, ...), custom_call_target="tpu_custom_call" | custom-call | bytes 4194304 | tf_op jit(solution)/shard_map/fill/pallas_call | solution.py:389
  95.9 3.3 %collective-permute-done.12.refs_2_ = bf16[2,2,64,128]{3,2,1,0:T(8,128)(2,1)S(1)} collective-permute-done((bf16[2,2,64,128]{3,2,1,0:T(8,128)(2,1)S(1)}, bf16[2,2,64,128]{3,2,1,0:T(8,128)(2,1)S(1)}, u32[]{:S(2)}, u32[]{:S(2)}) %collective-permute-start.12) | collective-permute-done | bytes 65568 | tf_op jit(solution)/shard_map/ppermute | solution.py:61
  99.2 0.6 collective-permute-done.13.refs_3_
  99.8 0.8 place.1
  (1 shorter events, 0.0 us)
Async XLA Ops:
  1.7 27.3 %collective-permute-start = (bf16[2,2,64,128]{3,2,1,0:T(8,128)(2,1)S(1)}, bf16[2,2,64,128]{3,2,1,0:T(8,128)(2,1)S(1)}, u32[]{:S(2)}, u32[]{:S(2)}) collective-permute-start(bf16[2,2,64,128]{3,2,1,0:T(8,128)(2,1)S(1)} %get-tuple-element.33), channel_id=1, source_target_pairs={{0,1},{1,2},{2,3},{3,0},{4,7},{5,4},{6,5},{7,6},{8,9},{9,10},{10,1... | collective-permute-start | bytes 196616 | tf_op jit(solution)/shard_map/ppermute | solution.py:61
  10.8 18.2 %collective-permute-start.1 = (bf16[2,2,64,128]{3,2,1,0:T(8,128)(2,1)S(1)}, bf16[2,2,64,128]{3,2,1,0:T(8,128)(2,1)S(1)}, u32[]{:S(2)}, u32[]{:S(2)}) collective-permute-start(bf16[2,2,64,128]{3,2,1,0:T(8,128)(2,1)S(1)} %get-tuple-element.34), channel_id=1, source_target_pairs={{0,2},{1,3},{2,0},{3,1},{4,6},{5,7},{6,4},{7,5},{8,10},{9,11},{10,... | collective-permute-start | bytes 196616 | tf_op jit(solution)/shard_map/ppermute | solution.py:61
  19.9 12.1 %collective-permute-start.2 = (bf16[2,2,64,128]{3,2,1,0:T(8,128)(2,1)S(1)}, bf16[2,2,64,128]{3,2,1,0:T(8,128)(2,1)S(1)}, u32[]{:S(2)}, u32[]{:S(2)}) collective-permute-start(bf16[2,2,64,128]{3,2,1,0:T(8,128)(2,1)S(1)} %get-tuple-element.35), channel_id=1, source_target_pairs={{0,3},{1,0},{2,1},{3,2},{4,5},{5,6},{6,7},{7,4},{8,11},{9,8},{10,9... | collective-permute-start | bytes 196616 | tf_op jit(solution)/shard_map/ppermute | solution.py:61
  25.4 1.2 %copy-start = (bf16[2,1,256,1024]{3,2,1,0:T(8,128)(2,1)S(1)}, bf16[2,1,256,1024]{3,2,1,0:T(8,128)(2,1)}, u32[]{:S(2)}) copy-start(bf16[2,1,256,1024]{3,2,1,0:T(8,128)(2,1)} %q_ref.1) | copy-start | bytes 3145732
  26.6 1.2 %copy-start.1 = (bf16[2,1,256,1024]{3,2,1,0:T(8,128)(2,1)S(1)}, bf16[2,1,256,1024]{3,2,1,0:T(8,128)(2,1)}, u32[]{:S(2)}) copy-start(bf16[2,1,256,1024]{3,2,1,0:T(8,128)(2,1)} %g_ref.1) | copy-start | bytes 3145732
  27.8 0.7 copy-start.2
  32.0 15.2 %collective-permute-start.3 = (bf16[2,256,128]{2,1,0:T(8,128)(2,1)S(1)}, bf16[2,256,128]{2,1,0:T(8,128)(2,1)S(1)}, u32[]{:S(2)}, u32[]{:S(2)}) collective-permute-start(bf16[2,256,128]{2,1,0:T(8,128)(2,1)S(1)} %get-tuple-element.37.here_ref.refs_3_), channel_id=1, source_target_pairs={{0,8},{8,16},{12,4},{16,24},{20,12},{24,32},{28,20},{32,40},{36,28... | collective-permute-start | bytes 393224 | tf_op jit(solution)/shard_map/ppermute | solution.py:48
  35.1 12.1 %collective-permute-start.4 = (bf16[2,256,128]{2,1,0:T(8,128)(2,1)S(1)}, bf16[2,256,128]{2,1,0:T(8,128)(2,1)S(1)}, u32[]{:S(2)}, u32[]{:S(2)}) collective-permute-start(bf16[2,256,128]{2,1,0:T(8,128)(2,1)S(1)} %get-tuple-element.38.here_ref.refs_7_), channel_id=1, source_target_pairs={{4,8},{8,4},{12,16},{16,12},{20,24},{24,20},{28,32},{32,28},{36,40... | collective-permute-start | bytes 393224 | tf_op jit(solution)/shard_map/ppermute | solution.py:48
  40.4 19.0 %collective-permute-start.6 = (bf16[2,256,128]{2,1,0:T(8,128)(2,1)S(1)}, bf16[2,256,128]{2,1,0:T(8,128)(2,1)S(1)}, u32[]{:S(2)}, u32[]{:S(2)}) collective-permute-start(bf16[2,256,128]{2,1,0:T(8,128)(2,1)S(1)} %get-tuple-element.37.here_ref.refs_3_), channel_id=1, source_target_pairs={{0,4},{4,0},{8,12},{12,8},{16,20},{20,16},{24,28},{28,24},{32,36},... | collective-permute-start | bytes 393224 | tf_op jit(solution)/shard_map/ppermute | solution.py:48
  42.3 17.1 %collective-permute-start.5 = (bf16[2,256,128]{2,1,0:T(8,128)(2,1)S(1)}, bf16[2,256,128]{2,1,0:T(8,128)(2,1)S(1)}, u32[]{:S(2)}, u32[]{:S(2)}) collective-permute-start(bf16[2,256,128]{2,1,0:T(8,128)(2,1)S(1)} %get-tuple-element.38.here_ref.refs_7_), channel_id=1, source_target_pairs={{4,12},{8,0},{12,20},{16,8},{20,28},{24,16},{28,36},{32,24},{36,44... | collective-permute-start | bytes 393224 | tf_op jit(solution)/shard_map/ppermute | solution.py:48
  51.6 16.0 %collective-permute-start.7 = (bf16[2,256,128]{2,1,0:T(8,128)(2,1)S(1)}, bf16[2,256,128]{2,1,0:T(8,128)(2,1)S(1)}, u32[]{:S(2)}, u32[]{:S(2)}) collective-permute-start(bf16[2,256,128]{2,1,0:T(8,128)(2,1)S(1)} %get-tuple-element.46), channel_id=1, source_target_pairs={{8,0},{16,8},{4,12},{24,16},{12,20},{32,24},{20,28},{40,32},{28,36... | collective-permute-start | bytes 393224 | tf_op jit(solution)/shard_map/ppermute | solution.py:48
  54.3 13.3 %collective-permute-start.9 = (bf16[2,256,128]{2,1,0:T(8,128)(2,1)S(1)}, bf16[2,256,128]{2,1,0:T(8,128)(2,1)S(1)}, u32[]{:S(2)}, u32[]{:S(2)}) collective-permute-start(bf16[2,256,128]{2,1,0:T(8,128)(2,1)S(1)} %get-tuple-element.49), channel_id=1, source_target_pairs={{8,4},{4,8},{16,12},{12,16},{24,20},{20,24},{32,28},{28,32},{40,36... | collective-permute-start | bytes 393224 | tf_op jit(solution)/shard_map/ppermute | solution.py:48
  63.8 3.9 %collective-permute-start.8 = (bf16[2,256,128]{2,1,0:T(8,128)(2,1)S(1)}, bf16[2,256,128]{2,1,0:T(8,128)(2,1)S(1)}, u32[]{:S(2)}, u32[]{:S(2)}) collective-permute-start(bf16[2,256,128]{2,1,0:T(8,128)(2,1)S(1)} %get-tuple-element.47), channel_id=1, source_target_pairs={{4,0},{0,4},{12,8},{8,12},{20,16},{16,20},{28,24},{24,28},{36,32},... | collective-permute-start | bytes 393224 | tf_op jit(solution)/shard_map/ppermute | solution.py:48
  65.7 11.1 %collective-permute-start.10 = (bf16[2,256,128]{2,1,0:T(8,128)(2,1)S(1)}, bf16[2,256,128]{2,1,0:T(8,128)(2,1)S(1)}, u32[]{:S(2)}, u32[]{:S(2)}) collective-permute-start(bf16[2,256,128]{2,1,0:T(8,128)(2,1)S(1)} %get-tuple-element.50), channel_id=1, source_target_pairs={{12,4},{0,8},{20,12},{8,16},{28,20},{16,24},{36,28},{24,32},{44,36... | collective-permute-start | bytes 393224 | tf_op jit(solution)/shard_map/ppermute | solution.py:48
  76.8 17.7 %collective-permute-start.11 = (bf16[2,2,64,128]{3,2,1,0:T(8,128)(2,1)S(1)}, bf16[2,2,64,128]{3,2,1,0:T(8,128)(2,1)S(1)}, u32[]{:S(2)}, u32[]{:S(2)}) collective-permute-start(bf16[2,2,64,128]{3,2,1,0:T(8,128)(2,1)S(1)} %get-tuple-element.51), channel_id=1, source_target_pairs={{0,1},{1,2},{2,3},{3,0},{4,7},{5,4},{6,5},{7,6},{8,9},{9,10},{10,1... | collective-permute-start | bytes 196616 | tf_op jit(solution)/shard_map/ppermute | solution.py:61
  83.3 15.9 %collective-permute-start.12 = (bf16[2,2,64,128]{3,2,1,0:T(8,128)(2,1)S(1)}, bf16[2,2,64,128]{3,2,1,0:T(8,128)(2,1)S(1)}, u32[]{:S(2)}, u32[]{:S(2)}) collective-permute-start(bf16[2,2,64,128]{3,2,1,0:T(8,128)(2,1)S(1)} %get-tuple-element.55), channel_id=1, source_target_pairs={{0,2},{1,3},{2,0},{3,1},{4,6},{5,7},{6,4},{7,5},{8,10},{9,11},{10,... | collective-permute-start | bytes 196616 | tf_op jit(solution)/shard_map/ppermute | solution.py:61
  88.4 11.4 %collective-permute-start.13 = (bf16[2,2,64,128]{3,2,1,0:T(8,128)(2,1)S(1)}, bf16[2,2,64,128]{3,2,1,0:T(8,128)(2,1)S(1)}, u32[]{:S(2)}, u32[]{:S(2)}) collective-permute-start(bf16[2,2,64,128]{3,2,1,0:T(8,128)(2,1)S(1)} %get-tuple-element.56), channel_id=1, source_target_pairs={{0,3},{1,0},{2,1},{3,2},{4,5},{5,6},{6,7},{7,4},{8,11},{9,8},{10,9... | collective-permute-start | bytes 196616 | tf_op jit(solution)/shard_map/ppermute | solution.py:61

commit v5 on v4

--- a/solution.py
+++ b/solution.py
@@ -24,19 +24,13 @@
     return i + 2 if i + 2 < contexts else i + 1
 
 
-def across_y(i, contexts):
-    if i % 2:
-        return min(i + 1, contexts - 1)
-    return i - 1
-
-
 def far_y(i, contexts):
     if i % 2:
         return i + 2 if i + 2 < contexts else i - 1
     return i - 2
 
 
-def near_x(i, contexts):
+def partner(i, contexts):
     return i ^ 1
 
 
@@ -91,14 +85,19 @@
             out[:, aligned(source, rows), :] = piece[block]
 
 
+def both_kernel(x_ref, came_ref, after_ref, out_ref):
+    out_ref[0] = x_ref[...]
+    out_ref[1] = came_ref[...]
+
+
 def total_kernel(groups, *refs):
-    terms, pieces = refs[:6], refs[6:]
+    terms, pieces = (refs[:3], refs[3:5]), refs[5:]
     tp, core = lax.axis_index("tp"), lax.rem(lax.axis_index("cp"), 2)
     rows = pieces[0].shape[2]
     for step, piece in enumerate(pieces):
         place = aligned(lax.rem(tp + offset(step, core, groups), groups), rows)
         for block in range(2):
-            own, *came = [ref[:, place, :] for ref in terms[3 * block : 3 * block + 3]]
+            own, *came = [ref[:, place, :] for ref in terms[block]]
             for term in came:
                 own = own + term.astype(jnp.float32)
             piece[block] = own.astype(piece.dtype)
@@ -207,30 +206,22 @@
     return jnp.concatenate([old, field[:, side:].astype(bf), own], axis=1)
 
 
-def attend_kernel(
-    turn,
-    qg_ref,
-    oldest_ref,
-    middle_ref,
-    here_ref,
-    bias_ref,
-    attn_ref,
-    ds_ref,
-    to_oldest_ref,
-    to_middle_ref,
-    own_ref,
-    kt_ref,
-    vt_ref,
-    dk_ref,
-    dv_ref,
-):
+def window(turn, kind, oldest_ref, shared_ref, here_ref):
+    return jnp.concatenate(
+        [oldest_ref[kind], shared_ref[1 - turn, kind], here_ref[kind]], axis=0
+    )
+
+
+def attend_kernel(turn, qg_ref, oldest_ref, shared_ref, here_ref, bias_ref, *refs):
+    if turn == 0:
+        more_ref = None
+    else:
+        more_ref, *refs = refs
+    attn_ref, ds_ref, to_oldest_ref, to_middle_ref, own_ref, kt_ref, vt_ref, dk_ref, dv_ref = refs
     side, heads = attn_ref.shape[0], ds_ref.shape[0]
     bf = jnp.bfloat16
     over, down = ((1,), (0,)), ((0,), (0,))
-    keys, values = [
-        jnp.concatenate([oldest_ref[kind], middle_ref[kind], here_ref[kind]], axis=0)
-        for kind in range(2)
-    ]
+    keys, values = [window(turn, kind, oldest_ref, shared_ref, here_ref) for kind in range(2)]
     kt_ref[...] = keys.T
     vt_ref[...] = values.T
 
@@ -274,15 +265,17 @@
     for kind, (ref, factor) in enumerate(((dk_ref, FACTOR), (dv_ref, 1.0))):
         for n, out in enumerate((to_oldest_ref, to_middle_ref, own_ref)):
             term = ref[:, n * side : (n + 1) * side].T * factor
+            if n == 0 and more_ref is not None:
+                term = term + more_ref[kind].astype(jnp.float32)
             out[kind] = term.astype(out.dtype)
 
 
 def query_kernel(*refs):
     inputs, outs = refs[:-2], refs[-2:]
     for turn, out in enumerate(outs):
-        ds_ref, *blocks = inputs[4 * turn : 4 * turn + 4]
+        ds_ref, *line = inputs[4 * turn : 4 * turn + 4]
         heads = ds_ref.shape[0]
-        keys = jnp.concatenate([ref[0] for ref in blocks], axis=0)
+        keys = window(turn, 0, *line)
         for head in range(heads):
             dq = dot(ds_ref[head], keys, ((1,), (0,))) * FACTOR
             out[:, head * HD : (head + 1) * HD] = dq.astype(out.dtype)
@@ -327,17 +320,27 @@
         compiler_params=SMALL,
         name="join",
     )(kv, *came, bias)
-    x_line = (move(x, far_x), move(y, across_y), x)
-    y_line = (move(y, far_y), move(x, near_x), y)
+    came_y, came_x = move(y, far_y), move(x, far_x)
+    both = pl.pallas_call(
+        both_kernel,
+        out_shape=shape((2, 2, side, HD), bf),
+        in_specs=[VMEM, VMEM, ANY],
+        out_specs=VMEM,
+        compiler_params=SMALL,
+        name="both",
+    )(x, came_y, came_x)
+    shared = move(both, partner)
+    x_line = (came_x, shared, x)
+    y_line = (came_y, shared, y)
 
     heads = width // HD
     work = heads * side * 3 * side
     half = shape((side, width), bf)
 
-    def attend(turn, *line):
+    def attend(turn, line, *more):
         return pl.pallas_call(
             functools.partial(attend_kernel, turn),
-            in_specs=[VMEM] * 5,
+            in_specs=[VMEM] * (5 + len(more)),
             out_specs=[VMEM] * 5,
             scratch_shapes=[pltpu.VMEM((HD, 3 * side), bf)] * 2
             + [pltpu.VMEM((HD, 3 * side), jnp.float32)] * 2,
@@ -353,17 +356,15 @@
                 flops=10 * work * HD, bytes_accessed=6 * side * width, transcendentals=work
             ),
             name="attend",
-        )(qg, *line, bias)
-
-    attn_x, ds_x, to_far_x, to_across_y, own_x = attend(0, *x_line)
-    attn_y, ds_y, to_far_y, to_near_x, own_y = attend(1, *y_line)
+        )(qg, *line, bias, *more)
+
+    attn_x, ds_x, for_far_x, for_partner, own_x = attend(0, x_line)
+    more = move(for_partner, partner, back=True)
+    from_far_x = move(for_far_x, far_x, back=True)
+    attn_y, ds_y, for_far_y, for_partner, own_y = attend(1, y_line, more)
     terms = (
-        own_x,
-        move(to_far_x, far_x, back=True),
-        move(to_near_x, near_x, back=True),
-        own_y,
-        move(to_across_y, across_y, back=True),
-        move(to_far_y, far_y, back=True),
+        (own_x, from_far_x, move(for_partner, partner, back=True)),
+        (own_y, move(for_far_y, far_y, back=True)),
     )
     dq_x, dq_y = pl.pallas_call(
         query_kernel,
@@ -380,11 +381,11 @@
     pieces = pl.pallas_call(
         functools.partial(total_kernel, groups),
         out_shape=[piece] * groups,
-        in_specs=[VMEM] * 6,
+        in_specs=[VMEM] * 5,
         out_specs=[VMEM] * groups,
         compiler_params=SMALL,
         name="total",
-    )(*terms)
+    )(*terms[0], *terms[1])
     returned = [pieces[0]] + [around(block, step) for step, block in enumerate(pieces[1:], 1)]
     attn_out, q_grad, filled = pl.pallas_call(
         fill_kernel,

time: 101 us -> 105 us (1.040)
  the two profiles are of different devices: /device:TPU:64 before, /device:TPU:96 now
where the time goes in v5:
time: 105 us
  starting transfers between devices  60.5 us (58%)
  waiting for transfers between devices  25.9 us (25%)
  Pallas kernels  13.2 us (13%)
  local copies, waits for them, and re-layouts  3.12 us (3%)
    ppermute x6, starting transfers between devices, around(): return lax.ppermute(block, ('cp', 'tp'), route)  38.8 us
    ppermute x7, starting transfers between devices, move(): return lax.ppermute(block, 'cp', route)  21.6 us
    ppermute x7, waiting for transfers between devices, move(): return lax.ppermute(block, 'cp', route)  18.2 us
    pallas_call x2, Pallas kernels, attend(): pl.pallas_call(functools.partial(attend_kernel, turn), in_specs=[VMEM] *...  8.64 us
    ppermute x6, waiting for transfers between devices, around(): return lax.ppermute(block, ('cp', 'tp'), route)  7.77 us
    unnamed x6, local copies, waits for them, and re-layouts  3.12 us
  transfers between devices with their start and end apart: 13, of which 7 were waited for; matrix products, arithmetic and copies ran while one was open for 0% of the time, Pallas kernels for 8%

profile of v5, /device:TPU:96, one launch (start us, length us, event | category | flops | bytes accessed | tf_op | source)
XLA Modules:
  0.0 104.6 jit_solution(7622535655111861797)
XLA Ops:
  0.6 1.0 pad_maximum_fusion.kv_ref
  1.6 0.1 split.1
  1.7 9.1 %collective-permute-start = (bf16[2,2,64,128]{3,2,1,0:T(8,128)(2,1)S(1)}, bf16[2,2,64,128]{3,2,1,0:T(8,128)(2,1)S(1)}, u32[]{:S(2)}, u32[]{:S(2)}) collective-permute-start(bf16[2,2,64,128]{3,2,1,0:T(8,128)(2,1)S(1)} %get-tuple-element.33), channel_id=1, source_target_pairs={{0,1},{1,2},{2,3},{3,0},{4,7},{5,4},{6,5},{7,6},{8,9},{9,10},{10,1... | collective-permute-start | bytes 196616 | tf_op jit(solution)/shard_map/ppermute | solution.py:55
  10.8 8.2 %collective-permute-start.1 = (bf16[2,2,64,128]{3,2,1,0:T(8,128)(2,1)S(1)}, bf16[2,2,64,128]{3,2,1,0:T(8,128)(2,1)S(1)}, u32[]{:S(2)}, u32[]{:S(2)}) collective-permute-start(bf16[2,2,64,128]{3,2,1,0:T(8,128)(2,1)S(1)} %get-tuple-element.34), channel_id=1, source_target_pairs={{0,2},{1,3},{2,0},{3,1},{4,6},{5,7},{6,4},{7,5},{8,10},{9,11},{10,... | collective-permute-start | bytes 196616 | tf_op jit(solution)/shard_map/ppermute | solution.py:55
  19.0 5.5 %collective-permute-start.2 = (bf16[2,2,64,128]{3,2,1,0:T(8,128)(2,1)S(1)}, bf16[2,2,64,128]{3,2,1,0:T(8,128)(2,1)S(1)}, u32[]{:S(2)}, u32[]{:S(2)}) collective-permute-start(bf16[2,2,64,128]{3,2,1,0:T(8,128)(2,1)S(1)} %get-tuple-element.35), channel_id=1, source_target_pairs={{0,3},{1,0},{2,1},{3,2},{4,5},{5,6},{6,7},{7,4},{8,11},{9,8},{10,9... | collective-permute-start | bytes 196616 | tf_op jit(solution)/shard_map/ppermute | solution.py:55
  24.5 0.0 copy-start
  24.5 1.2 %copy-done = bf16[2,1,256,1024]{3,2,1,0:T(8,128)(2,1)S(1)} copy-done((bf16[2,1,256,1024]{3,2,1,0:T(8,128)(2,1)S(1)}, bf16[2,1,256,1024]{3,2,1,0:T(8,128)(2,1)}, u32[]{:S(2)}) %copy-start) | copy-done | bytes 1048600
  25.7 0.0 copy-start.1
  25.7 1.2 %copy-done.1 = bf16[2,1,256,1024]{3,2,1,0:T(8,128)(2,1)S(1)} copy-done((bf16[2,1,256,1024]{3,2,1,0:T(8,128)(2,1)S(1)}, bf16[2,1,256,1024]{3,2,1,0:T(8,128)(2,1)}, u32[]{:S(2)}) %copy-start.1) | copy-done | bytes 1048600
  26.9 0.0 copy-start.2
  26.9 0.7 copy-done.2
  27.6 0.5 prepare.1
  28.1 0.0 collective-permute-done.refs_0_
  28.1 0.0 collective-permute-done.1.refs_1_
  28.1 2.2 %collective-permute-done.2.refs_2_ = bf16[2,2,64,128]{3,2,1,0:T(8,128)(2,1)S(1)} collective-permute-done((bf16[2,2,64,128]{3,2,1,0:T(8,128)(2,1)S(1)}, bf16[2,2,64,128]{3,2,1,0:T(8,128)(2,1)S(1)}, u32[]{:S(2)}, u32[]{:S(2)}) %collective-permute-start.2) | collective-permute-done | bytes 65568 | tf_op jit(solution)/shard_map/ppermute | solution.py:55
  30.4 8.0 %collective-permute-start.4 = (bf16[2,256,128]{2,1,0:T(8,128)(2,1)S(1)}, bf16[2,256,128]{2,1,0:T(8,128)(2,1)S(1)}, u32[]{:S(2)}, u32[]{:S(2)}) collective-permute-start(bf16[2,256,128]{2,1,0:T(8,128)(2,1)S(1)} %get-tuple-element.38.here_ref.refs_7_), channel_id=1, source_target_pairs={{4,12},{8,0},{12,20},{16,8},{20,28},{24,16},{28,36},{32,24},{36,44... | collective-permute-start | bytes 393224 | tf_op jit(solution)/shard_map/ppermute | solution.py:42
  38.4 1.9 %collective-permute-start.3 = (bf16[2,256,128]{2,1,0:T(8,128)(2,1)S(1)}, bf16[2,256,128]{2,1,0:T(8,128)(2,1)S(1)}, u32[]{:S(2)}, u32[]{:S(2)}) collective-permute-start(bf16[2,256,128]{2,1,0:T(8,128)(2,1)S(1)} %get-tuple-element.37.x_ref.here_ref.refs_3_), channel_id=1, source_target_pairs={{0,8},{8,16},{12,4},{16,24},{20,12},{24,32},{28,20},{32,40},{36,28... | collective-permute-start | bytes 393224 | tf_op jit(solution)/shard_map/ppermute | solution.py:42
  40.3 0.8 collective-permute-done.4.came_ref.oldest_ref.refs_5_
  41.1 8.4 %collective-permute-done.3.after_ref.oldest_ref.refs_1_ = bf16[2,256,128]{2,1,0:T(8,128)(2,1)S(1)} collective-permute-done((bf16[2,256,128]{2,1,0:T(8,128)(2,1)S(1)}, bf16[2,256,128]{2,1,0:T(8,128)(2,1)S(1)}, u32[]{:S(2)}, u32[]{:S(2)}) %collective-permute-start.3) | collective-permute-done | bytes 131104 | tf_op jit(solution)/shard_map/ppermute | solution.py:42
  49.5 1.9 %collective-permute-start.5 = (bf16[2,2,256,128]{3,2,1,0:T(8,128)(2,1)S(1)}, bf16[2,2,256,128]{3,2,1,0:T(8,128)(2,1)S(1)}, u32[]{:S(2)}, u32[]{:S(2)}) collective-permute-start(bf16[2,2,256,128]{3,2,1,0:T(8,128)(2,1)S(1)} %both.1), channel_id=1, source_target_pairs={{0,4},{4,0},{8,12},{12,8},{16,20},{20,16},{24,28},{28,24},{32,36},... | collective-permute-start | bytes 786440 | tf_op jit(solution)/shard_map/ppermute | solution.py:42
  51.4 1.5 %collective-permute-done.5.shared_ref.refs_2_.refs_6_ = bf16[2,2,256,128]{3,2,1,0:T(8,128)(2,1)S(1)} collective-permute-done((bf16[2,2,256,128]{3,2,1,0:T(8,128)(2,1)S(1)}, bf16[2,2,256,128]{3,2,1,0:T(8,128)(2,1)S(1)}, u32[]{:S(2)}, u32[]{:S(2)}) %collective-permute-start.5) | collective-permute-done | bytes 262176 | tf_op jit(solution)/shard_map/ppermute | solution.py:42
  52.9 4.3 %attend.2 = (bf16[256,1024]{1,0:T(8,128)(2,1)S(1)}, bf16[8,256,768]{2,1,0:T(8,128)(2,1)S(1)}, bf16[2,256,128]{2,1,0:T(8,128)(2,1)S(1)}, bf16[2,256,128]{2,1,0:T(8,128)(2,1)S(1)}, f32[2,256,128]{2,1,0:T(8,128)S(1)}) custom-call(bf16[2,2,256,1024]{3,2,1,0:T(8,128)(2,1)S(1)} %get-tuple-element.32.qg_ref, ...), custom_call_target="tpu_custom_call" | custom-call | flops 2013265920 | bytes 1572864 | tf_op jit(solution)/shard_map/attend/pallas_call | solution.py:341
  57.3 2.0 %collective-permute-start.6 = (bf16[2,256,128]{2,1,0:T(8,128)(2,1)S(1)}, bf16[2,256,128]{2,1,0:T(8,128)(2,1)S(1)}, u32[]{:S(2)}, u32[]{:S(2)}) collective-permute-start(bf16[2,256,128]{2,1,0:T(8,128)(2,1)S(1)} %get-tuple-element.40), channel_id=1, source_target_pairs={{4,0},{0,4},{12,8},{8,12},{20,16},{16,20},{28,24},{24,28},{36,32},... | collective-permute-start | bytes 393224 | tf_op jit(solution)/shard_map/ppermute | solution.py:42
  59.3 1.9 %collective-permute-start.7 = (bf16[2,256,128]{2,1,0:T(8,128)(2,1)S(1)}, bf16[2,256,128]{2,1,0:T(8,128)(2,1)S(1)}, u32[]{:S(2)}, u32[]{:S(2)}) collective-permute-start(bf16[2,256,128]{2,1,0:T(8,128)(2,1)S(1)} %get-tuple-element.47), channel_id=1, source_target_pairs={{8,0},{16,8},{4,12},{24,16},{12,20},{32,24},{20,28},{40,32},{28,36... | collective-permute-start | bytes 393224 | tf_op jit(solution)/shard_map/ppermute | solution.py:42
  61.2 0.0 collective-permute-done.6.refs_0_
  61.3 4.3 %attend.3 = (bf16[256,1024]{1,0:T(8,128)(2,1)S(1)}, bf16[8,256,768]{2,1,0:T(8,128)(2,1)S(1)}, bf16[2,256,128]{2,1,0:T(8,128)(2,1)S(1)}, bf16[2,256,128]{2,1,0:T(8,128)(2,1)S(1)}, f32[2,256,128]{2,1,0:T(8,128)S(1)}) custom-call(bf16[2,2,256,1024]{3,2,1,0:T(8,128)(2,1)S(1)} %get-tuple-element.32.qg_ref, ...), custom_call_target="tpu_custom_call" | custom-call | flops 2013265920 | bytes 1572864 | tf_op jit(solution)/shard_map/attend/pallas_call | solution.py:341
  65.6 2.3 %collective-permute-start.8 = (bf16[2,256,128]{2,1,0:T(8,128)(2,1)S(1)}, bf16[2,256,128]{2,1,0:T(8,128)(2,1)S(1)}, u32[]{:S(2)}, u32[]{:S(2)}) collective-permute-start(bf16[2,256,128]{2,1,0:T(8,128)(2,1)S(1)} %get-tuple-element.48), channel_id=1, source_target_pairs={{4,0},{0,4},{12,8},{8,12},{20,16},{16,20},{28,24},{24,28},{36,32},... | collective-permute-start | bytes 393224 | tf_op jit(solution)/shard_map/ppermute | solution.py:42
  67.9 3.6 %collective-permute-start.9 = (bf16[2,256,128]{2,1,0:T(8,128)(2,1)S(1)}, bf16[2,256,128]{2,1,0:T(8,128)(2,1)S(1)}, u32[]{:S(2)}, u32[]{:S(2)}) collective-permute-start(bf16[2,256,128]{2,1,0:T(8,128)(2,1)S(1)} %get-tuple-element.50), channel_id=1, source_target_pairs={{12,4},{0,8},{20,12},{8,16},{28,20},{16,24},{36,28},{24,32},{44,36... | collective-permute-start | bytes 393224 | tf_op jit(solution)/shard_map/ppermute | solution.py:42
  71.4 0.0 collective-permute-done.7.refs_1_
  71.4 0.0 collective-permute-done.8.refs_2_
  71.5 7.5 %collective-permute-done.9.refs_4_ = bf16[2,256,128]{2,1,0:T(8,128)(2,1)S(1)} collective-permute-done((bf16[2,256,128]{2,1,0:T(8,128)(2,1)S(1)}, bf16[2,256,128]{2,1,0:T(8,128)(2,1)S(1)}, u32[]{:S(2)}, u32[]{:S(2)}) %collective-permute-start.9) | collective-permute-done | bytes 131104 | tf_op jit(solution)/shard_map/ppermute | solution.py:42
  79.0 0.1 total.1
  79.0 5.7 %collective-permute-start.10 = (bf16[2,2,64,128]{3,2,1,0:T(8,128)(2,1)S(1)}, bf16[2,2,64,128]{3,2,1,0:T(8,128)(2,1)S(1)}, u32[]{:S(2)}, u32[]{:S(2)}) collective-permute-start(bf16[2,2,64,128]{3,2,1,0:T(8,128)(2,1)S(1)} %get-tuple-element.51), channel_id=1, source_target_pairs={{0,1},{1,2},{2,3},{3,0},{4,7},{5,4},{6,5},{7,6},{8,9},{9,10},{10,1... | collective-permute-start | bytes 196616 | tf_op jit(solution)/shard_map/ppermute | solution.py:55
  84.7 7.7 %collective-permute-start.11 = (bf16[2,2,64,128]{3,2,1,0:T(8,128)(2,1)S(1)}, bf16[2,2,64,128]{3,2,1,0:T(8,128)(2,1)S(1)}, u32[]{:S(2)}, u32[]{:S(2)}) collective-permute-start(bf16[2,2,64,128]{3,2,1,0:T(8,128)(2,1)S(1)} %get-tuple-element.55), channel_id=1, source_target_pairs={{0,2},{1,3},{2,0},{3,1},{4,6},{5,7},{6,4},{7,5},{8,10},{9,11},{10,... | collective-permute-start | bytes 196616 | tf_op jit(solution)/shard_map/ppermute | solution.py:55
  92.4 2.7 %collective-permute-start.12 = (bf16[2,2,64,128]{3,2,1,0:T(8,128)(2,1)S(1)}, bf16[2,2,64,128]{3,2,1,0:T(8,128)(2,1)S(1)}, u32[]{:S(2)}, u32[]{:S(2)}) collective-permute-start(bf16[2,2,64,128]{3,2,1,0:T(8,128)(2,1)S(1)} %get-tuple-element.56), channel_id=1, source_target_pairs={{0,3},{1,0},{2,1},{3,2},{4,5},{5,6},{6,7},{7,4},{8,11},{9,8},{10,9... | collective-permute-start | bytes 196616 | tf_op jit(solution)/shard_map/ppermute | solution.py:55
  95.1 1.8 %query.1 = (bf16[256,1024]{1,0:T(8,128)(2,1)S(1)}, bf16[256,1024]{1,0:T(8,128)(2,1)S(1)}) custom-call(bf16[8,256,768]{2,1,0:T(8,128)(2,1)S(1)} %get-tuple-element.42.refs_0_, bf16[2,256,128]{2,1,0:T(8,128)(2,1)S(1)} %collective-permute-done.3.after_ref.oldest_ref.refs_1_, bf16[2,2,256,128]{3,2,1,0:T(8,128)(2,1)S(1)} %collective-permute-done.5.shared_ref.refs_2_.refs_6_, ...), custom_call_target="tpu_custom_call" | custom-call | flops 805306368 | bytes 6291456 | tf_op jit(solution)/shard_map/query/pallas_call | solution.py:369
  96.9 0.0 collective-permute-done.10.refs_4_.refs_1_
  96.9 1.4 %fill.1 = (bf16[2,1,256,1024]{3,2,1,0:T(8,128)(2,1)}, bf16[2,1,256,1024]{3,2,1,0:T(8,128)(2,1)}, f32[8,128]{1,0:T(8,128)S(1)}) custom-call(bf16[256,1024]{1,0:T(8,128)(2,1)S(1)} %get-tuple-element.39.refs_0_, bf16[256,1024]{1,0:T(8,128)(2,1)S(1)} %get-tuple-element.41.refs_1_, bf16[256,1024]{1,0:T(8,128)(2,1)S(1)} %get-tuple-element.44.refs_2_, ...), custom_call_target="tpu_custom_call" | custom-call | bytes 4194304 | tf_op jit(solution)/shard_map/fill/pallas_call | solution.py:390
  98.3 3.4 %collective-permute-done.11.refs_2_ = bf16[2,2,64,128]{3,2,1,0:T(8,128)(2,1)S(1)} collective-permute-done((bf16[2,2,64,128]{3,2,1,0:T(8,128)(2,1)S(1)}, bf16[2,2,64,128]{3,2,1,0:T(8,128)(2,1)S(1)}, u32[]{:S(2)}, u32[]{:S(2)}) %collective-permute-start.11) | collective-permute-done | bytes 65568 | tf_op jit(solution)/shard_map/ppermute | solution.py:55
  101.6 2.2 %collective-permute-done.12.refs_3_ = bf16[2,2,64,128]{3,2,1,0:T(8,128)(2,1)S(1)} collective-permute-done((bf16[2,2,64,128]{3,2,1,0:T(8,128)(2,1)S(1)}, bf16[2,2,64,128]{3,2,1,0:T(8,128)(2,1)S(1)}, u32[]{:S(2)}, u32[]{:S(2)}) %collective-permute-start.12) | collective-permute-done | bytes 65568 | tf_op jit(solution)/shard_map/ppermute | solution.py:55
  103.8 0.8 place.1
  (2 shorter events, 0.1 us)
Async XLA Ops:
  1.7 26.4 %collective-permute-start = (bf16[2,2,64,128]{3,2,1,0:T(8,128)(2,1)S(1)}, bf16[2,2,64,128]{3,2,1,0:T(8,128)(2,1)S(1)}, u32[]{:S(2)}, u32[]{:S(2)}) collective-permute-start(bf16[2,2,64,128]{3,2,1,0:T(8,128)(2,1)S(1)} %get-tuple-element.33), channel_id=1, source_target_pairs={{0,1},{1,2},{2,3},{3,0},{4,7},{5,4},{6,5},{7,6},{8,9},{9,10},{10,1... | collective-permute-start | bytes 196616 | tf_op jit(solution)/shard_map/ppermute | solution.py:55
  10.8 17.3 %collective-permute-start.1 = (bf16[2,2,64,128]{3,2,1,0:T(8,128)(2,1)S(1)}, bf16[2,2,64,128]{3,2,1,0:T(8,128)(2,1)S(1)}, u32[]{:S(2)}, u32[]{:S(2)}) collective-permute-start(bf16[2,2,64,128]{3,2,1,0:T(8,128)(2,1)S(1)} %get-tuple-element.34), channel_id=1, source_target_pairs={{0,2},{1,3},{2,0},{3,1},{4,6},{5,7},{6,4},{7,5},{8,10},{9,11},{10,... | collective-permute-start | bytes 196616 | tf_op jit(solution)/shard_map/ppermute | solution.py:55
  19.0 11.3 %collective-permute-start.2 = (bf16[2,2,64,128]{3,2,1,0:T(8,128)(2,1)S(1)}, bf16[2,2,64,128]{3,2,1,0:T(8,128)(2,1)S(1)}, u32[]{:S(2)}, u32[]{:S(2)}) collective-permute-start(bf16[2,2,64,128]{3,2,1,0:T(8,128)(2,1)S(1)} %get-tuple-element.35), channel_id=1, source_target_pairs={{0,3},{1,0},{2,1},{3,2},{4,5},{5,6},{6,7},{7,4},{8,11},{9,8},{10,9... | collective-permute-start | bytes 196616 | tf_op jit(solution)/shard_map/ppermute | solution.py:55
  24.5 1.2 %copy-start = (bf16[2,1,256,1024]{3,2,1,0:T(8,128)(2,1)S(1)}, bf16[2,1,256,1024]{3,2,1,0:T(8,128)(2,1)}, u32[]{:S(2)}) copy-start(bf16[2,1,256,1024]{3,2,1,0:T(8,128)(2,1)} %q_ref.1) | copy-start | bytes 3145732
  25.7 1.2 %copy-start.1 = (bf16[2,1,256,1024]{3,2,1,0:T(8,128)(2,1)S(1)}, bf16[2,1,256,1024]{3,2,1,0:T(8,128)(2,1)}, u32[]{:S(2)}) copy-start(bf16[2,1,256,1024]{3,2,1,0:T(8,128)(2,1)} %g_ref.1) | copy-start | bytes 3145732
  26.9 0.7 copy-start.2
  30.4 10.7 %collective-permute-start.4 = (bf16[2,256,128]{2,1,0:T(8,128)(2,1)S(1)}, bf16[2,256,128]{2,1,0:T(8,128)(2,1)S(1)}, u32[]{:S(2)}, u32[]{:S(2)}) collective-permute-start(bf16[2,256,128]{2,1,0:T(8,128)(2,1)S(1)} %get-tuple-element.38.here_ref.refs_7_), channel_id=1, source_target_pairs={{4,12},{8,0},{12,20},{16,8},{20,28},{24,16},{28,36},{32,24},{36,44... | collective-permute-start | bytes 393224 | tf_op jit(solution)/shard_map/ppermute | solution.py:42
  38.4 11.1 %collective-permute-start.3 = (bf16[2,256,128]{2,1,0:T(8,128)(2,1)S(1)}, bf16[2,256,128]{2,1,0:T(8,128)(2,1)S(1)}, u32[]{:S(2)}, u32[]{:S(2)}) collective-permute-start(bf16[2,256,128]{2,1,0:T(8,128)(2,1)S(1)} %get-tuple-element.37.x_ref.here_ref.refs_3_), channel_id=1, source_target_pairs={{0,8},{8,16},{12,4},{16,24},{20,12},{24,32},{28,20},{32,40},{36,28... | collective-permute-start | bytes 393224 | tf_op jit(solution)/shard_map/ppermute | solution.py:42
  49.5 3.4 %collective-permute-start.5 = (bf16[2,2,256,128]{3,2,1,0:T(8,128)(2,1)S(1)}, bf16[2,2,256,128]{3,2,1,0:T(8,128)(2,1)S(1)}, u32[]{:S(2)}, u32[]{:S(2)}) collective-permute-start(bf16[2,2,256,128]{3,2,1,0:T(8,128)(2,1)S(1)} %both.1), channel_id=1, source_target_pairs={{0,4},{4,0},{8,12},{12,8},{16,20},{20,16},{24,28},{28,24},{32,36},... | collective-permute-start | bytes 786440 | tf_op jit(solution)/shard_map/ppermute | solution.py:42
  57.3 4.0 %collective-permute-start.6 = (bf16[2,256,128]{2,1,0:T(8,128)(2,1)S(1)}, bf16[2,256,128]{2,1,0:T(8,128)(2,1)S(1)}, u32[]{:S(2)}, u32[]{:S(2)}) collective-permute-start(bf16[2,256,128]{2,1,0:T(8,128)(2,1)S(1)} %get-tuple-element.40), channel_id=1, source_target_pairs={{4,0},{0,4},{12,8},{8,12},{20,16},{16,20},{28,24},{24,28},{36,32},... | collective-permute-start | bytes 393224 | tf_op jit(solution)/shard_map/ppermute | solution.py:42
  59.3 12.1 %collective-permute-start.7 = (bf16[2,256,128]{2,1,0:T(8,128)(2,1)S(1)}, bf16[2,256,128]{2,1,0:T(8,128)(2,1)S(1)}, u32[]{:S(2)}, u32[]{:S(2)}) collective-permute-start(bf16[2,256,128]{2,1,0:T(8,128)(2,1)S(1)} %get-tuple-element.47), channel_id=1, source_target_pairs={{8,0},{16,8},{4,12},{24,16},{12,20},{32,24},{20,28},{40,32},{28,36... | collective-permute-start | bytes 393224 | tf_op jit(solution)/shard_map/ppermute | solution.py:42
  65.6 5.9 %collective-permute-start.8 = (bf16[2,256,128]{2,1,0:T(8,128)(2,1)S(1)}, bf16[2,256,128]{2,1,0:T(8,128)(2,1)S(1)}, u32[]{:S(2)}, u32[]{:S(2)}) collective-permute-start(bf16[2,256,128]{2,1,0:T(8,128)(2,1)S(1)} %get-tuple-element.48), channel_id=1, source_target_pairs={{4,0},{0,4},{12,8},{8,12},{20,16},{16,20},{28,24},{24,28},{36,32},... | collective-permute-start | bytes 393224 | tf_op jit(solution)/shard_map/ppermute | solution.py:42
  67.9 11.1 %collective-permute-start.9 = (bf16[2,256,128]{2,1,0:T(8,128)(2,1)S(1)}, bf16[2,256,128]{2,1,0:T(8,128)(2,1)S(1)}, u32[]{:S(2)}, u32[]{:S(2)}) collective-permute-start(bf16[2,256,128]{2,1,0:T(8,128)(2,1)S(1)} %get-tuple-element.50), channel_id=1, source_target_pairs={{12,4},{0,8},{20,12},{8,16},{28,20},{16,24},{36,28},{24,32},{44,36... | collective-permute-start | bytes 393224 | tf_op jit(solution)/shard_map/ppermute | solution.py:42
  79.0 17.9 %collective-permute-start.10 = (bf16[2,2,64,128]{3,2,1,0:T(8,128)(2,1)S(1)}, bf16[2,2,64,128]{3,2,1,0:T(8,128)(2,1)S(1)}, u32[]{:S(2)}, u32[]{:S(2)}) collective-permute-start(bf16[2,2,64,128]{3,2,1,0:T(8,128)(2,1)S(1)} %get-tuple-element.51), channel_id=1, source_target_pairs={{0,1},{1,2},{2,3},{3,0},{4,7},{5,4},{6,5},{7,6},{8,9},{9,10},{10,1... | collective-permute-start | bytes 196616 | tf_op jit(solution)/shard_map/ppermute | solution.py:55
  84.7 16.9 %collective-permute-start.11 = (bf16[2,2,64,128]{3,2,1,0:T(8,128)(2,1)S(1)}, bf16[2,2,64,128]{3,2,1,0:T(8,128)(2,1)S(1)}, u32[]{:S(2)}, u32[]{:S(2)}) collective-permute-start(bf16[2,2,64,128]{3,2,1,0:T(8,128)(2,1)S(1)} %get-tuple-element.55), channel_id=1, source_target_pairs={{0,2},{1,3},{2,0},{3,1},{4,6},{5,7},{6,4},{7,5},{8,10},{9,11},{10,... | collective-permute-start | bytes 196616 | tf_op jit(solution)/shard_map/ppermute | solution.py:55
  92.4 11.4 %collective-permute-start.12 = (bf16[2,2,64,128]{3,2,1,0:T(8,128)(2,1)S(1)}, bf16[2,2,64,128]{3,2,1,0:T(8,128)(2,1)S(1)}, u32[]{:S(2)}, u32[]{:S(2)}) collective-permute-start(bf16[2,2,64,128]{3,2,1,0:T(8,128)(2,1)S(1)} %get-tuple-element.56), channel_id=1, source_target_pairs={{0,3},{1,0},{2,1},{3,2},{4,5},{5,6},{6,7},{7,4},{8,11},{9,8},{10,9... | collective-permute-start | bytes 196616 | tf_op jit(solution)/shard_map/ppermute | solution.py:55

commit v6 on v5

--- a/solution.py
+++ b/solution.py
@@ -22,6 +22,12 @@
     if i % 2:
         return i - 2
     return i + 2 if i + 2 < contexts else i + 1
+
+
+def across_y(i, contexts):
+    if i % 2:
+        return min(i + 1, contexts - 1)
+    return i - 1
 
 
 def far_y(i, contexts):
@@ -83,11 +89,6 @@
         source = lax.rem(tp - offset(step, core, groups) + groups, groups)
         for block, out in enumerate(outs):
             out[:, aligned(source, rows), :] = piece[block]
-
-
-def both_kernel(x_ref, came_ref, after_ref, out_ref):
-    out_ref[0] = x_ref[...]
-    out_ref[1] = came_ref[...]
 
 
 def total_kernel(groups, *refs):
@@ -206,13 +207,11 @@
     return jnp.concatenate([old, field[:, side:].astype(bf), own], axis=1)
 
 
-def window(turn, kind, oldest_ref, shared_ref, here_ref):
-    return jnp.concatenate(
-        [oldest_ref[kind], shared_ref[1 - turn, kind], here_ref[kind]], axis=0
-    )
-
-
-def attend_kernel(turn, qg_ref, oldest_ref, shared_ref, here_ref, bias_ref, *refs):
+def window(kind, *line):
+    return jnp.concatenate([ref[kind] for ref in line], axis=0)
+
+
+def attend_kernel(turn, qg_ref, oldest_ref, middle_ref, here_ref, bias_ref, *refs):
     if turn == 0:
         more_ref = None
     else:
@@ -221,7 +220,7 @@
     side, heads = attn_ref.shape[0], ds_ref.shape[0]
     bf = jnp.bfloat16
     over, down = ((1,), (0,)), ((0,), (0,))
-    keys, values = [window(turn, kind, oldest_ref, shared_ref, here_ref) for kind in range(2)]
+    keys, values = [window(kind, oldest_ref, middle_ref, here_ref) for kind in range(2)]
     kt_ref[...] = keys.T
     vt_ref[...] = values.T
 
@@ -275,7 +274,7 @@
     for turn, out in enumerate(outs):
         ds_ref, *line = inputs[4 * turn : 4 * turn + 4]
         heads = ds_ref.shape[0]
-        keys = window(turn, 0, *line)
+        keys = window(0, *line)
         for head in range(heads):
             dq = dot(ds_ref[head], keys, ((1,), (0,))) * FACTOR
             out[:, head * HD : (head + 1) * HD] = dq.astype(out.dtype)
@@ -320,18 +319,8 @@
         compiler_params=SMALL,
         name="join",
     )(kv, *came, bias)
-    came_y, came_x = move(y, far_y), move(x, far_x)
-    both = pl.pallas_call(
-        both_kernel,
-        out_shape=shape((2, 2, side, HD), bf),
-        in_specs=[VMEM, VMEM, ANY],
-        out_specs=VMEM,
-        compiler_params=SMALL,
-        name="both",
-    )(x, came_y, came_x)
-    shared = move(both, partner)
-    x_line = (came_x, shared, x)
-    y_line = (came_y, shared, y)
+    x_line = (move(x, far_x), move(y, across_y), x)
+    y_line = (move(y, far_y), move(x, partner), y)
 
     heads = width // HD
     work = heads * side * 3 * side

time: 105 us -> 100 us (0.952)
  the two profiles are of different devices: /device:TPU:96 before, /device:TPU:64 now
where the time goes in v6:
time: 100 us; the launch traced here: 99.4 us
  starting transfers between devices  65.8 us (66%)
  waiting for transfers between devices  15.4 us (15%)
  Pallas kernels  13.2 us (13%)
  local copies, waits for them, and re-layouts  3.12 us (3%)
    ppermute x6, starting transfers between devices, around(): return lax.ppermute(block, ('cp', 'tp'), route)  39.5 us
    ppermute x8, starting transfers between devices, move(): return lax.ppermute(block, 'cp', route)  26.3 us
    ppermute x8, waiting for transfers between devices, move(): return lax.ppermute(block, 'cp', route)  9.15 us
    pallas_call x2, Pallas kernels, attend(): pl.pallas_call(functools.partial(attend_kernel, turn), in_specs=[VMEM] *...  8.64 us
    ppermute x6, waiting for transfers between devices, around(): return lax.ppermute(block, ('cp', 'tp'), route)  6.25 us
    unnamed x6, local copies, waits for them, and re-layouts  3.12 us
  transfers between devices with their start and end apart: 14, of which 4 were waited for; matrix products, arithmetic and copies ran while one was open for 0% of the time, Pallas kernels for 12%

profile of v6, /device:TPU:64, one launch (start us, length us, event | category | flops | bytes accessed | tf_op | source)
XLA Modules:
  0.0 99.4 jit_solution(5968554927381240672)
XLA Ops:
  0.6 1.0 %pad_maximum_fusion.kv_ref = bf16[2,2,1,64,512]{4,3,2,1,0:T(8,128)(2,1)S(1)} fusion(bf16[1,2,1,64,512]{4,3,2,1,0:T(8,128)(2,1)} %bitcast.4, bf16[1,2,1,64,512]{4,3,2,1,0:T(8,128)(2,1)} %bitcast.5), kind=kLoop, calls=%fused_computation | loop fusion | flops 131072 | bytes 524288 | tf_op jit(solution)/shard_map/stack | solution.py:291
  1.6 0.1 split.1
  1.7 9.1 %collective-permute-start = (bf16[2,2,64,128]{3,2,1,0:T(8,128)(2,1)S(1)}, bf16[2,2,64,128]{3,2,1,0:T(8,128)(2,1)S(1)}, u32[]{:S(2)}, u32[]{:S(2)}) collective-permute-start(bf16[2,2,64,128]{3,2,1,0:T(8,128)(2,1)S(1)} %get-tuple-element.33), channel_id=1, source_target_pairs={{0,1},{1,2},{2,3},{3,0},{4,7},{5,4},{6,5},{7,6},{8,9},{9,10},{10,1... | collective-permute-start | bytes 196616 | tf_op jit(solution)/shard_map/ppermute | solution.py:61
  10.8 9.1 %collective-permute-start.1 = (bf16[2,2,64,128]{3,2,1,0:T(8,128)(2,1)S(1)}, bf16[2,2,64,128]{3,2,1,0:T(8,128)(2,1)S(1)}, u32[]{:S(2)}, u32[]{:S(2)}) collective-permute-start(bf16[2,2,64,128]{3,2,1,0:T(8,128)(2,1)S(1)} %get-tuple-element.34), channel_id=1, source_target_pairs={{0,2},{1,3},{2,0},{3,1},{4,6},{5,7},{6,4},{7,5},{8,10},{9,11},{10,... | collective-permute-start | bytes 196616 | tf_op jit(solution)/shard_map/ppermute | solution.py:61
  19.9 5.5 %collective-permute-start.2 = (bf16[2,2,64,128]{3,2,1,0:T(8,128)(2,1)S(1)}, bf16[2,2,64,128]{3,2,1,0:T(8,128)(2,1)S(1)}, u32[]{:S(2)}, u32[]{:S(2)}) collective-permute-start(bf16[2,2,64,128]{3,2,1,0:T(8,128)(2,1)S(1)} %get-tuple-element.35), channel_id=1, source_target_pairs={{0,3},{1,0},{2,1},{3,2},{4,5},{5,6},{6,7},{7,4},{8,11},{9,8},{10,9... | collective-permute-start | bytes 196616 | tf_op jit(solution)/shard_map/ppermute | solution.py:61
  25.4 0.0 copy-start
  25.4 1.2 %copy-done = bf16[2,1,256,1024]{3,2,1,0:T(8,128)(2,1)S(1)} copy-done((bf16[2,1,256,1024]{3,2,1,0:T(8,128)(2,1)S(1)}, bf16[2,1,256,1024]{3,2,1,0:T(8,128)(2,1)}, u32[]{:S(2)}) %copy-start) | copy-done | bytes 1048600
  26.6 0.0 copy-start.1
  26.6 1.2 %copy-done.1 = bf16[2,1,256,1024]{3,2,1,0:T(8,128)(2,1)S(1)} copy-done((bf16[2,1,256,1024]{3,2,1,0:T(8,128)(2,1)S(1)}, bf16[2,1,256,1024]{3,2,1,0:T(8,128)(2,1)}, u32[]{:S(2)}) %copy-start.1) | copy-done | bytes 1048600
  27.8 0.0 copy-start.2
  27.8 0.7 copy-done.2
  28.5 0.5 prepare.1
  29.0 0.0 collective-permute-done.refs_0_
  29.0 0.0 collective-permute-done.1.refs_1_
  29.0 2.9 %collective-permute-done.2.refs_2_ = bf16[2,2,64,128]{3,2,1,0:T(8,128)(2,1)S(1)} collective-permute-done((bf16[2,2,64,128]{3,2,1,0:T(8,128)(2,1)S(1)}, bf16[2,2,64,128]{3,2,1,0:T(8,128)(2,1)S(1)}, u32[]{:S(2)}, u32[]{:S(2)}) %collective-permute-start.2) | collective-permute-done | bytes 65568 | tf_op jit(solution)/shard_map/ppermute | solution.py:61
  32.0 3.1 %collective-permute-start.3 = (bf16[2,256,128]{2,1,0:T(8,128)(2,1)S(1)}, bf16[2,256,128]{2,1,0:T(8,128)(2,1)S(1)}, u32[]{:S(2)}, u32[]{:S(2)}) collective-permute-start(bf16[2,256,128]{2,1,0:T(8,128)(2,1)S(1)} %get-tuple-element.37.here_ref.refs_3_), channel_id=1, source_target_pairs={{0,8},{8,16},{12,4},{16,24},{20,12},{24,32},{28,20},{32,40},{36,28... | collective-permute-start | bytes 393224 | tf_op jit(solution)/shard_map/ppermute | solution.py:48
  35.1 5.2 %collective-permute-start.4 = (bf16[2,256,128]{2,1,0:T(8,128)(2,1)S(1)}, bf16[2,256,128]{2,1,0:T(8,128)(2,1)S(1)}, u32[]{:S(2)}, u32[]{:S(2)}) collective-permute-start(bf16[2,256,128]{2,1,0:T(8,128)(2,1)S(1)} %get-tuple-element.38.here_ref.refs_7_), channel_id=1, source_target_pairs={{4,8},{8,4},{12,16},{16,12},{20,24},{24,20},{28,32},{32,28},{36,40... | collective-permute-start | bytes 393224 | tf_op jit(solution)/shard_map/ppermute | solution.py:48
  40.4 1.9 %collective-permute-start.6 = (bf16[2,256,128]{2,1,0:T(8,128)(2,1)S(1)}, bf16[2,256,128]{2,1,0:T(8,128)(2,1)S(1)}, u32[]{:S(2)}, u32[]{:S(2)}) collective-permute-start(bf16[2,256,128]{2,1,0:T(8,128)(2,1)S(1)} %get-tuple-element.37.here_ref.refs_3_), channel_id=1, source_target_pairs={{0,4},{4,0},{8,12},{12,8},{16,20},{20,16},{24,28},{28,24},{32,36},... | collective-permute-start | bytes 393224 | tf_op jit(solution)/shard_map/ppermute | solution.py:48
  42.3 4.9 %collective-permute-start.5 = (bf16[2,256,128]{2,1,0:T(8,128)(2,1)S(1)}, bf16[2,256,128]{2,1,0:T(8,128)(2,1)S(1)}, u32[]{:S(2)}, u32[]{:S(2)}) collective-permute-start(bf16[2,256,128]{2,1,0:T(8,128)(2,1)S(1)} %get-tuple-element.38.here_ref.refs_7_), channel_id=1, source_target_pairs={{4,12},{8,0},{12,20},{16,8},{20,28},{24,16},{28,36},{32,24},{36,44... | collective-permute-start | bytes 393224 | tf_op jit(solution)/shard_map/ppermute | solution.py:48
  47.3 0.0 collective-permute-done.3.oldest_ref.refs_1_
  47.3 0.0 collective-permute-done.4.middle_ref.refs_2_
  47.3 4.3 %attend.2 = (bf16[256,1024]{1,0:T(8,128)(2,1)S(1)}, bf16[8,256,768]{2,1,0:T(8,128)(2,1)S(1)}, bf16[2,256,128]{2,1,0:T(8,128)(2,1)S(1)}, bf16[2,256,128]{2,1,0:T(8,128)(2,1)S(1)}, f32[2,256,128]{2,1,0:T(8,128)S(1)}) custom-call(bf16[2,2,256,1024]{3,2,1,0:T(8,128)(2,1)S(1)} %get-tuple-element.32.qg_ref, ...), custom_call_target="tpu_custom_call" | custom-call | flops 2013265920 | bytes 1572864 | tf_op jit(solution)/shard_map/attend/pallas_call | solution.py:330
  51.6 1.9 %collective-permute-start.7 = (bf16[2,256,128]{2,1,0:T(8,128)(2,1)S(1)}, bf16[2,256,128]{2,1,0:T(8,128)(2,1)S(1)}, u32[]{:S(2)}, u32[]{:S(2)}) collective-permute-start(bf16[2,256,128]{2,1,0:T(8,128)(2,1)S(1)} %get-tuple-element.40), channel_id=1, source_target_pairs={{4,0},{0,4},{12,8},{8,12},{20,16},{16,20},{28,24},{24,28},{36,32},... | collective-permute-start | bytes 393224 | tf_op jit(solution)/shard_map/ppermute | solution.py:48
  53.5 5.3 %collective-permute-start.8 = (bf16[2,256,128]{2,1,0:T(8,128)(2,1)S(1)}, bf16[2,256,128]{2,1,0:T(8,128)(2,1)S(1)}, u32[]{:S(2)}, u32[]{:S(2)}) collective-permute-start(bf16[2,256,128]{2,1,0:T(8,128)(2,1)S(1)} %get-tuple-element.47), channel_id=1, source_target_pairs={{8,0},{16,8},{4,12},{24,16},{12,20},{32,24},{20,28},{40,32},{28,36... | collective-permute-start | bytes 393224 | tf_op jit(solution)/shard_map/ppermute | solution.py:48
  58.9 0.0 collective-permute-done.6.middle_ref.refs_6_
  58.9 0.0 collective-permute-done.5.oldest_ref.refs_5_
  58.9 0.0 collective-permute-done.7.refs_0_
  58.9 4.3 %attend.3 = (bf16[256,1024]{1,0:T(8,128)(2,1)S(1)}, bf16[8,256,768]{2,1,0:T(8,128)(2,1)S(1)}, bf16[2,256,128]{2,1,0:T(8,128)(2,1)S(1)}, bf16[2,256,128]{2,1,0:T(8,128)(2,1)S(1)}, f32[2,256,128]{2,1,0:T(8,128)S(1)}) custom-call(bf16[2,2,256,1024]{3,2,1,0:T(8,128)(2,1)S(1)} %get-tuple-element.32.qg_ref, ...), custom_call_target="tpu_custom_call" | custom-call | flops 2013265920 | bytes 1572864 | tf_op jit(solution)/shard_map/attend/pallas_call | solution.py:330
  63.2 1.9 %collective-permute-start.9 = (bf16[2,256,128]{2,1,0:T(8,128)(2,1)S(1)}, bf16[2,256,128]{2,1,0:T(8,128)(2,1)S(1)}, u32[]{:S(2)}, u32[]{:S(2)}) collective-permute-start(bf16[2,256,128]{2,1,0:T(8,128)(2,1)S(1)} %get-tuple-element.48), channel_id=1, source_target_pairs={{4,0},{0,4},{12,8},{8,12},{20,16},{16,20},{28,24},{24,28},{36,32},... | collective-permute-start | bytes 393224 | tf_op jit(solution)/shard_map/ppermute | solution.py:48
  65.2 1.9 %collective-permute-start.10 = (bf16[2,256,128]{2,1,0:T(8,128)(2,1)S(1)}, bf16[2,256,128]{2,1,0:T(8,128)(2,1)S(1)}, u32[]{:S(2)}, u32[]{:S(2)}) collective-permute-start(bf16[2,256,128]{2,1,0:T(8,128)(2,1)S(1)} %get-tuple-element.50), channel_id=1, source_target_pairs={{12,4},{0,8},{20,12},{8,16},{28,20},{16,24},{36,28},{24,32},{44,36... | collective-permute-start | bytes 393224 | tf_op jit(solution)/shard_map/ppermute | solution.py:48
  67.1 0.0 collective-permute-done.8.refs_1_
  67.1 0.0 collective-permute-done.9.refs_2_
  67.1 9.1 %collective-permute-done.10.refs_4_ = bf16[2,256,128]{2,1,0:T(8,128)(2,1)S(1)} collective-permute-done((bf16[2,256,128]{2,1,0:T(8,128)(2,1)S(1)}, bf16[2,256,128]{2,1,0:T(8,128)(2,1)S(1)}, u32[]{:S(2)}, u32[]{:S(2)}) %collective-permute-start.10) | collective-permute-done | bytes 131104 | tf_op jit(solution)/shard_map/ppermute | solution.py:48
  76.2 0.1 total.1
  76.3 6.5 %collective-permute-start.11 = (bf16[2,2,64,128]{3,2,1,0:T(8,128)(2,1)S(1)}, bf16[2,2,64,128]{3,2,1,0:T(8,128)(2,1)S(1)}, u32[]{:S(2)}, u32[]{:S(2)}) collective-permute-start(bf16[2,2,64,128]{3,2,1,0:T(8,128)(2,1)S(1)} %get-tuple-element.51), channel_id=1, source_target_pairs={{0,1},{1,2},{2,3},{3,0},{4,7},{5,4},{6,5},{7,6},{8,9},{9,10},{10,1... | collective-permute-start | bytes 196616 | tf_op jit(solution)/shard_map/ppermute | solution.py:61
  82.8 5.1 %collective-permute-start.12 = (bf16[2,2,64,128]{3,2,1,0:T(8,128)(2,1)S(1)}, bf16[2,2,64,128]{3,2,1,0:T(8,128)(2,1)S(1)}, u32[]{:S(2)}, u32[]{:S(2)}) collective-permute-start(bf16[2,2,64,128]{3,2,1,0:T(8,128)(2,1)S(1)} %get-tuple-element.55), channel_id=1, source_target_pairs={{0,2},{1,3},{2,0},{3,1},{4,6},{5,7},{6,4},{7,5},{8,10},{9,11},{10,... | collective-permute-start | bytes 196616 | tf_op jit(solution)/shard_map/ppermute | solution.py:61
  87.9 4.3 %collective-permute-start.13 = (bf16[2,2,64,128]{3,2,1,0:T(8,128)(2,1)S(1)}, bf16[2,2,64,128]{3,2,1,0:T(8,128)(2,1)S(1)}, u32[]{:S(2)}, u32[]{:S(2)}) collective-permute-start(bf16[2,2,64,128]{3,2,1,0:T(8,128)(2,1)S(1)} %get-tuple-element.56), channel_id=1, source_target_pairs={{0,3},{1,0},{2,1},{3,2},{4,5},{5,6},{6,7},{7,4},{8,11},{9,8},{10,9... | collective-permute-start | bytes 196616 | tf_op jit(solution)/shard_map/ppermute | solution.py:61
  92.2 1.8 %query.1 = (bf16[256,1024]{1,0:T(8,128)(2,1)S(1)}, bf16[256,1024]{1,0:T(8,128)(2,1)S(1)}) custom-call(bf16[8,256,768]{2,1,0:T(8,128)(2,1)S(1)} %get-tuple-element.42.refs_0_, bf16[2,256,128]{2,1,0:T(8,128)(2,1)S(1)} %collective-permute-done.3.oldest_ref.refs_1_, bf16[2,256,128]{2,1,0:T(8,128)(2,1)S(1)} %collective-permute-done.4.middle_ref.refs_2_, ...), custom_call_target="tpu_custom_call" | custom-call | flops 805306368 | bytes 6291456 | tf_op jit(solution)/shard_map/query/pallas_call | solution.py:358
  94.0 0.0 collective-permute-done.11.refs_4_.refs_1_
  94.0 1.4 %fill.1 = (bf16[2,1,256,1024]{3,2,1,0:T(8,128)(2,1)}, bf16[2,1,256,1024]{3,2,1,0:T(8,128)(2,1)}, f32[8,128]{1,0:T(8,128)S(1)}) custom-call(bf16[256,1024]{1,0:T(8,128)(2,1)S(1)} %get-tuple-element.39.refs_0_, bf16[256,1024]{1,0:T(8,128)(2,1)S(1)} %get-tuple-element.41.refs_1_, bf16[256,1024]{1,0:T(8,128)(2,1)S(1)} %get-tuple-element.44.refs_2_, ...), custom_call_target="tpu_custom_call" | custom-call | bytes 4194304 | tf_op jit(solution)/shard_map/fill/pallas_call | solution.py:379
  95.3 2.3 %collective-permute-done.12.refs_2_ = bf16[2,2,64,128]{3,2,1,0:T(8,128)(2,1)S(1)} collective-permute-done((bf16[2,2,64,128]{3,2,1,0:T(8,128)(2,1)S(1)}, bf16[2,2,64,128]{3,2,1,0:T(8,128)(2,1)S(1)}, u32[]{:S(2)}, u32[]{:S(2)}) %collective-permute-start.12) | collective-permute-done | bytes 65568 | tf_op jit(solution)/shard_map/ppermute | solution.py:61
  97.7 1.0 collective-permute-done.13.refs_3_
  98.7 0.8 place.1
  (1 shorter events, 0.0 us)
Async XLA Ops:
  1.7 27.3 %collective-permute-start = (bf16[2,2,64,128]{3,2,1,0:T(8,128)(2,1)S(1)}, bf16[2,2,64,128]{3,2,1,0:T(8,128)(2,1)S(1)}, u32[]{:S(2)}, u32[]{:S(2)}) collective-permute-start(bf16[2,2,64,128]{3,2,1,0:T(8,128)(2,1)S(1)} %get-tuple-element.33), channel_id=1, source_target_pairs={{0,1},{1,2},{2,3},{3,0},{4,7},{5,4},{6,5},{7,6},{8,9},{9,10},{10,1... | collective-permute-start | bytes 196616 | tf_op jit(solution)/shard_map/ppermute | solution.py:61
  10.8 18.2 %collective-permute-start.1 = (bf16[2,2,64,128]{3,2,1,0:T(8,128)(2,1)S(1)}, bf16[2,2,64,128]{3,2,1,0:T(8,128)(2,1)S(1)}, u32[]{:S(2)}, u32[]{:S(2)}) collective-permute-start(bf16[2,2,64,128]{3,2,1,0:T(8,128)(2,1)S(1)} %get-tuple-element.34), channel_id=1, source_target_pairs={{0,2},{1,3},{2,0},{3,1},{4,6},{5,7},{6,4},{7,5},{8,10},{9,11},{10,... | collective-permute-start | bytes 196616 | tf_op jit(solution)/shard_map/ppermute | solution.py:61
  19.9 12.1 %collective-permute-start.2 = (bf16[2,2,64,128]{3,2,1,0:T(8,128)(2,1)S(1)}, bf16[2,2,64,128]{3,2,1,0:T(8,128)(2,1)S(1)}, u32[]{:S(2)}, u32[]{:S(2)}) collective-permute-start(bf16[2,2,64,128]{3,2,1,0:T(8,128)(2,1)S(1)} %get-tuple-element.35), channel_id=1, source_target_pairs={{0,3},{1,0},{2,1},{3,2},{4,5},{5,6},{6,7},{7,4},{8,11},{9,8},{10,9... | collective-permute-start | bytes 196616 | tf_op jit(solution)/shard_map/ppermute | solution.py:61
  25.4 1.2 %copy-start = (bf16[2,1,256,1024]{3,2,1,0:T(8,128)(2,1)S(1)}, bf16[2,1,256,1024]{3,2,1,0:T(8,128)(2,1)}, u32[]{:S(2)}) copy-start(bf16[2,1,256,1024]{3,2,1,0:T(8,128)(2,1)} %q_ref.1) | copy-start | bytes 3145732
  26.6 1.2 %copy-start.1 = (bf16[2,1,256,1024]{3,2,1,0:T(8,128)(2,1)S(1)}, bf16[2,1,256,1024]{3,2,1,0:T(8,128)(2,1)}, u32[]{:S(2)}) copy-start(bf16[2,1,256,1024]{3,2,1,0:T(8,128)(2,1)} %g_ref.1) | copy-start | bytes 3145732
  27.8 0.7 copy-start.2
  32.0 15.2 %collective-permute-start.3 = (bf16[2,256,128]{2,1,0:T(8,128)(2,1)S(1)}, bf16[2,256,128]{2,1,0:T(8,128)(2,1)S(1)}, u32[]{:S(2)}, u32[]{:S(2)}) collective-permute-start(bf16[2,256,128]{2,1,0:T(8,128)(2,1)S(1)} %get-tuple-element.37.here_ref.refs_3_), channel_id=1, source_target_pairs={{0,8},{8,16},{12,4},{16,24},{20,12},{24,32},{28,20},{32,40},{36,28... | collective-permute-start | bytes 393224 | tf_op jit(solution)/shard_map/ppermute | solution.py:48
  35.1 12.1 %collective-permute-start.4 = (bf16[2,256,128]{2,1,0:T(8,128)(2,1)S(1)}, bf16[2,256,128]{2,1,0:T(8,128)(2,1)S(1)}, u32[]{:S(2)}, u32[]{:S(2)}) collective-permute-start(bf16[2,256,128]{2,1,0:T(8,128)(2,1)S(1)} %get-tuple-element.38.here_ref.refs_7_), channel_id=1, source_target_pairs={{4,8},{8,4},{12,16},{16,12},{20,24},{24,20},{28,32},{32,28},{36,40... | collective-permute-start | bytes 393224 | tf_op jit(solution)/shard_map/ppermute | solution.py:48
  40.4 18.5 %collective-permute-start.6 = (bf16[2,256,128]{2,1,0:T(8,128)(2,1)S(1)}, bf16[2,256,128]{2,1,0:T(8,128)(2,1)S(1)}, u32[]{:S(2)}, u32[]{:S(2)}) collective-permute-start(bf16[2,256,128]{2,1,0:T(8,128)(2,1)S(1)} %get-tuple-element.37.here_ref.refs_3_), channel_id=1, source_target_pairs={{0,4},{4,0},{8,12},{12,8},{16,20},{20,16},{24,28},{28,24},{32,36},... | collective-permute-start | bytes 393224 | tf_op jit(solution)/shard_map/ppermute | solution.py:48
  42.3 16.6 %collective-permute-start.5 = (bf16[2,256,128]{2,1,0:T(8,128)(2,1)S(1)}, bf16[2,256,128]{2,1,0:T(8,128)(2,1)S(1)}, u32[]{:S(2)}, u32[]{:S(2)}) collective-permute-start(bf16[2,256,128]{2,1,0:T(8,128)(2,1)S(1)} %get-tuple-element.38.here_ref.refs_7_), channel_id=1, source_target_pairs={{4,12},{8,0},{12,20},{16,8},{20,28},{24,16},{28,36},{32,24},{36,44... | collective-permute-start | bytes 393224 | tf_op jit(solution)/shard_map/ppermute | solution.py:48
  51.6 7.3 %collective-permute-start.7 = (bf16[2,256,128]{2,1,0:T(8,128)(2,1)S(1)}, bf16[2,256,128]{2,1,0:T(8,128)(2,1)S(1)}, u32[]{:S(2)}, u32[]{:S(2)}) collective-permute-start(bf16[2,256,128]{2,1,0:T(8,128)(2,1)S(1)} %get-tuple-element.40), channel_id=1, source_target_pairs={{4,0},{0,4},{12,8},{8,12},{20,16},{16,20},{28,24},{24,28},{36,32},... | collective-permute-start | bytes 393224 | tf_op jit(solution)/shard_map/ppermute | solution.py:48
  53.5 13.6 %collective-permute-start.8 = (bf16[2,256,128]{2,1,0:T(8,128)(2,1)S(1)}, bf16[2,256,128]{2,1,0:T(8,128)(2,1)S(1)}, u32[]{:S(2)}, u32[]{:S(2)}) collective-permute-start(bf16[2,256,128]{2,1,0:T(8,128)(2,1)S(1)} %get-tuple-element.47), channel_id=1, source_target_pairs={{8,0},{16,8},{4,12},{24,16},{12,20},{32,24},{20,28},{40,32},{28,36... | collective-permute-start | bytes 393224 | tf_op jit(solution)/shard_map/ppermute | solution.py:48
  63.2 3.9 %collective-permute-start.9 = (bf16[2,256,128]{2,1,0:T(8,128)(2,1)S(1)}, bf16[2,256,128]{2,1,0:T(8,128)(2,1)S(1)}, u32[]{:S(2)}, u32[]{:S(2)}) collective-permute-start(bf16[2,256,128]{2,1,0:T(8,128)(2,1)S(1)} %get-tuple-element.48), channel_id=1, source_target_pairs={{4,0},{0,4},{12,8},{8,12},{20,16},{16,20},{28,24},{24,28},{36,32},... | collective-permute-start | bytes 393224 | tf_op jit(solution)/shard_map/ppermute | solution.py:48
  65.2 11.1 %collective-permute-start.10 = (bf16[2,256,128]{2,1,0:T(8,128)(2,1)S(1)}, bf16[2,256,128]{2,1,0:T(8,128)(2,1)S(1)}, u32[]{:S(2)}, u32[]{:S(2)}) collective-permute-start(bf16[2,256,128]{2,1,0:T(8,128)(2,1)S(1)} %get-tuple-element.50), channel_id=1, source_target_pairs={{12,4},{0,8},{20,12},{8,16},{28,20},{16,24},{36,28},{24,32},{44,36... | collective-permute-start | bytes 393224 | tf_op jit(solution)/shard_map/ppermute | solution.py:48
  76.3 17.7 %collective-permute-start.11 = (bf16[2,2,64,128]{3,2,1,0:T(8,128)(2,1)S(1)}, bf16[2,2,64,128]{3,2,1,0:T(8,128)(2,1)S(1)}, u32[]{:S(2)}, u32[]{:S(2)}) collective-permute-start(bf16[2,2,64,128]{3,2,1,0:T(8,128)(2,1)S(1)} %get-tuple-element.51), channel_id=1, source_target_pairs={{0,1},{1,2},{2,3},{3,0},{4,7},{5,4},{6,5},{7,6},{8,9},{9,10},{10,1... | collective-permute-start | bytes 196616 | tf_op jit(solution)/shard_map/ppermute | solution.py:61
  82.8 14.9 %collective-permute-start.12 = (bf16[2,2,64,128]{3,2,1,0:T(8,128)(2,1)S(1)}, bf16[2,2,64,128]{3,2,1,0:T(8,128)(2,1)S(1)}, u32[]{:S(2)}, u32[]{:S(2)}) collective-permute-start(bf16[2,2,64,128]{3,2,1,0:T(8,128)(2,1)S(1)} %get-tuple-element.55), channel_id=1, source_target_pairs={{0,2},{1,3},{2,0},{3,1},{4,6},{5,7},{6,4},{7,5},{8,10},{9,11},{10,... | collective-permute-start | bytes 196616 | tf_op jit(solution)/shard_map/ppermute | solution.py:61
  87.9 10.8 %collective-permute-start.13 = (bf16[2,2,64,128]{3,2,1,0:T(8,128)(2,1)S(1)}, bf16[2,2,64,128]{3,2,1,0:T(8,128)(2,1)S(1)}, u32[]{:S(2)}, u32[]{:S(2)}) collective-permute-start(bf16[2,2,64,128]{3,2,1,0:T(8,128)(2,1)S(1)} %get-tuple-element.56), channel_id=1, source_target_pairs={{0,3},{1,0},{2,1},{3,2},{4,5},{5,6},{6,7},{7,4},{8,11},{9,8},{10,9... | collective-permute-start | bytes 196616 | tf_op jit(solution)/shard_map/ppermute | solution.py:61

commit v7 on v6

--- a/solution.py
+++ b/solution.py
@@ -61,6 +61,11 @@
     return lax.ppermute(block, ("cp", "tp"), route)
 
 
+def exchange(double, single):
+    came, before = around(double, 1), around(single, 3)
+    return came, around(came[1], 1), before
+
+
 def dot(a, b, contract):
     return lax.dot_general(a, b, (contract, ((), ())), preferred_element_type=jnp.float32)
 
@@ -69,9 +74,15 @@
     return pl.ds(pl.multiple_of(index * size, size), size)
 
 
-def split_kernel(groups, kv_ref, *pieces):
+def views(double_ref, *singles):
+    if len(singles) == 1:
+        return double_ref.at[0], double_ref.at[1], singles[0]
+    return double_ref.at[0], *singles
+
+
+def split_kernel(groups, kv_ref, *refs):
     tp, core = lax.axis_index("tp"), lax.rem(lax.axis_index("cp"), 2)
-    for step, piece in enumerate(pieces, 1):
+    for step, piece in enumerate(views(*refs), 1):
         lanes = aligned(lax.rem(tp + offset(step, core, groups), groups), HD)
         for kind in range(2):
             for block, half in enumerate((core, 1 - core)):
@@ -79,7 +90,7 @@
 
 
 def join_kernel(groups, kv_ref, *refs):
-    pieces, outs = refs[:-3], refs[-2:]
+    pieces, outs = views(*refs[:-3]), refs[-2:]
     tp, core = lax.axis_index("tp"), lax.rem(lax.axis_index("cp"), 2)
     rows = kv_ref.shape[3]
     for kind in range(2):
@@ -92,7 +103,7 @@
 
 
 def total_kernel(groups, *refs):
-    terms, pieces = (refs[:3], refs[3:5]), refs[5:]
+    terms, pieces = (refs[:3], refs[3:5]), (refs[5], *views(*refs[6:]))
     tp, core = lax.axis_index("tp"), lax.rem(lax.axis_index("cp"), 2)
     rows = pieces[0].shape[2]
     for step, piece in enumerate(pieces):
@@ -105,7 +116,7 @@
 
 
 def place_kernel(groups, *refs):
-    pieces, outs = refs[:-3], refs[-2:]
+    pieces, outs = (refs[0], *views(*refs[1:-3])), refs[-2:]
     tp, core = lax.axis_index("tp"), lax.rem(lax.axis_index("cp"), 2)
     for step, piece in enumerate(pieces):
         lanes = aligned(lax.rem(tp - offset(step, core, groups) + groups, groups), HD)
@@ -286,18 +297,18 @@
     rows = keys.shape[2]
     bf = jnp.bfloat16
     shape = jax.ShapeDtypeStruct
-    piece = shape((2, 2, rows, HD), bf)
+    piece, double = shape((2, 2, rows, HD), bf), shape((2, 2, 2, rows, HD), bf)
 
     kv = jnp.stack([keys, values])
     sent = pl.pallas_call(
         functools.partial(split_kernel, groups),
-        out_shape=[piece] * (groups - 1),
+        out_shape=[double, piece],
         in_specs=[VMEM],
-        out_specs=[VMEM] * (groups - 1),
+        out_specs=[VMEM] * 2,
         compiler_params=SMALL,
         name="split",
     )(kv)
-    came = [around(block, step) for step, block in enumerate(sent, 1)]
+    came = exchange(*sent)
     qg, bias = pl.pallas_call(
         functools.partial(prepare_kernel, contexts),
         out_shape=[shape((2, 2, side, width), bf), shape((2, side, 2 * side), jnp.float32)],
@@ -367,15 +378,15 @@
         name="query",
     )(ds_x, *x_line, ds_y, *y_line)
 
-    pieces = pl.pallas_call(
+    kept, *sent = pl.pallas_call(
         functools.partial(total_kernel, groups),
-        out_shape=[piece] * groups,
+        out_shape=[piece, double, piece],
         in_specs=[VMEM] * 5,
-        out_specs=[VMEM] * groups,
+        out_specs=[VMEM] * 3,
         compiler_params=SMALL,
         name="total",
     )(*terms[0], *terms[1])
-    returned = [pieces[0]] + [around(block, step) for step, block in enumerate(pieces[1:], 1)]
+    returned = exchange(*sent)
     attn_out, q_grad, filled = pl.pallas_call(
         fill_kernel,
         out_shape=[shape(queries.shape, bf)] * 2 + [shape((8, HD), jnp.float32)],
@@ -387,7 +398,7 @@
             flops=0, bytes_accessed=16 * side * width, transcendentals=0
         ),
         name="fill",
-    )(attn_x, attn_y, dq_x, dq_y, returned[1])
+    )(attn_x, attn_y, dq_x, dq_y, returned[2])
     k_grad, v_grad = pl.pallas_call(
         functools.partial(place_kernel, groups),
         out_shape=[shape(keys.shape, bf)] * 2,
@@ -395,7 +406,7 @@
         out_specs=[VMEM] * 2,
         compiler_params=SMALL,
         name="place",
-    )(*returned, filled)
+    )(kept, *returned, filled)
     return (attn_out, q_grad, k_grad, v_grad)
 
 

time: 100 us -> 105 us (1.050)
  the two profiles are of different devices: /device:TPU:64 before, /device:TPU:32 now
where the time goes in v7:
time: 105 us
  starting transfers between devices  62 us (59%)
  waiting for transfers between devices  24.5 us (23%)
  Pallas kernels  13.2 us (13%)
  local copies, waits for them, and re-layouts  3.13 us (3%)
    ppermute x6, starting transfers between devices, around(): return lax.ppermute(block, ('cp', 'tp'), route)  31 us
    ppermute x8, starting transfers between devices, move(): return lax.ppermute(block, 'cp', route)  30.9 us
    ppermute x6, waiting for transfers between devices, around(): return lax.ppermute(block, ('cp', 'tp'), route)  15.3 us
    ppermute x8, waiting for transfers between devices, move(): return lax.ppermute(block, 'cp', route)  9.15 us
    pallas_call x2, Pallas kernels, attend(): pl.pallas_call(functools.partial(attend_kernel, turn), in_specs=[VMEM] *...  8.65 us
    unnamed x6, local copies, waits for them, and re-layouts  3.12 us
  transfers between devices with their start and end apart: 14, of which 5 were waited for; matrix products, arithmetic and copies ran while one was open for 0% of the time, Pallas kernels for 12%

profile of v7, /device:TPU:32, one launch (start us, length us, event | category | flops | bytes accessed | tf_op | source)
XLA Modules:
  0.0 104.6 jit_solution(11397492730725171809)
XLA Ops:
  0.6 1.0 pad_maximum_fusion.kv_ref
  1.6 0.1 split.1
  1.7 9.1 %collective-permute-start = (bf16[2,2,2,64,128]{4,3,2,1,0:T(8,128)(2,1)S(1)}, bf16[2,2,2,64,128]{4,3,2,1,0:T(8,128)(2,1)S(1)}, u32[]{:S(2)}, u32[]{:S(2)}) collective-permute-start(bf16[2,2,2,64,128]{4,3,2,1,0:T(8,128)(2,1)S(1)} %get-tuple-element.31), channel_id=1, source_target_pairs={{0,1},{1,2},{2,3},{3,0},{4,7},{5,4},{6,5},{7,6},{8,9},{9,10},{10,1... | collective-permute-start | bytes 393224 | tf_op jit(solution)/shard_map/ppermute | solution.py:61
  10.8 4.7 %collective-permute-start.2 = (bf16[2,2,64,128]{3,2,1,0:T(8,128)(2,1)S(1)}, bf16[2,2,64,128]{3,2,1,0:T(8,128)(2,1)S(1)}, u32[]{:S(2)}, u32[]{:S(2)}) collective-permute-start(bf16[2,2,64,128]{3,2,1,0:T(8,128)(2,1)S(1)} %get-tuple-element.32), channel_id=1, source_target_pairs={{0,3},{1,0},{2,1},{3,2},{4,5},{5,6},{6,7},{7,4},{8,11},{9,8},{10,9... | collective-permute-start | bytes 196616 | tf_op jit(solution)/shard_map/ppermute | solution.py:61
  15.5 2.6 %collective-permute-done.refs_0_ = bf16[2,2,2,64,128]{4,3,2,1,0:T(8,128)(2,1)S(1)} collective-permute-done((bf16[2,2,2,64,128]{4,3,2,1,0:T(8,128)(2,1)S(1)}, bf16[2,2,2,64,128]{4,3,2,1,0:T(8,128)(2,1)S(1)}, u32[]{:S(2)}, u32[]{:S(2)}) %collective-permute-start) | collective-permute-done | bytes 131104 | tf_op jit(solution)/shard_map/ppermute | solution.py:61
  18.1 5.6 %collective-permute-start.1 = (bf16[2,2,64,128]{3,2,1,0:T(8,128)(2,1)S(1)}, bf16[2,2,64,128]{3,2,1,0:T(8,128)(2,1)S(1)}, u32[]{:S(2)}, u32[]{:S(2)}) collective-permute-start(bf16[2,2,64,128]{3,2,1,0:T(8,128)(2,1)S(1)} %slice_bitcast_fusion.1), channel_id=1, source_target_pairs={{0,1},{1,2},{2,3},{3,0},{4,7},{5,4},{6,5},{7,6},{8,9},{9,10},{10,1... | collective-permute-start | bytes 196616 | tf_op jit(solution)/shard_map/ppermute | solution.py:61
  23.7 0.0 copy-start
  23.7 1.2 %copy-done = bf16[2,1,256,1024]{3,2,1,0:T(8,128)(2,1)S(1)} copy-done((bf16[2,1,256,1024]{3,2,1,0:T(8,128)(2,1)S(1)}, bf16[2,1,256,1024]{3,2,1,0:T(8,128)(2,1)}, u32[]{:S(2)}) %copy-start) | copy-done | bytes 1048600
  24.9 0.0 copy-start.1
  24.9 1.2 %copy-done.1 = bf16[2,1,256,1024]{3,2,1,0:T(8,128)(2,1)S(1)} copy-done((bf16[2,1,256,1024]{3,2,1,0:T(8,128)(2,1)S(1)}, bf16[2,1,256,1024]{3,2,1,0:T(8,128)(2,1)}, u32[]{:S(2)}) %copy-start.1) | copy-done | bytes 1048600
  26.2 0.0 copy-start.2
  26.2 0.7 copy-done.2
  26.8 0.5 prepare.1
  27.3 0.0 collective-permute-done.2.refs_2_
  27.3 2.9 %collective-permute-done.1.refs_1_ = bf16[2,2,64,128]{3,2,1,0:T(8,128)(2,1)S(1)} collective-permute-done((bf16[2,2,64,128]{3,2,1,0:T(8,128)(2,1)S(1)}, bf16[2,2,64,128]{3,2,1,0:T(8,128)(2,1)S(1)}, u32[]{:S(2)}, u32[]{:S(2)}) %collective-permute-start.1) | collective-permute-done | bytes 65568 | tf_op jit(solution)/shard_map/ppermute | solution.py:61
  30.3 3.4 %collective-permute-start.3 = (bf16[2,256,128]{2,1,0:T(8,128)(2,1)S(1)}, bf16[2,256,128]{2,1,0:T(8,128)(2,1)S(1)}, u32[]{:S(2)}, u32[]{:S(2)}) collective-permute-start(bf16[2,256,128]{2,1,0:T(8,128)(2,1)S(1)} %get-tuple-element.34.here_ref.refs_3_), channel_id=1, source_target_pairs={{0,8},{8,16},{12,4},{16,24},{20,12},{24,32},{28,20},{32,40},{36,28... | collective-permute-start | bytes 393224 | tf_op jit(solution)/shard_map/ppermute | solution.py:48
  33.7 9.6 %collective-permute-start.4 = (bf16[2,256,128]{2,1,0:T(8,128)(2,1)S(1)}, bf16[2,256,128]{2,1,0:T(8,128)(2,1)S(1)}, u32[]{:S(2)}, u32[]{:S(2)}) collective-permute-start(bf16[2,256,128]{2,1,0:T(8,128)(2,1)S(1)} %get-tuple-element.35.here_ref.refs_7_), channel_id=1, source_target_pairs={{4,8},{8,4},{12,16},{16,12},{20,24},{24,20},{28,32},{32,28},{36,40... | collective-permute-start | bytes 393224 | tf_op jit(solution)/shard_map/ppermute | solution.py:48
  43.3 1.9 %collective-permute-start.6 = (bf16[2,256,128]{2,1,0:T(8,128)(2,1)S(1)}, bf16[2,256,128]{2,1,0:T(8,128)(2,1)S(1)}, u32[]{:S(2)}, u32[]{:S(2)}) collective-permute-start(bf16[2,256,128]{2,1,0:T(8,128)(2,1)S(1)} %get-tuple-element.34.here_ref.refs_3_), channel_id=1, source_target_pairs={{0,4},{4,0},{8,12},{12,8},{16,20},{20,16},{24,28},{28,24},{32,36},... | collective-permute-start | bytes 393224 | tf_op jit(solution)/shard_map/ppermute | solution.py:48
  45.3 2.4 %collective-permute-start.5 = (bf16[2,256,128]{2,1,0:T(8,128)(2,1)S(1)}, bf16[2,256,128]{2,1,0:T(8,128)(2,1)S(1)}, u32[]{:S(2)}, u32[]{:S(2)}) collective-permute-start(bf16[2,256,128]{2,1,0:T(8,128)(2,1)S(1)} %get-tuple-element.35.here_ref.refs_7_), channel_id=1, source_target_pairs={{4,12},{8,0},{12,20},{16,8},{20,28},{24,16},{28,36},{32,24},{36,44... | collective-permute-start | bytes 393224 | tf_op jit(solution)/shard_map/ppermute | solution.py:48
  47.7 0.0 collective-permute-done.3.oldest_ref.refs_1_
  47.7 0.0 collective-permute-done.4.middle_ref.refs_2_
  47.7 4.3 %attend.2 = (bf16[256,1024]{1,0:T(8,128)(2,1)S(1)}, bf16[8,256,768]{2,1,0:T(8,128)(2,1)S(1)}, bf16[2,256,128]{2,1,0:T(8,128)(2,1)S(1)}, bf16[2,256,128]{2,1,0:T(8,128)(2,1)S(1)}, f32[2,256,128]{2,1,0:T(8,128)S(1)}) custom-call(bf16[2,2,256,1024]{3,2,1,0:T(8,128)(2,1)S(1)} %get-tuple-element.30.qg_ref, ...), custom_call_target="tpu_custom_call" | custom-call | flops 2013265920 | bytes 1572864 | tf_op jit(solution)/shard_map/attend/pallas_call | solution.py:341
  52.1 2.8 %collective-permute-start.7 = (bf16[2,256,128]{2,1,0:T(8,128)(2,1)S(1)}, bf16[2,256,128]{2,1,0:T(8,128)(2,1)S(1)}, u32[]{:S(2)}, u32[]{:S(2)}) collective-permute-start(bf16[2,256,128]{2,1,0:T(8,128)(2,1)S(1)} %get-tuple-element.37), channel_id=1, source_target_pairs={{4,0},{0,4},{12,8},{8,12},{20,16},{16,20},{28,24},{24,28},{36,32},... | collective-permute-start | bytes 393224 | tf_op jit(solution)/shard_map/ppermute | solution.py:48
  54.9 7.0 %collective-permute-start.8 = (bf16[2,256,128]{2,1,0:T(8,128)(2,1)S(1)}, bf16[2,256,128]{2,1,0:T(8,128)(2,1)S(1)}, u32[]{:S(2)}, u32[]{:S(2)}) collective-permute-start(bf16[2,256,128]{2,1,0:T(8,128)(2,1)S(1)} %get-tuple-element.44), channel_id=1, source_target_pairs={{8,0},{16,8},{4,12},{24,16},{12,20},{32,24},{20,28},{40,32},{28,36... | collective-permute-start | bytes 393224 | tf_op jit(solution)/shard_map/ppermute | solution.py:48
  61.8 0.0 collective-permute-done.6.middle_ref.refs_6_
  61.8 0.0 collective-permute-done.5.oldest_ref.refs_5_
  61.8 0.0 collective-permute-done.7.refs_0_
  61.9 4.3 %attend.3 = (bf16[256,1024]{1,0:T(8,128)(2,1)S(1)}, bf16[8,256,768]{2,1,0:T(8,128)(2,1)S(1)}, bf16[2,256,128]{2,1,0:T(8,128)(2,1)S(1)}, bf16[2,256,128]{2,1,0:T(8,128)(2,1)S(1)}, f32[2,256,128]{2,1,0:T(8,128)S(1)}) custom-call(bf16[2,2,256,1024]{3,2,1,0:T(8,128)(2,1)S(1)} %get-tuple-element.30.qg_ref, ...), custom_call_target="tpu_custom_call" | custom-call | flops 2013265920 | bytes 1572864 | tf_op jit(solution)/shard_map/attend/pallas_call | solution.py:341
  66.2 1.9 %collective-permute-start.9 = (bf16[2,256,128]{2,1,0:T(8,128)(2,1)S(1)}, bf16[2,256,128]{2,1,0:T(8,128)(2,1)S(1)}, u32[]{:S(2)}, u32[]{:S(2)}) collective-permute-start(bf16[2,256,128]{2,1,0:T(8,128)(2,1)S(1)} %get-tuple-element.45), channel_id=1, source_target_pairs={{4,0},{0,4},{12,8},{8,12},{20,16},{16,20},{28,24},{24,28},{36,32},... | collective-permute-start | bytes 393224 | tf_op jit(solution)/shard_map/ppermute | solution.py:48
  68.1 1.9 %collective-permute-start.10 = (bf16[2,256,128]{2,1,0:T(8,128)(2,1)S(1)}, bf16[2,256,128]{2,1,0:T(8,128)(2,1)S(1)}, u32[]{:S(2)}, u32[]{:S(2)}) collective-permute-start(bf16[2,256,128]{2,1,0:T(8,128)(2,1)S(1)} %get-tuple-element.47), channel_id=1, source_target_pairs={{12,4},{0,8},{20,12},{8,16},{28,20},{16,24},{36,28},{24,32},{44,36... | collective-permute-start | bytes 393224 | tf_op jit(solution)/shard_map/ppermute | solution.py:48
  70.0 0.0 collective-permute-done.8.refs_1_
  70.0 0.0 collective-permute-done.9.refs_2_
  70.1 9.1 %collective-permute-done.10.refs_4_ = bf16[2,256,128]{2,1,0:T(8,128)(2,1)S(1)} collective-permute-done((bf16[2,256,128]{2,1,0:T(8,128)(2,1)S(1)}, bf16[2,256,128]{2,1,0:T(8,128)(2,1)S(1)}, u32[]{:S(2)}, u32[]{:S(2)}) %collective-permute-start.10) | collective-permute-done | bytes 131104 | tf_op jit(solution)/shard_map/ppermute | solution.py:48
  79.2 0.1 total.1
  79.3 2.1 %collective-permute-start.12 = (bf16[2,2,2,64,128]{4,3,2,1,0:T(8,128)(2,1)S(1)}, bf16[2,2,2,64,128]{4,3,2,1,0:T(8,128)(2,1)S(1)}, u32[]{:S(2)}, u32[]{:S(2)}) collective-permute-start(bf16[2,2,2,64,128]{4,3,2,1,0:T(8,128)(2,1)S(1)} %get-tuple-element.52), channel_id=1, source_target_pairs={{0,1},{1,2},{2,3},{3,0},{4,7},{5,4},{6,5},{7,6},{8,9},{9,10},{10,1... | collective-permute-start | bytes 393224 | tf_op jit(solution)/shard_map/ppermute | solution.py:61
  81.3 7.7 %collective-permute-start.11 = (bf16[2,2,64,128]{3,2,1,0:T(8,128)(2,1)S(1)}, bf16[2,2,64,128]{3,2,1,0:T(8,128)(2,1)S(1)}, u32[]{:S(2)}, u32[]{:S(2)}) collective-permute-start(bf16[2,2,64,128]{3,2,1,0:T(8,128)(2,1)S(1)} %get-tuple-element.48), channel_id=1, source_target_pairs={{0,3},{1,0},{2,1},{3,2},{4,5},{5,6},{6,7},{7,4},{8,11},{9,8},{10,9... | collective-permute-start | bytes 196616 | tf_op jit(solution)/shard_map/ppermute | solution.py:61
  89.0 4.8 %collective-permute-done.12.refs_1_ = bf16[2,2,2,64,128]{4,3,2,1,0:T(8,128)(2,1)S(1)} collective-permute-done((bf16[2,2,2,64,128]{4,3,2,1,0:T(8,128)(2,1)S(1)}, bf16[2,2,2,64,128]{4,3,2,1,0:T(8,128)(2,1)S(1)}, u32[]{:S(2)}, u32[]{:S(2)}) %collective-permute-start.12) | collective-permute-done | bytes 131104 | tf_op jit(solution)/shard_map/ppermute | solution.py:61
  93.8 1.9 %collective-permute-start.13 = (bf16[2,2,64,128]{3,2,1,0:T(8,128)(2,1)S(1)}, bf16[2,2,64,128]{3,2,1,0:T(8,128)(2,1)S(1)}, u32[]{:S(2)}, u32[]{:S(2)}) collective-permute-start(bf16[2,2,64,128]{3,2,1,0:T(8,128)(2,1)S(1)} %slice_bitcast_fusion), channel_id=1, source_target_pairs={{0,1},{1,2},{2,3},{3,0},{4,7},{5,4},{6,5},{7,6},{8,9},{9,10},{10,1... | collective-permute-start | bytes 196616 | tf_op jit(solution)/shard_map/ppermute | solution.py:61
  95.7 1.8 %query.1 = (bf16[256,1024]{1,0:T(8,128)(2,1)S(1)}, bf16[256,1024]{1,0:T(8,128)(2,1)S(1)}) custom-call(bf16[8,256,768]{2,1,0:T(8,128)(2,1)S(1)} %get-tuple-element.39.refs_0_, bf16[2,256,128]{2,1,0:T(8,128)(2,1)S(1)} %collective-permute-done.3.oldest_ref.refs_1_, bf16[2,256,128]{2,1,0:T(8,128)(2,1)S(1)} %collective-permute-done.4.middle_ref.refs_2_, ...), custom_call_target="tpu_custom_call" | custom-call | flops 805306368 | bytes 6291456 | tf_op jit(solution)/shard_map/query/pallas_call | solution.py:369
  97.5 0.0 collective-permute-done.11.refs_4_.refs_3_
  97.6 1.4 %fill.1 = (bf16[2,1,256,1024]{3,2,1,0:T(8,128)(2,1)}, bf16[2,1,256,1024]{3,2,1,0:T(8,128)(2,1)}, f32[8,128]{1,0:T(8,128)S(1)}) custom-call(bf16[256,1024]{1,0:T(8,128)(2,1)S(1)} %get-tuple-element.36.refs_0_, bf16[256,1024]{1,0:T(8,128)(2,1)S(1)} %get-tuple-element.38.refs_1_, bf16[256,1024]{1,0:T(8,128)(2,1)S(1)} %get-tuple-element.41.refs_2_, ...), custom_call_target="tpu_custom_call" | custom-call | bytes 4194304 | tf_op jit(solution)/shard_map/fill/pallas_call | solution.py:390
  98.9 5.0 %collective-permute-done.13.refs_2_ = bf16[2,2,64,128]{3,2,1,0:T(8,128)(2,1)S(1)} collective-permute-done((bf16[2,2,64,128]{3,2,1,0:T(8,128)(2,1)S(1)}, bf16[2,2,64,128]{3,2,1,0:T(8,128)(2,1)S(1)}, u32[]{:S(2)}, u32[]{:S(2)}) %collective-permute-start.13) | collective-permute-done | bytes 65568 | tf_op jit(solution)/shard_map/ppermute | solution.py:61
  103.9 0.8 place.1
  (3 shorter events, 0.0 us)
Async XLA Ops:
  1.7 16.4 %collective-permute-start = (bf16[2,2,2,64,128]{4,3,2,1,0:T(8,128)(2,1)S(1)}, bf16[2,2,2,64,128]{4,3,2,1,0:T(8,128)(2,1)S(1)}, u32[]{:S(2)}, u32[]{:S(2)}) collective-permute-start(bf16[2,2,2,64,128]{4,3,2,1,0:T(8,128)(2,1)S(1)} %get-tuple-element.31), channel_id=1, source_target_pairs={{0,1},{1,2},{2,3},{3,0},{4,7},{5,4},{6,5},{7,6},{8,9},{9,10},{10,1... | collective-permute-start | bytes 393224 | tf_op jit(solution)/shard_map/ppermute | solution.py:61
  10.8 16.5 %collective-permute-start.2 = (bf16[2,2,64,128]{3,2,1,0:T(8,128)(2,1)S(1)}, bf16[2,2,64,128]{3,2,1,0:T(8,128)(2,1)S(1)}, u32[]{:S(2)}, u32[]{:S(2)}) collective-permute-start(bf16[2,2,64,128]{3,2,1,0:T(8,128)(2,1)S(1)} %get-tuple-element.32), channel_id=1, source_target_pairs={{0,3},{1,0},{2,1},{3,2},{4,5},{5,6},{6,7},{7,4},{8,11},{9,8},{10,9... | collective-permute-start | bytes 196616 | tf_op jit(solution)/shard_map/ppermute | solution.py:61
  18.1 12.2 %collective-permute-start.1 = (bf16[2,2,64,128]{3,2,1,0:T(8,128)(2,1)S(1)}, bf16[2,2,64,128]{3,2,1,0:T(8,128)(2,1)S(1)}, u32[]{:S(2)}, u32[]{:S(2)}) collective-permute-start(bf16[2,2,64,128]{3,2,1,0:T(8,128)(2,1)S(1)} %slice_bitcast_fusion.1), channel_id=1, source_target_pairs={{0,1},{1,2},{2,3},{3,0},{4,7},{5,4},{6,5},{7,6},{8,9},{9,10},{10,1... | collective-permute-start | bytes 196616 | tf_op jit(solution)/shard_map/ppermute | solution.py:61
  23.7 1.2 %copy-start = (bf16[2,1,256,1024]{3,2,1,0:T(8,128)(2,1)S(1)}, bf16[2,1,256,1024]{3,2,1,0:T(8,128)(2,1)}, u32[]{:S(2)}) copy-start(bf16[2,1,256,1024]{3,2,1,0:T(8,128)(2,1)} %q_ref.1) | copy-start | bytes 3145732
  24.9 1.2 %copy-start.1 = (bf16[2,1,256,1024]{3,2,1,0:T(8,128)(2,1)S(1)}, bf16[2,1,256,1024]{3,2,1,0:T(8,128)(2,1)}, u32[]{:S(2)}) copy-start(bf16[2,1,256,1024]{3,2,1,0:T(8,128)(2,1)} %g_ref.1) | copy-start | bytes 3145732
  26.2 0.7 copy-start.2
  30.3 17.4 %collective-permute-start.3 = (bf16[2,256,128]{2,1,0:T(8,128)(2,1)S(1)}, bf16[2,256,128]{2,1,0:T(8,128)(2,1)S(1)}, u32[]{:S(2)}, u32[]{:S(2)}) collective-permute-start(bf16[2,256,128]{2,1,0:T(8,128)(2,1)S(1)} %get-tuple-element.34.here_ref.refs_3_), channel_id=1, source_target_pairs={{0,8},{8,16},{12,4},{16,24},{20,12},{24,32},{28,20},{32,40},{36,28... | collective-permute-start | bytes 393224 | tf_op jit(solution)/shard_map/ppermute | solution.py:48
  33.7 14.0 %collective-permute-start.4 = (bf16[2,256,128]{2,1,0:T(8,128)(2,1)S(1)}, bf16[2,256,128]{2,1,0:T(8,128)(2,1)S(1)}, u32[]{:S(2)}, u32[]{:S(2)}) collective-permute-start(bf16[2,256,128]{2,1,0:T(8,128)(2,1)S(1)} %get-tuple-element.35.here_ref.refs_7_), channel_id=1, source_target_pairs={{4,8},{8,4},{12,16},{16,12},{20,24},{24,20},{28,32},{32,28},{36,40... | collective-permute-start | bytes 393224 | tf_op jit(solution)/shard_map/ppermute | solution.py:48
  43.3 18.5 %collective-permute-start.6 = (bf16[2,256,128]{2,1,0:T(8,128)(2,1)S(1)}, bf16[2,256,128]{2,1,0:T(8,128)(2,1)S(1)}, u32[]{:S(2)}, u32[]{:S(2)}) collective-permute-start(bf16[2,256,128]{2,1,0:T(8,128)(2,1)S(1)} %get-tuple-element.34.here_ref.refs_3_), channel_id=1, source_target_pairs={{0,4},{4,0},{8,12},{12,8},{16,20},{20,16},{24,28},{28,24},{32,36},... | collective-permute-start | bytes 393224 | tf_op jit(solution)/shard_map/ppermute | solution.py:48
  45.3 16.6 %collective-permute-start.5 = (bf16[2,256,128]{2,1,0:T(8,128)(2,1)S(1)}, bf16[2,256,128]{2,1,0:T(8,128)(2,1)S(1)}, u32[]{:S(2)}, u32[]{:S(2)}) collective-permute-start(bf16[2,256,128]{2,1,0:T(8,128)(2,1)S(1)} %get-tuple-element.35.here_ref.refs_7_), channel_id=1, source_target_pairs={{4,12},{8,0},{12,20},{16,8},{20,28},{24,16},{28,36},{32,24},{36,44... | collective-permute-start | bytes 393224 | tf_op jit(solution)/shard_map/ppermute | solution.py:48
  52.1 9.8 %collective-permute-start.7 = (bf16[2,256,128]{2,1,0:T(8,128)(2,1)S(1)}, bf16[2,256,128]{2,1,0:T(8,128)(2,1)S(1)}, u32[]{:S(2)}, u32[]{:S(2)}) collective-permute-start(bf16[2,256,128]{2,1,0:T(8,128)(2,1)S(1)} %get-tuple-element.37), channel_id=1, source_target_pairs={{4,0},{0,4},{12,8},{8,12},{20,16},{16,20},{28,24},{24,28},{36,32},... | collective-permute-start | bytes 393224 | tf_op jit(solution)/shard_map/ppermute | solution.py:48
  54.9 15.2 %collective-permute-start.8 = (bf16[2,256,128]{2,1,0:T(8,128)(2,1)S(1)}, bf16[2,256,128]{2,1,0:T(8,128)(2,1)S(1)}, u32[]{:S(2)}, u32[]{:S(2)}) collective-permute-start(bf16[2,256,128]{2,1,0:T(8,128)(2,1)S(1)} %get-tuple-element.44), channel_id=1, source_target_pairs={{8,0},{16,8},{4,12},{24,16},{12,20},{32,24},{20,28},{40,32},{28,36... | collective-permute-start | bytes 393224 | tf_op jit(solution)/shard_map/ppermute | solution.py:48
  66.2 3.9 %collective-permute-start.9 = (bf16[2,256,128]{2,1,0:T(8,128)(2,1)S(1)}, bf16[2,256,128]{2,1,0:T(8,128)(2,1)S(1)}, u32[]{:S(2)}, u32[]{:S(2)}) collective-permute-start(bf16[2,256,128]{2,1,0:T(8,128)(2,1)S(1)} %get-tuple-element.45), channel_id=1, source_target_pairs={{4,0},{0,4},{12,8},{8,12},{20,16},{16,20},{28,24},{24,28},{36,32},... | collective-permute-start | bytes 393224 | tf_op jit(solution)/shard_map/ppermute | solution.py:48
  68.1 11.1 %collective-permute-start.10 = (bf16[2,256,128]{2,1,0:T(8,128)(2,1)S(1)}, bf16[2,256,128]{2,1,0:T(8,128)(2,1)S(1)}, u32[]{:S(2)}, u32[]{:S(2)}) collective-permute-start(bf16[2,256,128]{2,1,0:T(8,128)(2,1)S(1)} %get-tuple-element.47), channel_id=1, source_target_pairs={{12,4},{0,8},{20,12},{8,16},{28,20},{16,24},{36,28},{24,32},{44,36... | collective-permute-start | bytes 393224 | tf_op jit(solution)/shard_map/ppermute | solution.py:48
  79.3 14.6 %collective-permute-start.12 = (bf16[2,2,2,64,128]{4,3,2,1,0:T(8,128)(2,1)S(1)}, bf16[2,2,2,64,128]{4,3,2,1,0:T(8,128)(2,1)S(1)}, u32[]{:S(2)}, u32[]{:S(2)}) collective-permute-start(bf16[2,2,2,64,128]{4,3,2,1,0:T(8,128)(2,1)S(1)} %get-tuple-element.52), channel_id=1, source_target_pairs={{0,1},{1,2},{2,3},{3,0},{4,7},{5,4},{6,5},{7,6},{8,9},{9,10},{10,1... | collective-permute-start | bytes 393224 | tf_op jit(solution)/shard_map/ppermute | solution.py:61
  81.3 16.2 %collective-permute-start.11 = (bf16[2,2,64,128]{3,2,1,0:T(8,128)(2,1)S(1)}, bf16[2,2,64,128]{3,2,1,0:T(8,128)(2,1)S(1)}, u32[]{:S(2)}, u32[]{:S(2)}) collective-permute-start(bf16[2,2,64,128]{3,2,1,0:T(8,128)(2,1)S(1)} %get-tuple-element.48), channel_id=1, source_target_pairs={{0,3},{1,0},{2,1},{3,2},{4,5},{5,6},{6,7},{7,4},{8,11},{9,8},{10,9... | collective-permute-start | bytes 196616 | tf_op jit(solution)/shard_map/ppermute | solution.py:61
  93.8 10.1 %collective-permute-start.13 = (bf16[2,2,64,128]{3,2,1,0:T(8,128)(2,1)S(1)}, bf16[2,2,64,128]{3,2,1,0:T(8,128)(2,1)S(1)}, u32[]{:S(2)}, u32[]{:S(2)}) collective-permute-start(bf16[2,2,64,128]{3,2,1,0:T(8,128)(2,1)S(1)} %slice_bitcast_fusion), channel_id=1, source_target_pairs={{0,1},{1,2},{2,3},{3,0},{4,7},{5,4},{6,5},{7,6},{8,9},{9,10},{10,1... | collective-permute-start | bytes 196616 | tf_op jit(solution)/shard_map/ppermute | solution.py:61

commit v8 on v7

--- a/solution.py
+++ b/solution.py
@@ -48,22 +48,22 @@
     return lax.ppermute(block, "cp", route)
 
 
-def offset(step, core, groups):
-    return jnp.where(core == 0, step, groups - step)
-
-
-def around(block, step):
+def apart(step, core):
+    return step if step == 2 else jnp.where(core == 0, step, 4 - step)
+
+
+def swap(block, step):
     contexts, groups = lax.axis_size("cp"), lax.axis_size("tp")
     route = []
     for i in range(contexts):
-        turn = step if i % 2 == 0 else groups - step
-        route += [(i * groups + t, i * groups + (t + turn) % groups) for t in range(groups)]
+        bits = step if i % 2 == 0 else 4 - step
+        route += [(i * groups + t, i * groups + (t ^ bits)) for t in range(groups)]
     return lax.ppermute(block, ("cp", "tp"), route)
 
 
 def exchange(double, single):
-    came, before = around(double, 1), around(single, 3)
-    return came, around(came[1], 1), before
+    first = swap(double, 1)
+    return first, swap(jnp.stack([single, first[1]]), 3)
 
 
 def dot(a, b, contract):
@@ -74,40 +74,42 @@
     return pl.ds(pl.multiple_of(index * size, size), size)
 
 
-def views(double_ref, *singles):
-    if len(singles) == 1:
-        return double_ref.at[0], double_ref.at[1], singles[0]
-    return double_ref.at[0], *singles
-
-
-def split_kernel(groups, kv_ref, *refs):
+def leaving(double_ref, single_ref):
+    return double_ref.at[0], double_ref.at[1], single_ref
+
+
+def arriving(first_ref, second_ref):
+    return first_ref.at[0], second_ref.at[1], second_ref.at[0]
+
+
+def split_kernel(kv_ref, *refs):
     tp, core = lax.axis_index("tp"), lax.rem(lax.axis_index("cp"), 2)
-    for step, piece in enumerate(views(*refs), 1):
-        lanes = aligned(lax.rem(tp + offset(step, core, groups), groups), HD)
+    for step, piece in enumerate(leaving(*refs), 1):
+        lanes = aligned(tp ^ apart(step, core), HD)
         for kind in range(2):
             for block, half in enumerate((core, 1 - core)):
                 piece[block, kind] = kv_ref[kind, half, 0, :, lanes]
 
 
-def join_kernel(groups, kv_ref, *refs):
-    pieces, outs = views(*refs[:-3]), refs[-2:]
+def join_kernel(kv_ref, *refs):
+    pieces, outs = arriving(*refs[:-3]), refs[-2:]
     tp, core = lax.axis_index("tp"), lax.rem(lax.axis_index("cp"), 2)
     rows = kv_ref.shape[3]
     for kind in range(2):
         for half, out in zip((core, 1 - core), outs):
             out[kind, aligned(tp, rows), :] = kv_ref[kind, half, 0, :, aligned(tp, HD)]
     for step, piece in enumerate(pieces, 1):
-        source = lax.rem(tp - offset(step, core, groups) + groups, groups)
+        source = tp ^ apart(step, core)
         for block, out in enumerate(outs):
             out[:, aligned(source, rows), :] = piece[block]
 
 
-def total_kernel(groups, *refs):
-    terms, pieces = (refs[:3], refs[3:5]), (refs[5], *views(*refs[6:]))
+def total_kernel(*refs):
+    terms, pieces = (refs[:3], refs[3:5]), (refs[5], *leaving(*refs[6:]))
     tp, core = lax.axis_index("tp"), lax.rem(lax.axis_index("cp"), 2)
     rows = pieces[0].shape[2]
     for step, piece in enumerate(pieces):
-        place = aligned(lax.rem(tp + offset(step, core, groups), groups), rows)
+        place = aligned(tp if step == 0 else tp ^ apart(step, core), rows)
         for block in range(2):
             own, *came = [ref[:, place, :] for ref in terms[block]]
             for term in came:
@@ -115,11 +117,11 @@
             piece[block] = own.astype(piece.dtype)
 
 
-def place_kernel(groups, *refs):
-    pieces, outs = (refs[0], *views(*refs[1:-3])), refs[-2:]
+def place_kernel(*refs):
+    pieces, outs = (refs[0], *arriving(*refs[1:-3])), refs[-2:]
     tp, core = lax.axis_index("tp"), lax.rem(lax.axis_index("cp"), 2)
     for step, piece in enumerate(pieces):
-        lanes = aligned(lax.rem(tp - offset(step, core, groups) + groups, groups), HD)
+        lanes = aligned(tp if step == 0 else tp ^ apart(step, core), HD)
         for block, half in enumerate((core, 1 - core)):
             for kind, out in enumerate(outs):
                 out[half, 0, :, lanes] = piece[block, kind]
@@ -293,7 +295,7 @@
 
 def local(queries, keys, values, out_grad, doc_lengths):
     side, width = queries.shape[2], queries.shape[3]
-    contexts, groups = lax.axis_size("cp"), lax.axis_size("tp")
+    contexts = lax.axis_size("cp")
     rows = keys.shape[2]
     bf = jnp.bfloat16
     shape = jax.ShapeDtypeStruct
@@ -301,7 +303,7 @@
 
     kv = jnp.stack([keys, values])
     sent = pl.pallas_call(
-        functools.partial(split_kernel, groups),
+        split_kernel,
         out_shape=[double, piece],
         in_specs=[VMEM],
         out_specs=[VMEM] * 2,
@@ -323,9 +325,9 @@
     )(queries, out_grad, doc_lengths[None, :])
     block = shape((2, side, HD), bf)
     x, y = pl.pallas_call(
-        functools.partial(join_kernel, groups),
+        join_kernel,
         out_shape=[block] * 2,
-        in_specs=[VMEM] * groups + [ANY],
+        in_specs=[VMEM] * 3 + [ANY],
         out_specs=[VMEM] * 2,
         compiler_params=SMALL,
         name="join",
@@ -379,7 +381,7 @@
     )(ds_x, *x_line, ds_y, *y_line)
 
     kept, *sent = pl.pallas_call(
-        functools.partial(total_kernel, groups),
+        total_kernel,
         out_shape=[piece, double, piece],
         in_specs=[VMEM] * 5,
         out_specs=[VMEM] * 3,
@@ -398,11 +400,11 @@
             flops=0, bytes_accessed=16 * side * width, transcendentals=0
         ),
         name="fill",
-    )(attn_x, attn_y, dq_x, dq_y, returned[2])
+    )(attn_x, attn_y, dq_x, dq_y, returned[0])
     k_grad, v_grad = pl.pallas_call(
-        functools.partial(place_kernel, groups),
+        place_kernel,
         out_shape=[shape(keys.shape, bf)] * 2,
-        in_specs=[VMEM] * groups + [ANY],
+        in_specs=[VMEM] * 3 + [ANY],
         out_specs=[VMEM] * 2,
         compiler_params=SMALL,
         name="place",

time: 105 us -> 106 us (level)
  waiting for transfers between devices: 24.5 us -> 35.6 us
  starting transfers between devices: 62 us -> 52.1 us
    ppermute x6 -> x4, waiting for transfers between devices: 15.3 us -> 25.2 us  [swap(): return lax.ppermute(block, ('cp', 'tp'), route)]
    ppermute x6 -> x4, starting transfers between devices: 31 us -> 25.8 us  [swap(): return lax.ppermute(block, ('cp', 'tp'), route)]
    ppermute x8, starting transfers between devices: 30.9 us -> 26.2 us  [move(): return lax.ppermute(block, 'cp', route)]
    ppermute x8, waiting for transfers between devices: 9.15 us -> 10.4 us  [move(): return lax.ppermute(block, 'cp', route)]
  transfers between devices with their start and end apart: 14 -> 12, of which waited for: 5 -> 5; matrix products, arithmetic and copies ran while one was open for 0% -> 0% of each run, Pallas kernels for 12% -> 12%
where the time goes in v8:
time: 106 us
  starting transfers between devices  52.1 us (49%)
  waiting for transfers between devices  35.6 us (34%)
  Pallas kernels  13.2 us (12%)
  local copies, waits for them, and re-layouts  3.13 us (3%)
    ppermute x8, starting transfers between devices, move(): return lax.ppermute(block, 'cp', route)  26.2 us
    ppermute x4, starting transfers between devices, swap(): return lax.ppermute(block, ('cp', 'tp'), route)  25.8 us
    ppermute x4, waiting for transfers between devices, swap(): return lax.ppermute(block, ('cp', 'tp'), route)  25.2 us
    ppermute x8, waiting for transfers between devices, move(): return lax.ppermute(block, 'cp', route)  10.4 us
    pallas_call x2, Pallas kernels, attend(): pl.pallas_call(functools.partial(attend_kernel, turn), in_specs=[VMEM] *...  8.64 us
    unnamed x6, local copies, waits for them, and re-layouts  3.12 us
  transfers between devices with their start and end apart: 12, of which 5 were waited for; matrix products, arithmetic and copies ran while one was open for 0% of the time, Pallas kernels for 12%

profile of v8, /device:TPU:32, one launch (start us, length us, event | category | flops | bytes accessed | tf_op | source)
XLA Modules:
  0.0 105.9 jit_solution(17210534558347283933)
XLA Ops:
  0.6 1.0 pad_maximum_fusion.kv_ref
  1.6 0.1 split.1
  1.7 9.1 %collective-permute-start = (bf16[2,2,2,64,128]{4,3,2,1,0:T(8,128)(2,1)S(1)}, bf16[2,2,2,64,128]{4,3,2,1,0:T(8,128)(2,1)S(1)}, u32[]{:S(2)}, u32[]{:S(2)}) collective-permute-start(bf16[2,2,2,64,128]{4,3,2,1,0:T(8,128)(2,1)S(1)} %get-tuple-element.31), channel_id=1, source_target_pairs={{0,1},{1,0},{2,3},{3,2},{4,7},{5,6},{6,5},{7,4},{8,9},{9,8},{10,11... | collective-permute-start | bytes 393224 | tf_op jit(solution)/shard_map/ppermute | solution.py:61
  10.8 4.6 %collective-permute-done.refs_0_ = bf16[2,2,2,64,128]{4,3,2,1,0:T(8,128)(2,1)S(1)} collective-permute-done((bf16[2,2,2,64,128]{4,3,2,1,0:T(8,128)(2,1)S(1)}, bf16[2,2,2,64,128]{4,3,2,1,0:T(8,128)(2,1)S(1)}, u32[]{:S(2)}, u32[]{:S(2)}) %collective-permute-start) | collective-permute-done | bytes 131104 | tf_op jit(solution)/shard_map/ppermute | solution.py:61
  15.4 12.1 %collective-permute-start.1 = (bf16[2,2,2,64,128]{4,3,2,1,0:T(8,128)(2,1)S(1)}, bf16[2,2,2,64,128]{4,3,2,1,0:T(8,128)(2,1)S(1)}, u32[]{:S(2)}, u32[]{:S(2)}) collective-permute-start(bf16[2,2,2,64,128]{4,3,2,1,0:T(8,128)(2,1)S(1)} %pad_maximum_fusion.1), channel_id=1, source_target_pairs={{0,3},{1,2},{2,1},{3,0},{4,5},{5,4},{6,7},{7,6},{8,11},{9,10},{10,... | collective-permute-start | bytes 393224 | tf_op jit(solution)/shard_map/ppermute | solution.py:61
  27.5 0.0 copy-start
  27.5 1.2 %copy-done = bf16[2,1,256,1024]{3,2,1,0:T(8,128)(2,1)S(1)} copy-done((bf16[2,1,256,1024]{3,2,1,0:T(8,128)(2,1)S(1)}, bf16[2,1,256,1024]{3,2,1,0:T(8,128)(2,1)}, u32[]{:S(2)}) %copy-start) | copy-done | bytes 1048600
  28.8 0.0 copy-start.1
  28.8 1.2 %copy-done.1 = bf16[2,1,256,1024]{3,2,1,0:T(8,128)(2,1)S(1)} copy-done((bf16[2,1,256,1024]{3,2,1,0:T(8,128)(2,1)S(1)}, bf16[2,1,256,1024]{3,2,1,0:T(8,128)(2,1)}, u32[]{:S(2)}) %copy-start.1) | copy-done | bytes 1048600
  30.0 0.0 copy-start.2
  30.0 0.7 copy-done.2
  30.7 0.5 prepare.1
  31.2 2.6 %collective-permute-done.1.refs_1_ = bf16[2,2,2,64,128]{4,3,2,1,0:T(8,128)(2,1)S(1)} collective-permute-done((bf16[2,2,2,64,128]{4,3,2,1,0:T(8,128)(2,1)S(1)}, bf16[2,2,2,64,128]{4,3,2,1,0:T(8,128)(2,1)S(1)}, u32[]{:S(2)}, u32[]{:S(2)}) %collective-permute-start.1) | collective-permute-done | bytes 131104 | tf_op jit(solution)/shard_map/ppermute | solution.py:61
  33.8 3.8 %collective-permute-start.2 = (bf16[2,256,128]{2,1,0:T(8,128)(2,1)S(1)}, bf16[2,256,128]{2,1,0:T(8,128)(2,1)S(1)}, u32[]{:S(2)}, u32[]{:S(2)}) collective-permute-start(bf16[2,256,128]{2,1,0:T(8,128)(2,1)S(1)} %get-tuple-element.34.here_ref.refs_3_), channel_id=1, source_target_pairs={{0,8},{8,16},{12,4},{16,24},{20,12},{24,32},{28,20},{32,40},{36,28... | collective-permute-start | bytes 393224 | tf_op jit(solution)/shard_map/ppermute | solution.py:48
  37.6 4.5 %collective-permute-start.3 = (bf16[2,256,128]{2,1,0:T(8,128)(2,1)S(1)}, bf16[2,256,128]{2,1,0:T(8,128)(2,1)S(1)}, u32[]{:S(2)}, u32[]{:S(2)}) collective-permute-start(bf16[2,256,128]{2,1,0:T(8,128)(2,1)S(1)} %get-tuple-element.35.here_ref.refs_7_), channel_id=1, source_target_pairs={{4,8},{8,4},{12,16},{16,12},{20,24},{24,20},{28,32},{32,28},{36,40... | collective-permute-start | bytes 393224 | tf_op jit(solution)/shard_map/ppermute | solution.py:48
  42.1 1.9 %collective-permute-start.5 = (bf16[2,256,128]{2,1,0:T(8,128)(2,1)S(1)}, bf16[2,256,128]{2,1,0:T(8,128)(2,1)S(1)}, u32[]{:S(2)}, u32[]{:S(2)}) collective-permute-start(bf16[2,256,128]{2,1,0:T(8,128)(2,1)S(1)} %get-tuple-element.34.here_ref.refs_3_), channel_id=1, source_target_pairs={{0,4},{4,0},{8,12},{12,8},{16,20},{20,16},{24,28},{28,24},{32,36},... | collective-permute-start | bytes 393224 | tf_op jit(solution)/shard_map/ppermute | solution.py:48
  44.0 5.7 %collective-permute-start.4 = (bf16[2,256,128]{2,1,0:T(8,128)(2,1)S(1)}, bf16[2,256,128]{2,1,0:T(8,128)(2,1)S(1)}, u32[]{:S(2)}, u32[]{:S(2)}) collective-permute-start(bf16[2,256,128]{2,1,0:T(8,128)(2,1)S(1)} %get-tuple-element.35.here_ref.refs_7_), channel_id=1, source_target_pairs={{4,12},{8,0},{12,20},{16,8},{20,28},{24,16},{28,36},{32,24},{36,44... | collective-permute-start | bytes 393224 | tf_op jit(solution)/shard_map/ppermute | solution.py:48
  49.7 0.0 collective-permute-done.2.oldest_ref.refs_1_
  49.7 0.0 collective-permute-done.3.middle_ref.refs_2_
  49.7 4.3 %attend.2 = (bf16[256,1024]{1,0:T(8,128)(2,1)S(1)}, bf16[8,256,768]{2,1,0:T(8,128)(2,1)S(1)}, bf16[2,256,128]{2,1,0:T(8,128)(2,1)S(1)}, bf16[2,256,128]{2,1,0:T(8,128)(2,1)S(1)}, f32[2,256,128]{2,1,0:T(8,128)S(1)}) custom-call(bf16[2,2,256,1024]{3,2,1,0:T(8,128)(2,1)S(1)} %get-tuple-element.30.qg_ref, ...), custom_call_target="tpu_custom_call" | custom-call | flops 2013265920 | bytes 1572864 | tf_op jit(solution)/shard_map/attend/pallas_call | solution.py:343
  54.1 1.9 %collective-permute-start.6 = (bf16[2,256,128]{2,1,0:T(8,128)(2,1)S(1)}, bf16[2,256,128]{2,1,0:T(8,128)(2,1)S(1)}, u32[]{:S(2)}, u32[]{:S(2)}) collective-permute-start(bf16[2,256,128]{2,1,0:T(8,128)(2,1)S(1)} %get-tuple-element.37), channel_id=1, source_target_pairs={{4,0},{0,4},{12,8},{8,12},{20,16},{16,20},{28,24},{24,28},{36,32},... | collective-permute-start | bytes 393224 | tf_op jit(solution)/shard_map/ppermute | solution.py:48
  56.0 4.6 %collective-permute-start.7 = (bf16[2,256,128]{2,1,0:T(8,128)(2,1)S(1)}, bf16[2,256,128]{2,1,0:T(8,128)(2,1)S(1)}, u32[]{:S(2)}, u32[]{:S(2)}) collective-permute-start(bf16[2,256,128]{2,1,0:T(8,128)(2,1)S(1)} %get-tuple-element.44), channel_id=1, source_target_pairs={{8,0},{16,8},{4,12},{24,16},{12,20},{32,24},{20,28},{40,32},{28,36... | collective-permute-start | bytes 393224 | tf_op jit(solution)/shard_map/ppermute | solution.py:48
  60.6 0.0 collective-permute-done.5.middle_ref.refs_6_
  60.6 0.0 collective-permute-done.4.oldest_ref.refs_5_
  60.6 0.0 collective-permute-done.6.refs_0_
  60.6 4.3 %attend.3 = (bf16[256,1024]{1,0:T(8,128)(2,1)S(1)}, bf16[8,256,768]{2,1,0:T(8,128)(2,1)S(1)}, bf16[2,256,128]{2,1,0:T(8,128)(2,1)S(1)}, bf16[2,256,128]{2,1,0:T(8,128)(2,1)S(1)}, f32[2,256,128]{2,1,0:T(8,128)S(1)}) custom-call(bf16[2,2,256,1024]{3,2,1,0:T(8,128)(2,1)S(1)} %get-tuple-element.30.qg_ref, ...), custom_call_target="tpu_custom_call" | custom-call | flops 2013265920 | bytes 1572864 | tf_op jit(solution)/shard_map/attend/pallas_call | solution.py:343
  65.0 1.9 %collective-permute-start.8 = (bf16[2,256,128]{2,1,0:T(8,128)(2,1)S(1)}, bf16[2,256,128]{2,1,0:T(8,128)(2,1)S(1)}, u32[]{:S(2)}, u32[]{:S(2)}) collective-permute-start(bf16[2,256,128]{2,1,0:T(8,128)(2,1)S(1)} %get-tuple-element.45), channel_id=1, source_target_pairs={{4,0},{0,4},{12,8},{8,12},{20,16},{16,20},{28,24},{24,28},{36,32},... | collective-permute-start | bytes 393224 | tf_op jit(solution)/shard_map/ppermute | solution.py:48
  66.9 1.9 %collective-permute-start.9 = (bf16[2,256,128]{2,1,0:T(8,128)(2,1)S(1)}, bf16[2,256,128]{2,1,0:T(8,128)(2,1)S(1)}, u32[]{:S(2)}, u32[]{:S(2)}) collective-permute-start(bf16[2,256,128]{2,1,0:T(8,128)(2,1)S(1)} %get-tuple-element.47), channel_id=1, source_target_pairs={{12,4},{0,8},{20,12},{8,16},{28,20},{16,24},{36,28},{24,32},{44,36... | collective-permute-start | bytes 393224 | tf_op jit(solution)/shard_map/ppermute | solution.py:48
  68.8 0.0 collective-permute-done.7.refs_1_
  68.8 0.0 collective-permute-done.8.refs_2_
  68.8 10.4 %collective-permute-done.9.refs_4_ = bf16[2,256,128]{2,1,0:T(8,128)(2,1)S(1)} collective-permute-done((bf16[2,256,128]{2,1,0:T(8,128)(2,1)S(1)}, bf16[2,256,128]{2,1,0:T(8,128)(2,1)S(1)}, u32[]{:S(2)}, u32[]{:S(2)}) %collective-permute-start.9) | collective-permute-done | bytes 131104 | tf_op jit(solution)/shard_map/ppermute | solution.py:48
  79.3 0.1 total.1
  79.3 1.9 %collective-permute-start.10 = (bf16[2,2,2,64,128]{4,3,2,1,0:T(8,128)(2,1)S(1)}, bf16[2,2,2,64,128]{4,3,2,1,0:T(8,128)(2,1)S(1)}, u32[]{:S(2)}, u32[]{:S(2)}) collective-permute-start(bf16[2,2,2,64,128]{4,3,2,1,0:T(8,128)(2,1)S(1)} %get-tuple-element.48), channel_id=1, source_target_pairs={{0,1},{1,0},{2,3},{3,2},{4,7},{5,6},{6,5},{7,4},{8,9},{9,8},{10,11... | collective-permute-start | bytes 393224 | tf_op jit(solution)/shard_map/ppermute | solution.py:61
  81.3 13.1 %collective-permute-done.10.refs_4_.refs_1_ = bf16[2,2,2,64,128]{4,3,2,1,0:T(8,128)(2,1)S(1)} collective-permute-done((bf16[2,2,2,64,128]{4,3,2,1,0:T(8,128)(2,1)S(1)}, bf16[2,2,2,64,128]{4,3,2,1,0:T(8,128)(2,1)S(1)}, u32[]{:S(2)}, u32[]{:S(2)}) %collective-permute-start.10) | collective-permute-done | bytes 131104 | tf_op jit(solution)/shard_map/ppermute | solution.py:61
  94.3 2.7 %collective-permute-start.11 = (bf16[2,2,2,64,128]{4,3,2,1,0:T(8,128)(2,1)S(1)}, bf16[2,2,2,64,128]{4,3,2,1,0:T(8,128)(2,1)S(1)}, u32[]{:S(2)}, u32[]{:S(2)}) collective-permute-start(bf16[2,2,2,64,128]{4,3,2,1,0:T(8,128)(2,1)S(1)} %pad_maximum_fusion.2), channel_id=1, source_target_pairs={{0,3},{1,2},{2,1},{3,0},{4,5},{5,4},{6,7},{7,6},{8,11},{9,10},{10,... | collective-permute-start | bytes 393224 | tf_op jit(solution)/shard_map/ppermute | solution.py:61
  97.0 1.8 %query.1 = (bf16[256,1024]{1,0:T(8,128)(2,1)S(1)}, bf16[256,1024]{1,0:T(8,128)(2,1)S(1)}) custom-call(bf16[8,256,768]{2,1,0:T(8,128)(2,1)S(1)} %get-tuple-element.39.refs_0_, bf16[2,256,128]{2,1,0:T(8,128)(2,1)S(1)} %collective-permute-done.2.oldest_ref.refs_1_, bf16[2,256,128]{2,1,0:T(8,128)(2,1)S(1)} %collective-permute-done.3.middle_ref.refs_2_, ...), custom_call_target="tpu_custom_call" | custom-call | flops 805306368 | bytes 6291456 | tf_op jit(solution)/shard_map/query/pallas_call | solution.py:371
  98.8 1.4 %fill.1 = (bf16[2,1,256,1024]{3,2,1,0:T(8,128)(2,1)}, bf16[2,1,256,1024]{3,2,1,0:T(8,128)(2,1)}, f32[8,128]{1,0:T(8,128)S(1)}) custom-call(bf16[256,1024]{1,0:T(8,128)(2,1)S(1)} %get-tuple-element.36.refs_0_, bf16[256,1024]{1,0:T(8,128)(2,1)S(1)} %get-tuple-element.38.refs_1_, bf16[256,1024]{1,0:T(8,128)(2,1)S(1)} %get-tuple-element.41.refs_2_, ...), custom_call_target="tpu_custom_call" | custom-call | bytes 4194304 | tf_op jit(solution)/shard_map/fill/pallas_call | solution.py:392
  100.2 4.9 %collective-permute-done.11.refs_2_ = bf16[2,2,2,64,128]{4,3,2,1,0:T(8,128)(2,1)S(1)} collective-permute-done((bf16[2,2,2,64,128]{4,3,2,1,0:T(8,128)(2,1)S(1)}, bf16[2,2,2,64,128]{4,3,2,1,0:T(8,128)(2,1)S(1)}, u32[]{:S(2)}, u32[]{:S(2)}) %collective-permute-start.11) | collective-permute-done | bytes 131104 | tf_op jit(solution)/shard_map/ppermute | solution.py:61
  105.1 0.8 place.1
  (5 shorter events, 0.1 us)
Async XLA Ops:
  1.7 13.7 %collective-permute-start = (bf16[2,2,2,64,128]{4,3,2,1,0:T(8,128)(2,1)S(1)}, bf16[2,2,2,64,128]{4,3,2,1,0:T(8,128)(2,1)S(1)}, u32[]{:S(2)}, u32[]{:S(2)}) collective-permute-start(bf16[2,2,2,64,128]{4,3,2,1,0:T(8,128)(2,1)S(1)} %get-tuple-element.31), channel_id=1, source_target_pairs={{0,1},{1,0},{2,3},{3,2},{4,7},{5,6},{6,5},{7,4},{8,9},{9,8},{10,11... | collective-permute-start | bytes 393224 | tf_op jit(solution)/shard_map/ppermute | solution.py:61
  15.4 18.4 %collective-permute-start.1 = (bf16[2,2,2,64,128]{4,3,2,1,0:T(8,128)(2,1)S(1)}, bf16[2,2,2,64,128]{4,3,2,1,0:T(8,128)(2,1)S(1)}, u32[]{:S(2)}, u32[]{:S(2)}) collective-permute-start(bf16[2,2,2,64,128]{4,3,2,1,0:T(8,128)(2,1)S(1)} %pad_maximum_fusion.1), channel_id=1, source_target_pairs={{0,3},{1,2},{2,1},{3,0},{4,5},{5,4},{6,7},{7,6},{8,11},{9,10},{10,... | collective-permute-start | bytes 393224 | tf_op jit(solution)/shard_map/ppermute | solution.py:61
  27.5 1.2 %copy-start = (bf16[2,1,256,1024]{3,2,1,0:T(8,128)(2,1)S(1)}, bf16[2,1,256,1024]{3,2,1,0:T(8,128)(2,1)}, u32[]{:S(2)}) copy-start(bf16[2,1,256,1024]{3,2,1,0:T(8,128)(2,1)} %q_ref.1) | copy-start | bytes 3145732
  28.8 1.2 %copy-start.1 = (bf16[2,1,256,1024]{3,2,1,0:T(8,128)(2,1)S(1)}, bf16[2,1,256,1024]{3,2,1,0:T(8,128)(2,1)}, u32[]{:S(2)}) copy-start(bf16[2,1,256,1024]{3,2,1,0:T(8,128)(2,1)} %g_ref.1) | copy-start | bytes 3145732
  30.0 0.7 copy-start.2
  33.8 15.9 %collective-permute-start.2 = (bf16[2,256,128]{2,1,0:T(8,128)(2,1)S(1)}, bf16[2,256,128]{2,1,0:T(8,128)(2,1)S(1)}, u32[]{:S(2)}, u32[]{:S(2)}) collective-permute-start(bf16[2,256,128]{2,1,0:T(8,128)(2,1)S(1)} %get-tuple-element.34.here_ref.refs_3_), channel_id=1, source_target_pairs={{0,8},{8,16},{12,4},{16,24},{20,12},{24,32},{28,20},{32,40},{36,28... | collective-permute-start | bytes 393224 | tf_op jit(solution)/shard_map/ppermute | solution.py:48
  37.6 12.1 %collective-permute-start.3 = (bf16[2,256,128]{2,1,0:T(8,128)(2,1)S(1)}, bf16[2,256,128]{2,1,0:T(8,128)(2,1)S(1)}, u32[]{:S(2)}, u32[]{:S(2)}) collective-permute-start(bf16[2,256,128]{2,1,0:T(8,128)(2,1)S(1)} %get-tuple-element.35.here_ref.refs_7_), channel_id=1, source_target_pairs={{4,8},{8,4},{12,16},{16,12},{20,24},{24,20},{28,32},{32,28},{36,40... | collective-permute-start | bytes 393224 | tf_op jit(solution)/shard_map/ppermute | solution.py:48
  42.1 18.5 %collective-permute-start.5 = (bf16[2,256,128]{2,1,0:T(8,128)(2,1)S(1)}, bf16[2,256,128]{2,1,0:T(8,128)(2,1)S(1)}, u32[]{:S(2)}, u32[]{:S(2)}) collective-permute-start(bf16[2,256,128]{2,1,0:T(8,128)(2,1)S(1)} %get-tuple-element.34.here_ref.refs_3_), channel_id=1, source_target_pairs={{0,4},{4,0},{8,12},{12,8},{16,20},{20,16},{24,28},{28,24},{32,36},... | collective-permute-start | bytes 393224 | tf_op jit(solution)/shard_map/ppermute | solution.py:48
  44.0 16.6 %collective-permute-start.4 = (bf16[2,256,128]{2,1,0:T(8,128)(2,1)S(1)}, bf16[2,256,128]{2,1,0:T(8,128)(2,1)S(1)}, u32[]{:S(2)}, u32[]{:S(2)}) collective-permute-start(bf16[2,256,128]{2,1,0:T(8,128)(2,1)S(1)} %get-tuple-element.35.here_ref.refs_7_), channel_id=1, source_target_pairs={{4,12},{8,0},{12,20},{16,8},{20,28},{24,16},{28,36},{32,24},{36,44... | collective-permute-start | bytes 393224 | tf_op jit(solution)/shard_map/ppermute | solution.py:48
  54.1 6.6 %collective-permute-start.6 = (bf16[2,256,128]{2,1,0:T(8,128)(2,1)S(1)}, bf16[2,256,128]{2,1,0:T(8,128)(2,1)S(1)}, u32[]{:S(2)}, u32[]{:S(2)}) collective-permute-start(bf16[2,256,128]{2,1,0:T(8,128)(2,1)S(1)} %get-tuple-element.37), channel_id=1, source_target_pairs={{4,0},{0,4},{12,8},{8,12},{20,16},{16,20},{28,24},{24,28},{36,32},... | collective-permute-start | bytes 393224 | tf_op jit(solution)/shard_map/ppermute | solution.py:48
  56.0 12.8 %collective-permute-start.7 = (bf16[2,256,128]{2,1,0:T(8,128)(2,1)S(1)}, bf16[2,256,128]{2,1,0:T(8,128)(2,1)S(1)}, u32[]{:S(2)}, u32[]{:S(2)}) collective-permute-start(bf16[2,256,128]{2,1,0:T(8,128)(2,1)S(1)} %get-tuple-element.44), channel_id=1, source_target_pairs={{8,0},{16,8},{4,12},{24,16},{12,20},{32,24},{20,28},{40,32},{28,36... | collective-permute-start | bytes 393224 | tf_op jit(solution)/shard_map/ppermute | solution.py:48
  65.0 3.9 %collective-permute-start.8 = (bf16[2,256,128]{2,1,0:T(8,128)(2,1)S(1)}, bf16[2,256,128]{2,1,0:T(8,128)(2,1)S(1)}, u32[]{:S(2)}, u32[]{:S(2)}) collective-permute-start(bf16[2,256,128]{2,1,0:T(8,128)(2,1)S(1)} %get-tuple-element.45), channel_id=1, source_target_pairs={{4,0},{0,4},{12,8},{8,12},{20,16},{16,20},{28,24},{24,28},{36,32},... | collective-permute-start | bytes 393224 | tf_op jit(solution)/shard_map/ppermute | solution.py:48
  66.9 12.4 %collective-permute-start.9 = (bf16[2,256,128]{2,1,0:T(8,128)(2,1)S(1)}, bf16[2,256,128]{2,1,0:T(8,128)(2,1)S(1)}, u32[]{:S(2)}, u32[]{:S(2)}) collective-permute-start(bf16[2,256,128]{2,1,0:T(8,128)(2,1)S(1)} %get-tuple-element.47), channel_id=1, source_target_pairs={{12,4},{0,8},{20,12},{8,16},{28,20},{16,24},{36,28},{24,32},{44,36... | collective-permute-start | bytes 393224 | tf_op jit(solution)/shard_map/ppermute | solution.py:48
  79.3 15.0 %collective-permute-start.10 = (bf16[2,2,2,64,128]{4,3,2,1,0:T(8,128)(2,1)S(1)}, bf16[2,2,2,64,128]{4,3,2,1,0:T(8,128)(2,1)S(1)}, u32[]{:S(2)}, u32[]{:S(2)}) collective-permute-start(bf16[2,2,2,64,128]{4,3,2,1,0:T(8,128)(2,1)S(1)} %get-tuple-element.48), channel_id=1, source_target_pairs={{0,1},{1,0},{2,3},{3,2},{4,7},{5,6},{6,5},{7,4},{8,9},{9,8},{10,11... | collective-permute-start | bytes 393224 | tf_op jit(solution)/shard_map/ppermute | solution.py:61
  94.3 10.8 %collective-permute-start.11 = (bf16[2,2,2,64,128]{4,3,2,1,0:T(8,128)(2,1)S(1)}, bf16[2,2,2,64,128]{4,3,2,1,0:T(8,128)(2,1)S(1)}, u32[]{:S(2)}, u32[]{:S(2)}) collective-permute-start(bf16[2,2,2,64,128]{4,3,2,1,0:T(8,128)(2,1)S(1)} %pad_maximum_fusion.2), channel_id=1, source_target_pairs={{0,3},{1,2},{2,1},{3,0},{4,5},{5,4},{6,7},{7,6},{8,11},{9,10},{10,... | collective-permute-start | bytes 393224 | tf_op jit(solution)/shard_map/ppermute | solution.py:61

commit v9 on v6

--- a/solution.py
+++ b/solution.py
@@ -61,6 +61,13 @@
     return lax.ppermute(block, ("cp", "tp"), route)
 
 
+ARRIVAL = (2, 1, 3)
+
+
+def exchange(pieces):
+    return [around(pieces[step - 1], step) for step in ARRIVAL]
+
+
 def dot(a, b, contract):
     return lax.dot_general(a, b, (contract, ((), ())), preferred_element_type=jnp.float32)
 
@@ -85,7 +92,7 @@
     for kind in range(2):
         for half, out in zip((core, 1 - core), outs):
             out[kind, aligned(tp, rows), :] = kv_ref[kind, half, 0, :, aligned(tp, HD)]
-    for step, piece in enumerate(pieces, 1):
+    for step, piece in zip(ARRIVAL, pieces):
         source = lax.rem(tp - offset(step, core, groups) + groups, groups)
         for block, out in enumerate(outs):
             out[:, aligned(source, rows), :] = piece[block]
@@ -107,7 +114,7 @@
 def place_kernel(groups, *refs):
     pieces, outs = refs[:-3], refs[-2:]
     tp, core = lax.axis_index("tp"), lax.rem(lax.axis_index("cp"), 2)
-    for step, piece in enumerate(pieces):
+    for step, piece in zip((0, *ARRIVAL), pieces):
         lanes = aligned(lax.rem(tp - offset(step, core, groups) + groups, groups), HD)
         for block, half in enumerate((core, 1 - core)):
             for kind, out in enumerate(outs):
@@ -297,7 +304,7 @@
         compiler_params=SMALL,
         name="split",
     )(kv)
-    came = [around(block, step) for step, block in enumerate(sent, 1)]
+    came = exchange(sent)
     qg, bias = pl.pallas_call(
         functools.partial(prepare_kernel, contexts),
         out_shape=[shape((2, 2, side, width), bf), shape((2, side, 2 * side), jnp.float32)],
@@ -375,7 +382,7 @@
         compiler_params=SMALL,
         name="total",
     )(*terms[0], *terms[1])
-    returned = [pieces[0]] + [around(block, step) for step, block in enumerate(pieces[1:], 1)]
+    returned = [pieces[0], *exchange(pieces[1:])]
     attn_out, q_grad, filled = pl.pallas_call(
         fill_kernel,
         out_shape=[shape(queries.shape, bf)] * 2 + [shape((8, HD), jnp.float32)],

time: 100 us -> 99.9 us (level)
  the two profiles are of different devices: /device:TPU:64 before, /device:TPU:32 now
where the time goes in v9:
time: 99.9 us; the launch traced here: 99.4 us
  starting transfers between devices  67.7 us (68%)
  waiting for transfers between devices  13.4 us (13%)
  Pallas kernels  13.2 us (13%)
  local copies, waits for them, and re-layouts  3.12 us (3%)
    ppermute x6, starting transfers between devices, around(): return lax.ppermute(block, ('cp', 'tp'), route)  42.6 us
    ppermute x8, starting transfers between devices, move(): return lax.ppermute(block, 'cp', route)  25.2 us
    ppermute x8, waiting for transfers between devices, move(): return lax.ppermute(block, 'cp', route)  8.66 us
    pallas_call x2, Pallas kernels, attend(): pl.pallas_call(functools.partial(attend_kernel, turn), in_specs=[VMEM] *...  8.64 us
    ppermute x6, waiting for transfers between devices, around(): return lax.ppermute(block, ('cp', 'tp'), route)  4.77 us
    unnamed x6, local copies, waits for them, and re-layouts  3.12 us
  transfers between devices with their start and end apart: 14, of which 5 were waited for; matrix products, arithmetic and copies ran while one was open for 0% of the time, Pallas kernels for 12%

profile of v9, /device:TPU:32, one launch (start us, length us, event | category | flops | bytes accessed | tf_op | source)
XLA Modules:
  0.0 99.4 jit_solution(18045171722928697814)
XLA Ops:
  0.6 1.0 %pad_maximum_fusion.kv_ref = bf16[2,2,1,64,512]{4,3,2,1,0:T(8,128)(2,1)S(1)} fusion(bf16[1,2,1,64,512]{4,3,2,1,0:T(8,128)(2,1)} %bitcast.4, bf16[1,2,1,64,512]{4,3,2,1,0:T(8,128)(2,1)} %bitcast.5), kind=kLoop, calls=%fused_computation | loop fusion | flops 131072 | bytes 524288 | tf_op jit(solution)/shard_map/stack | solution.py:298
  1.6 0.1 split.1
  1.7 14.8 %collective-permute-start = (bf16[2,2,64,128]{3,2,1,0:T(8,128)(2,1)S(1)}, bf16[2,2,64,128]{3,2,1,0:T(8,128)(2,1)S(1)}, u32[]{:S(2)}, u32[]{:S(2)}) collective-permute-start(bf16[2,2,64,128]{3,2,1,0:T(8,128)(2,1)S(1)} %get-tuple-element.33), channel_id=1, source_target_pairs={{0,2},{1,3},{2,0},{3,1},{4,6},{5,7},{6,4},{7,5},{8,10},{9,11},{10,... | collective-permute-start | bytes 196616 | tf_op jit(solution)/shard_map/ppermute | solution.py:61
  16.5 4.3 %collective-permute-start.1 = (bf16[2,2,64,128]{3,2,1,0:T(8,128)(2,1)S(1)}, bf16[2,2,64,128]{3,2,1,0:T(8,128)(2,1)S(1)}, u32[]{:S(2)}, u32[]{:S(2)}) collective-permute-start(bf16[2,2,64,128]{3,2,1,0:T(8,128)(2,1)S(1)} %get-tuple-element.34), channel_id=1, source_target_pairs={{0,1},{1,2},{2,3},{3,0},{4,7},{5,4},{6,5},{7,6},{8,9},{9,10},{10,1... | collective-permute-start | bytes 196616 | tf_op jit(solution)/shard_map/ppermute | solution.py:61
  20.8 5.5 %collective-permute-start.2 = (bf16[2,2,64,128]{3,2,1,0:T(8,128)(2,1)S(1)}, bf16[2,2,64,128]{3,2,1,0:T(8,128)(2,1)S(1)}, u32[]{:S(2)}, u32[]{:S(2)}) collective-permute-start(bf16[2,2,64,128]{3,2,1,0:T(8,128)(2,1)S(1)} %get-tuple-element.35), channel_id=1, source_target_pairs={{0,3},{1,0},{2,1},{3,2},{4,5},{5,6},{6,7},{7,4},{8,11},{9,8},{10,9... | collective-permute-start | bytes 196616 | tf_op jit(solution)/shard_map/ppermute | solution.py:61
  26.3 0.0 copy-start
  26.3 1.2 %copy-done = bf16[2,1,256,1024]{3,2,1,0:T(8,128)(2,1)S(1)} copy-done((bf16[2,1,256,1024]{3,2,1,0:T(8,128)(2,1)S(1)}, bf16[2,1,256,1024]{3,2,1,0:T(8,128)(2,1)}, u32[]{:S(2)}) %copy-start) | copy-done | bytes 1048600
  27.5 0.0 copy-start.1
  27.5 1.2 %copy-done.1 = bf16[2,1,256,1024]{3,2,1,0:T(8,128)(2,1)S(1)} copy-done((bf16[2,1,256,1024]{3,2,1,0:T(8,128)(2,1)S(1)}, bf16[2,1,256,1024]{3,2,1,0:T(8,128)(2,1)}, u32[]{:S(2)}) %copy-start.1) | copy-done | bytes 1048600
  28.7 0.0 copy-start.2
  28.7 0.7 copy-done.2
  29.4 0.5 prepare.1
  29.9 0.0 collective-permute-done.refs_0_
  29.9 1.4 %collective-permute-done.1.refs_1_ = bf16[2,2,64,128]{3,2,1,0:T(8,128)(2,1)S(1)} collective-permute-done((bf16[2,2,64,128]{3,2,1,0:T(8,128)(2,1)S(1)}, bf16[2,2,64,128]{3,2,1,0:T(8,128)(2,1)S(1)}, u32[]{:S(2)}, u32[]{:S(2)}) %collective-permute-start.1) | collective-permute-done | bytes 65568 | tf_op jit(solution)/shard_map/ppermute | solution.py:61
  31.3 0.6 collective-permute-done.2.refs_2_
  32.0 3.4 %collective-permute-start.3 = (bf16[2,256,128]{2,1,0:T(8,128)(2,1)S(1)}, bf16[2,256,128]{2,1,0:T(8,128)(2,1)S(1)}, u32[]{:S(2)}, u32[]{:S(2)}) collective-permute-start(bf16[2,256,128]{2,1,0:T(8,128)(2,1)S(1)} %get-tuple-element.37.here_ref.refs_3_), channel_id=1, source_target_pairs={{0,8},{8,16},{12,4},{16,24},{20,12},{24,32},{28,20},{32,40},{36,28... | collective-permute-start | bytes 393224 | tf_op jit(solution)/shard_map/ppermute | solution.py:48
  35.4 3.3 %collective-permute-start.4 = (bf16[2,256,128]{2,1,0:T(8,128)(2,1)S(1)}, bf16[2,256,128]{2,1,0:T(8,128)(2,1)S(1)}, u32[]{:S(2)}, u32[]{:S(2)}) collective-permute-start(bf16[2,256,128]{2,1,0:T(8,128)(2,1)S(1)} %get-tuple-element.38.here_ref.refs_7_), channel_id=1, source_target_pairs={{4,8},{8,4},{12,16},{16,12},{20,24},{24,20},{28,32},{32,28},{36,40... | collective-permute-start | bytes 393224 | tf_op jit(solution)/shard_map/ppermute | solution.py:48
  38.7 2.1 %collective-permute-start.6 = (bf16[2,256,128]{2,1,0:T(8,128)(2,1)S(1)}, bf16[2,256,128]{2,1,0:T(8,128)(2,1)S(1)}, u32[]{:S(2)}, u32[]{:S(2)}) collective-permute-start(bf16[2,256,128]{2,1,0:T(8,128)(2,1)S(1)} %get-tuple-element.37.here_ref.refs_3_), channel_id=1, source_target_pairs={{0,4},{4,0},{8,12},{12,8},{16,20},{20,16},{24,28},{28,24},{32,36},... | collective-permute-start | bytes 393224 | tf_op jit(solution)/shard_map/ppermute | solution.py:48
  40.8 6.7 %collective-permute-start.5 = (bf16[2,256,128]{2,1,0:T(8,128)(2,1)S(1)}, bf16[2,256,128]{2,1,0:T(8,128)(2,1)S(1)}, u32[]{:S(2)}, u32[]{:S(2)}) collective-permute-start(bf16[2,256,128]{2,1,0:T(8,128)(2,1)S(1)} %get-tuple-element.38.here_ref.refs_7_), channel_id=1, source_target_pairs={{4,12},{8,0},{12,20},{16,8},{20,28},{24,16},{28,36},{32,24},{36,44... | collective-permute-start | bytes 393224 | tf_op jit(solution)/shard_map/ppermute | solution.py:48
  47.5 0.0 collective-permute-done.3.oldest_ref.refs_1_
  47.5 0.0 collective-permute-done.4.middle_ref.refs_2_
  47.5 4.3 %attend.2 = (bf16[256,1024]{1,0:T(8,128)(2,1)S(1)}, bf16[8,256,768]{2,1,0:T(8,128)(2,1)S(1)}, bf16[2,256,128]{2,1,0:T(8,128)(2,1)S(1)}, bf16[2,256,128]{2,1,0:T(8,128)(2,1)S(1)}, f32[2,256,128]{2,1,0:T(8,128)S(1)}) custom-call(bf16[2,2,256,1024]{3,2,1,0:T(8,128)(2,1)S(1)} %get-tuple-element.32.qg_ref, ...), custom_call_target="tpu_custom_call" | custom-call | flops 2013265920 | bytes 1572864 | tf_op jit(solution)/shard_map/attend/pallas_call | solution.py:337
  51.9 1.9 %collective-permute-start.7 = (bf16[2,256,128]{2,1,0:T(8,128)(2,1)S(1)}, bf16[2,256,128]{2,1,0:T(8,128)(2,1)S(1)}, u32[]{:S(2)}, u32[]{:S(2)}) collective-permute-start(bf16[2,256,128]{2,1,0:T(8,128)(2,1)S(1)} %get-tuple-element.40), channel_id=1, source_target_pairs={{4,0},{0,4},{12,8},{8,12},{20,16},{16,20},{28,24},{24,28},{36,32},... | collective-permute-start | bytes 393224 | tf_op jit(solution)/shard_map/ppermute | solution.py:48
  53.8 3.4 %collective-permute-start.8 = (bf16[2,256,128]{2,1,0:T(8,128)(2,1)S(1)}, bf16[2,256,128]{2,1,0:T(8,128)(2,1)S(1)}, u32[]{:S(2)}, u32[]{:S(2)}) collective-permute-start(bf16[2,256,128]{2,1,0:T(8,128)(2,1)S(1)} %get-tuple-element.47), channel_id=1, source_target_pairs={{8,0},{16,8},{4,12},{24,16},{12,20},{32,24},{20,28},{40,32},{28,36... | collective-permute-start | bytes 393224 | tf_op jit(solution)/shard_map/ppermute | solution.py:48
  57.2 0.0 collective-permute-done.6.middle_ref.refs_6_
  57.2 0.0 collective-permute-done.5.oldest_ref.refs_5_
  57.2 0.0 collective-permute-done.7.refs_0_
  57.3 4.3 %attend.3 = (bf16[256,1024]{1,0:T(8,128)(2,1)S(1)}, bf16[8,256,768]{2,1,0:T(8,128)(2,1)S(1)}, bf16[2,256,128]{2,1,0:T(8,128)(2,1)S(1)}, bf16[2,256,128]{2,1,0:T(8,128)(2,1)S(1)}, f32[2,256,128]{2,1,0:T(8,128)S(1)}) custom-call(bf16[2,2,256,1024]{3,2,1,0:T(8,128)(2,1)S(1)} %get-tuple-element.32.qg_ref, ...), custom_call_target="tpu_custom_call" | custom-call | flops 2013265920 | bytes 1572864 | tf_op jit(solution)/shard_map/attend/pallas_call | solution.py:337
  61.6 1.9 %collective-permute-start.9 = (bf16[2,256,128]{2,1,0:T(8,128)(2,1)S(1)}, bf16[2,256,128]{2,1,0:T(8,128)(2,1)S(1)}, u32[]{:S(2)}, u32[]{:S(2)}) collective-permute-start(bf16[2,256,128]{2,1,0:T(8,128)(2,1)S(1)} %get-tuple-element.48), channel_id=1, source_target_pairs={{4,0},{0,4},{12,8},{8,12},{20,16},{16,20},{28,24},{24,28},{36,32},... | collective-permute-start | bytes 393224 | tf_op jit(solution)/shard_map/ppermute | solution.py:48
  63.5 2.4 %collective-permute-start.10 = (bf16[2,256,128]{2,1,0:T(8,128)(2,1)S(1)}, bf16[2,256,128]{2,1,0:T(8,128)(2,1)S(1)}, u32[]{:S(2)}, u32[]{:S(2)}) collective-permute-start(bf16[2,256,128]{2,1,0:T(8,128)(2,1)S(1)} %get-tuple-element.50), channel_id=1, source_target_pairs={{12,4},{0,8},{20,12},{8,16},{28,20},{16,24},{36,28},{24,32},{44,36... | collective-permute-start | bytes 393224 | tf_op jit(solution)/shard_map/ppermute | solution.py:48
  65.9 0.0 collective-permute-done.8.refs_1_
  65.9 0.0 collective-permute-done.9.refs_2_
  66.0 8.6 %collective-permute-done.10.refs_4_ = bf16[2,256,128]{2,1,0:T(8,128)(2,1)S(1)} collective-permute-done((bf16[2,256,128]{2,1,0:T(8,128)(2,1)S(1)}, bf16[2,256,128]{2,1,0:T(8,128)(2,1)S(1)}, u32[]{:S(2)}, u32[]{:S(2)}) %collective-permute-start.10) | collective-permute-done | bytes 131104 | tf_op jit(solution)/shard_map/ppermute | solution.py:48
  74.6 0.1 total.1
  74.7 8.2 %collective-permute-start.11 = (bf16[2,2,64,128]{3,2,1,0:T(8,128)(2,1)S(1)}, bf16[2,2,64,128]{3,2,1,0:T(8,128)(2,1)S(1)}, u32[]{:S(2)}, u32[]{:S(2)}) collective-permute-start(bf16[2,2,64,128]{3,2,1,0:T(8,128)(2,1)S(1)} %get-tuple-element.51), channel_id=1, source_target_pairs={{0,2},{1,3},{2,0},{3,1},{4,6},{5,7},{6,4},{7,5},{8,10},{9,11},{10,... | collective-permute-start | bytes 196616 | tf_op jit(solution)/shard_map/ppermute | solution.py:61
  82.9 4.8 %collective-permute-start.12 = (bf16[2,2,64,128]{3,2,1,0:T(8,128)(2,1)S(1)}, bf16[2,2,64,128]{3,2,1,0:T(8,128)(2,1)S(1)}, u32[]{:S(2)}, u32[]{:S(2)}) collective-permute-start(bf16[2,2,64,128]{3,2,1,0:T(8,128)(2,1)S(1)} %get-tuple-element.55), channel_id=1, source_target_pairs={{0,1},{1,2},{2,3},{3,0},{4,7},{5,4},{6,5},{7,6},{8,9},{9,10},{10,1... | collective-permute-start | bytes 196616 | tf_op jit(solution)/shard_map/ppermute | solution.py:61
  87.7 4.9 %collective-permute-start.13 = (bf16[2,2,64,128]{3,2,1,0:T(8,128)(2,1)S(1)}, bf16[2,2,64,128]{3,2,1,0:T(8,128)(2,1)S(1)}, u32[]{:S(2)}, u32[]{:S(2)}) collective-permute-start(bf16[2,2,64,128]{3,2,1,0:T(8,128)(2,1)S(1)} %get-tuple-element.56), channel_id=1, source_target_pairs={{0,3},{1,0},{2,1},{3,2},{4,5},{5,6},{6,7},{7,4},{8,11},{9,8},{10,9... | collective-permute-start | bytes 196616 | tf_op jit(solution)/shard_map/ppermute | solution.py:61
  92.7 1.8 %query.1 = (bf16[256,1024]{1,0:T(8,128)(2,1)S(1)}, bf16[256,1024]{1,0:T(8,128)(2,1)S(1)}) custom-call(bf16[8,256,768]{2,1,0:T(8,128)(2,1)S(1)} %get-tuple-element.42.refs_0_, bf16[2,256,128]{2,1,0:T(8,128)(2,1)S(1)} %collective-permute-done.3.oldest_ref.refs_1_, bf16[2,256,128]{2,1,0:T(8,128)(2,1)S(1)} %collective-permute-done.4.middle_ref.refs_2_, ...), custom_call_target="tpu_custom_call" | custom-call | flops 805306368 | bytes 6291456 | tf_op jit(solution)/shard_map/query/pallas_call | solution.py:365
  94.5 0.0 collective-permute-done.11.refs_4_.refs_1_
  94.5 1.4 %fill.1 = (bf16[2,1,256,1024]{3,2,1,0:T(8,128)(2,1)}, bf16[2,1,256,1024]{3,2,1,0:T(8,128)(2,1)}, f32[8,128]{1,0:T(8,128)S(1)}) custom-call(bf16[256,1024]{1,0:T(8,128)(2,1)S(1)} %get-tuple-element.39.refs_0_, bf16[256,1024]{1,0:T(8,128)(2,1)S(1)} %get-tuple-element.41.refs_1_, bf16[256,1024]{1,0:T(8,128)(2,1)S(1)} %get-tuple-element.44.refs_2_, ...), custom_call_target="tpu_custom_call" | custom-call | bytes 4194304 | tf_op jit(solution)/shard_map/fill/pallas_call | solution.py:386
  95.9 0.3 collective-permute-done.12.refs_2_
  96.1 2.5 %collective-permute-done.13.refs_3_ = bf16[2,2,64,128]{3,2,1,0:T(8,128)(2,1)S(1)} collective-permute-done((bf16[2,2,64,128]{3,2,1,0:T(8,128)(2,1)S(1)}, bf16[2,2,64,128]{3,2,1,0:T(8,128)(2,1)S(1)}, u32[]{:S(2)}, u32[]{:S(2)}) %collective-permute-start.13) | collective-permute-done | bytes 65568 | tf_op jit(solution)/shard_map/ppermute | solution.py:61
  98.6 0.8 place.1
  (1 shorter events, 0.0 us)
Async XLA Ops:
  1.7 28.2 %collective-permute-start = (bf16[2,2,64,128]{3,2,1,0:T(8,128)(2,1)S(1)}, bf16[2,2,64,128]{3,2,1,0:T(8,128)(2,1)S(1)}, u32[]{:S(2)}, u32[]{:S(2)}) collective-permute-start(bf16[2,2,64,128]{3,2,1,0:T(8,128)(2,1)S(1)} %get-tuple-element.33), channel_id=1, source_target_pairs={{0,2},{1,3},{2,0},{3,1},{4,6},{5,7},{6,4},{7,5},{8,10},{9,11},{10,... | collective-permute-start | bytes 196616 | tf_op jit(solution)/shard_map/ppermute | solution.py:61
  16.5 14.8 %collective-permute-start.1 = (bf16[2,2,64,128]{3,2,1,0:T(8,128)(2,1)S(1)}, bf16[2,2,64,128]{3,2,1,0:T(8,128)(2,1)S(1)}, u32[]{:S(2)}, u32[]{:S(2)}) collective-permute-start(bf16[2,2,64,128]{3,2,1,0:T(8,128)(2,1)S(1)} %get-tuple-element.34), channel_id=1, source_target_pairs={{0,1},{1,2},{2,3},{3,0},{4,7},{5,4},{6,5},{7,6},{8,9},{9,10},{10,1... | collective-permute-start | bytes 196616 | tf_op jit(solution)/shard_map/ppermute | solution.py:61
  20.8 11.1 %collective-permute-start.2 = (bf16[2,2,64,128]{3,2,1,0:T(8,128)(2,1)S(1)}, bf16[2,2,64,128]{3,2,1,0:T(8,128)(2,1)S(1)}, u32[]{:S(2)}, u32[]{:S(2)}) collective-permute-start(bf16[2,2,64,128]{3,2,1,0:T(8,128)(2,1)S(1)} %get-tuple-element.35), channel_id=1, source_target_pairs={{0,3},{1,0},{2,1},{3,2},{4,5},{5,6},{6,7},{7,4},{8,11},{9,8},{10,9... | collective-permute-start | bytes 196616 | tf_op jit(solution)/shard_map/ppermute | solution.py:61
  26.3 1.2 %copy-start = (bf16[2,1,256,1024]{3,2,1,0:T(8,128)(2,1)S(1)}, bf16[2,1,256,1024]{3,2,1,0:T(8,128)(2,1)}, u32[]{:S(2)}) copy-start(bf16[2,1,256,1024]{3,2,1,0:T(8,128)(2,1)} %q_ref.1) | copy-start | bytes 3145732
  27.5 1.2 %copy-start.1 = (bf16[2,1,256,1024]{3,2,1,0:T(8,128)(2,1)S(1)}, bf16[2,1,256,1024]{3,2,1,0:T(8,128)(2,1)}, u32[]{:S(2)}) copy-start(bf16[2,1,256,1024]{3,2,1,0:T(8,128)(2,1)} %g_ref.1) | copy-start | bytes 3145732
  28.7 0.7 copy-start.2
  32.0 15.5 %collective-permute-start.3 = (bf16[2,256,128]{2,1,0:T(8,128)(2,1)S(1)}, bf16[2,256,128]{2,1,0:T(8,128)(2,1)S(1)}, u32[]{:S(2)}, u32[]{:S(2)}) collective-permute-start(bf16[2,256,128]{2,1,0:T(8,128)(2,1)S(1)} %get-tuple-element.37.here_ref.refs_3_), channel_id=1, source_target_pairs={{0,8},{8,16},{12,4},{16,24},{20,12},{24,32},{28,20},{32,40},{36,28... | collective-permute-start | bytes 393224 | tf_op jit(solution)/shard_map/ppermute | solution.py:48
  35.4 12.1 %collective-permute-start.4 = (bf16[2,256,128]{2,1,0:T(8,128)(2,1)S(1)}, bf16[2,256,128]{2,1,0:T(8,128)(2,1)S(1)}, u32[]{:S(2)}, u32[]{:S(2)}) collective-permute-start(bf16[2,256,128]{2,1,0:T(8,128)(2,1)S(1)} %get-tuple-element.38.here_ref.refs_7_), channel_id=1, source_target_pairs={{4,8},{8,4},{12,16},{16,12},{20,24},{24,20},{28,32},{32,28},{36,40... | collective-permute-start | bytes 393224 | tf_op jit(solution)/shard_map/ppermute | solution.py:48
  38.7 18.5 %collective-permute-start.6 = (bf16[2,256,128]{2,1,0:T(8,128)(2,1)S(1)}, bf16[2,256,128]{2,1,0:T(8,128)(2,1)S(1)}, u32[]{:S(2)}, u32[]{:S(2)}) collective-permute-start(bf16[2,256,128]{2,1,0:T(8,128)(2,1)S(1)} %get-tuple-element.37.here_ref.refs_3_), channel_id=1, source_target_pairs={{0,4},{4,0},{8,12},{12,8},{16,20},{20,16},{24,28},{28,24},{32,36},... | collective-permute-start | bytes 393224 | tf_op jit(solution)/shard_map/ppermute | solution.py:48
  40.8 16.4 %collective-permute-start.5 = (bf16[2,256,128]{2,1,0:T(8,128)(2,1)S(1)}, bf16[2,256,128]{2,1,0:T(8,128)(2,1)S(1)}, u32[]{:S(2)}, u32[]{:S(2)}) collective-permute-start(bf16[2,256,128]{2,1,0:T(8,128)(2,1)S(1)} %get-tuple-element.38.here_ref.refs_7_), channel_id=1, source_target_pairs={{4,12},{8,0},{12,20},{16,8},{20,28},{24,16},{28,36},{32,24},{36,44... | collective-permute-start | bytes 393224 | tf_op jit(solution)/shard_map/ppermute | solution.py:48
  51.9 5.4 %collective-permute-start.7 = (bf16[2,256,128]{2,1,0:T(8,128)(2,1)S(1)}, bf16[2,256,128]{2,1,0:T(8,128)(2,1)S(1)}, u32[]{:S(2)}, u32[]{:S(2)}) collective-permute-start(bf16[2,256,128]{2,1,0:T(8,128)(2,1)S(1)} %get-tuple-element.40), channel_id=1, source_target_pairs={{4,0},{0,4},{12,8},{8,12},{20,16},{16,20},{28,24},{24,28},{36,32},... | collective-permute-start | bytes 393224 | tf_op jit(solution)/shard_map/ppermute | solution.py:48
  53.8 12.1 %collective-permute-start.8 = (bf16[2,256,128]{2,1,0:T(8,128)(2,1)S(1)}, bf16[2,256,128]{2,1,0:T(8,128)(2,1)S(1)}, u32[]{:S(2)}, u32[]{:S(2)}) collective-permute-start(bf16[2,256,128]{2,1,0:T(8,128)(2,1)S(1)} %get-tuple-element.47), channel_id=1, source_target_pairs={{8,0},{16,8},{4,12},{24,16},{12,20},{32,24},{20,28},{40,32},{28,36... | collective-permute-start | bytes 393224 | tf_op jit(solution)/shard_map/ppermute | solution.py:48
  61.6 4.4 %collective-permute-start.9 = (bf16[2,256,128]{2,1,0:T(8,128)(2,1)S(1)}, bf16[2,256,128]{2,1,0:T(8,128)(2,1)S(1)}, u32[]{:S(2)}, u32[]{:S(2)}) collective-permute-start(bf16[2,256,128]{2,1,0:T(8,128)(2,1)S(1)} %get-tuple-element.48), channel_id=1, source_target_pairs={{4,0},{0,4},{12,8},{8,12},{20,16},{16,20},{28,24},{24,28},{36,32},... | collective-permute-start | bytes 393224 | tf_op jit(solution)/shard_map/ppermute | solution.py:48
  63.5 11.1 %collective-permute-start.10 = (bf16[2,256,128]{2,1,0:T(8,128)(2,1)S(1)}, bf16[2,256,128]{2,1,0:T(8,128)(2,1)S(1)}, u32[]{:S(2)}, u32[]{:S(2)}) collective-permute-start(bf16[2,256,128]{2,1,0:T(8,128)(2,1)S(1)} %get-tuple-element.50), channel_id=1, source_target_pairs={{12,4},{0,8},{20,12},{8,16},{28,20},{16,24},{36,28},{24,32},{44,36... | collective-permute-start | bytes 393224 | tf_op jit(solution)/shard_map/ppermute | solution.py:48
  74.7 19.8 %collective-permute-start.11 = (bf16[2,2,64,128]{3,2,1,0:T(8,128)(2,1)S(1)}, bf16[2,2,64,128]{3,2,1,0:T(8,128)(2,1)S(1)}, u32[]{:S(2)}, u32[]{:S(2)}) collective-permute-start(bf16[2,2,64,128]{3,2,1,0:T(8,128)(2,1)S(1)} %get-tuple-element.51), channel_id=1, source_target_pairs={{0,2},{1,3},{2,0},{3,1},{4,6},{5,7},{6,4},{7,5},{8,10},{9,11},{10,... | collective-permute-start | bytes 196616 | tf_op jit(solution)/shard_map/ppermute | solution.py:61
  82.9 13.2 %collective-permute-start.12 = (bf16[2,2,64,128]{3,2,1,0:T(8,128)(2,1)S(1)}, bf16[2,2,64,128]{3,2,1,0:T(8,128)(2,1)S(1)}, u32[]{:S(2)}, u32[]{:S(2)}) collective-permute-start(bf16[2,2,64,128]{3,2,1,0:T(8,128)(2,1)S(1)} %get-tuple-element.55), channel_id=1, source_target_pairs={{0,1},{1,2},{2,3},{3,0},{4,7},{5,4},{6,5},{7,6},{8,9},{9,10},{10,1... | collective-permute-start | bytes 196616 | tf_op jit(solution)/shard_map/ppermute | solution.py:61
  87.7 10.9 %collective-permute-start.13 = (bf16[2,2,64,128]{3,2,1,0:T(8,128)(2,1)S(1)}, bf16[2,2,64,128]{3,2,1,0:T(8,128)(2,1)S(1)}, u32[]{:S(2)}, u32[]{:S(2)}) collective-permute-start(bf16[2,2,64,128]{3,2,1,0:T(8,128)(2,1)S(1)} %get-tuple-element.56), channel_id=1, source_target_pairs={{0,3},{1,0},{2,1},{3,2},{4,5},{5,6},{6,7},{7,4},{8,11},{9,8},{10,9... | collective-permute-start | bytes 196616 | tf_op jit(solution)/shard_map/ppermute | solution.py:61
